TPU v7x, 32 devices: a whole 2x2x4 slice. The times are simulated.
32 devices in a mesh: dp: 4 (over x, core), seq: 8 (over z, y).
Axes of the slice: x: 2, y: 2, z: 4, core: 2. Of those that a mesh axis runs over, the one named last changes fastest.
Arguments:
- tokens: bfloat16 [2, 4, 1024, 2048], P(None, 'dp', 'seq'), may hold values from -6 to 6
- segments: int32 [2, 4, 1024], P(None, 'dp'), may hold values from 0 to 3, as said below
- attn_gain: bfloat16 [2048], P(('dp', 'seq')), may hold values from 0.099609375 to 1.8984375
- query_weight: bfloat16 [2048, 2048], P(('dp', 'seq')), may hold values from -0.125 to 0.125
- key_weight: bfloat16 [2048, 1024], P(('dp', 'seq')), may hold values from -0.125 to 0.125
- value_weight: bfloat16 [2048, 1024], P(('dp', 'seq')), may hold values from -0.125 to 0.125
- out_weight: bfloat16 [2048, 2048], P(('dp', 'seq')), may hold values from -1 to 1
- ffn_gain: bfloat16 [2048], P(('dp', 'seq')), may hold values from 0.099609375 to 1.8984375
- gate_weight: bfloat16 [2048, 8192], P(('dp', 'seq')), may hold values from -0.125 to 0.125
- up_weight: bfloat16 [2048, 8192], P(('dp', 'seq')), may hold values from -0.125 to 0.125
- down_weight: bfloat16 [2048, 8192], P(('dp', 'seq')), may hold values from -0.0625 to 0.0625
- cotangent: bfloat16 [2, 4, 1024, 2048], P(None, 'dp', 'seq'), may hold values from -6 to 6
Outputs:
- output: bfloat16 [2, 4, 1024, 2048], P(None, 'dp', 'seq')
- input_grad: float32 [2, 4, 1024, 2048], P(None, 'dp', 'seq')
- attn_gain_grad: float32 [2048], P(('dp', 'seq'))
- query_grad: float32 [2048, 2048], P(('dp', 'seq'))
- key_grad: float32 [2048, 1024], P(('dp', 'seq'))
- value_grad: float32 [2048, 1024], P(('dp', 'seq'))
- proj_grad: float32 [2048, 2048], P(('dp', 'seq'))
- ffn_gain_grad: float32 [2048], P(('dp', 'seq'))
- gate_grad: float32 [2048, 8192], P(('dp', 'seq'))
- up_grad: float32 [2048, 8192], P(('dp', 'seq'))
- down_grad: float32 [2048, 8192], P(('dp', 'seq'))
Inputs may be any that keep to these rules, and one draw needn't show every extreme that they name: `segments`: along each sequence the document number starts at 0 and never falls.
All inputs are finite; a program needn't handle non-finite values.
Results may differ from a plain program's by a relative error of at most 0.015.
Values may be sent and summed in bfloat16 or wider, within the bound.
A program may use at most 704 MiB of HBM per device.

v0:
```python
import jax
import jax.numpy as jnp
from jax import lax
from jax.sharding import PartitionSpec as P

HEADS = 8
KV_HEADS = 4
HEAD_DIM = 256
WINDOW = 1024


NORM_EPS = 1e-06
ROPE_BASE = 1000042.0
NEG_LARGE = -1e30


def add_members(members):
    total = members[0]
    for member in members[1:]:
        total = total + member
    return total


def rms_norm(values, gain_vec):
    return values * lax.rsqrt(jnp.mean(values * values, -1, keepdims=True) + NORM_EPS) * gain_vec


def rope_tables(positions):
    inv_freq = 1.0 / ROPE_BASE ** (jnp.arange(0, HEAD_DIM, 2, dtype=jnp.float32) / HEAD_DIM)
    angles = positions.astype(jnp.float32)[:, None] * inv_freq[None, :]
    return (jnp.cos(angles), jnp.sin(angles))


def rotate(values, cosine, sine_table):
    half_dim = values.shape[-1] // 2
    front_half = values[..., :half_dim]
    back_half = values[..., half_dim:]
    return jnp.concatenate(
        [
            front_half * cosine - back_half * sine_table,
            back_half * cosine + front_half * sine_table,
        ],
        -1,
    )


def unrotate(values, cosine, sine_table):
    half_dim = values.shape[-1] // 2
    front_half = values[..., :half_dim]
    back_half = values[..., half_dim:]
    return jnp.concatenate(
        [
            front_half * cosine + back_half * sine_table,
            back_half * cosine - front_half * sine_table,
        ],
        -1,
    )


def contract_rows(left_arg, right_arg):
    return lax.dot_general(
        left_arg, right_arg, (((0,), (0,)), ((), ())), preferred_element_type=jnp.float32
    )


def contract_cols(left_arg, right_arg):
    return lax.dot_general(
        left_arg, right_arg, (((1,), (1,)), ((), ())), preferred_element_type=jnp.float32
    )


def silu_product(left_arg, right_arg):
    return jax.nn.silu(left_arg) * right_arg


def shards(
    tokens,
    segments,
    attn_gain,
    query_weight,
    key_weight,
    value_weight,
    out_weight,
    ffn_gain,
    gate_weight,
    up_weight,
    down_weight,
    cotangent,
):
    micro_count, seq_local, piece_len, model_width = tokens.shape
    seq_len = segments.shape[2]
    row_count = seq_local * piece_len
    group_size = HEADS // KV_HEADS
    score_scale = HEAD_DIM ** (-0.5)
    ffn_width = gate_weight.shape[1]
    seq_index = lax.axis_index("seq")
    own_offset = seq_index * piece_len
    positions = own_offset + jnp.arange(piece_len, dtype=jnp.int32)
    key_positions = jnp.arange(seq_len, dtype=jnp.int32)
    cosine, sine_table = rope_tables(positions)
    cosine = cosine[None, :, None, :]
    sine_table = sine_table[None, :, None, :]
    causal = (key_positions[None, :] <= positions[:, None]) & (
        positions[:, None] - key_positions[None, :] < WINDOW
    )

    def masked_scores(query_heads, key_all, seg_mask):
        raw_scores = (
            jnp.einsum(
                "spgjd,skgd->sgjpk", query_heads, key_all, preferred_element_type=jnp.float32
            )
            * score_scale
        )
        return jnp.where(seg_mask[:, None, None], raw_scores, NEG_LARGE)

    def attention_backward(weights_attn, attn_kept, grad_hidden):
        gain_one, w_query, w_key, w_value, w_out = weights_attn
        inputs, normed, query_heads, key_all, value_all, seg_mask, row_max, row_sum, mixed_heads = (
            attn_kept
        )
        grad_attn = grad_hidden.astype(jnp.bfloat16)
        proj_term = contract_rows(mixed_heads, grad_attn)
        grad_mixed = (
            contract_cols(grad_attn, w_out)
            .astype(jnp.bfloat16)
            .reshape(seq_local, piece_len, KV_HEADS, group_size, HEAD_DIM)
        )
        masked = masked_scores(query_heads, key_all, seg_mask)
        prob_full = jnp.exp(masked - row_max) / row_sum
        prob_low = prob_full.astype(jnp.bfloat16)
        grad_probs = jnp.einsum(
            "spgjd,skgd->sgjpk", grad_mixed, value_all, preferred_element_type=jnp.float32
        )
        grad_scores = prob_full * (grad_probs - jnp.sum(prob_full * grad_probs, -1, keepdims=True))
        grad_scores = grad_scores.astype(jnp.bfloat16)
        grad_query = (
            jnp.einsum(
                "sgjpk,skgd->spgjd", grad_scores, key_all, preferred_element_type=jnp.float32
            )
            * score_scale
        )
        key_term = (
            jnp.einsum(
                "sgjpk,spgjd->ksgd", grad_scores, query_heads, preferred_element_type=jnp.float32
            )
            * score_scale
        )
        value_term = jnp.einsum(
            "sgjpk,spgjd->ksgd", prob_low, grad_mixed, preferred_element_type=jnp.float32
        )
        key_value_grad = lax.psum_scatter(
            jnp.concatenate([key_term, value_term], 2).astype(jnp.bfloat16),
            "seq",
            scatter_dimension=0,
            tiled=True,
        ).astype(jnp.float32)
        key_value_grad = jnp.transpose(key_value_grad, (1, 0, 2, 3))
        grad_key = (
            unrotate(key_value_grad[:, :, :KV_HEADS], cosine, sine_table)
            .astype(jnp.bfloat16)
            .reshape(row_count, KV_HEADS * HEAD_DIM)
        )
        grad_value = (
            key_value_grad[:, :, KV_HEADS:]
            .astype(jnp.bfloat16)
            .reshape(row_count, KV_HEADS * HEAD_DIM)
        )
        grad_query = unrotate(
            grad_query.reshape(seq_local, piece_len, HEADS, HEAD_DIM), cosine, sine_table
        )
        grad_query = grad_query.astype(jnp.bfloat16).reshape(row_count, HEADS * HEAD_DIM)
        grad_normed = (
            contract_cols(grad_query, w_query)
            + contract_cols(grad_key, w_key)
            + contract_cols(grad_value, w_value)
        )
        pull_norm = jax.vjp(
            rms_norm, inputs.reshape(row_count, model_width), gain_one.astype(jnp.float32)
        )[1]
        grad_inputs, grad_gain = pull_norm(grad_normed)
        attn_terms = (
            grad_gain,
            contract_rows(normed, grad_query),
            contract_rows(normed, grad_key),
            contract_rows(normed, grad_value),
            proj_term,
        )
        return (grad_hidden + grad_inputs, attn_terms)

    output_list = []
    input_list = []
    sum_list = []
    saved_list = []
    for micro_index in range(micro_count):
        attention_gain_one = lax.all_gather(attn_gain, ("dp", "seq"), axis=0, tiled=True)
        attention_w_query = lax.all_gather(query_weight, ("dp", "seq"), axis=0, tiled=True)
        attention_w_key = lax.all_gather(key_weight, ("dp", "seq"), axis=0, tiled=True)
        attention_w_value = lax.all_gather(value_weight, ("dp", "seq"), axis=0, tiled=True)
        attention_w_out = lax.all_gather(out_weight, ("dp", "seq"), axis=0, tiled=True)
        attention_inputs = tokens[micro_index].astype(jnp.float32)
        attention_normed = (
            rms_norm(attention_inputs, attention_gain_one.astype(jnp.float32))
            .astype(jnp.bfloat16)
            .reshape(row_count, model_width)
        )
        query_pre = jnp.dot(
            attention_normed, attention_w_query, preferred_element_type=jnp.float32
        ).reshape(seq_local, piece_len, HEADS, HEAD_DIM)
        key_pre = jnp.dot(
            attention_normed, attention_w_key, preferred_element_type=jnp.float32
        ).reshape(seq_local, piece_len, KV_HEADS, HEAD_DIM)
        value_heads = (
            jnp.dot(attention_normed, attention_w_value, preferred_element_type=jnp.float32)
            .astype(jnp.bfloat16)
            .reshape(seq_local, piece_len, KV_HEADS, HEAD_DIM)
        )
        attention_query_heads = (
            rotate(query_pre, cosine, sine_table)
            .astype(jnp.bfloat16)
            .reshape(seq_local, piece_len, KV_HEADS, group_size, HEAD_DIM)
        )
        key_heads = rotate(key_pre, cosine, sine_table).astype(jnp.bfloat16)
        attention_key_all = lax.all_gather(key_heads, "seq", axis=1, tiled=True)
        attention_value_all = lax.all_gather(value_heads, "seq", axis=1, tiled=True)
        seg_ids = segments[micro_index]
        seg_query = lax.dynamic_slice_in_dim(seg_ids, own_offset, piece_len, 1)
        attention_seg_mask = causal[None] & (seg_query[:, :, None] == seg_ids[:, None, :])
        attention_masked = masked_scores(
            attention_query_heads, attention_key_all, attention_seg_mask
        )
        attention_row_max = jnp.max(attention_masked, -1, keepdims=True)
        exp_scores = jnp.exp(attention_masked - attention_row_max)
        attention_row_sum = jnp.sum(exp_scores, -1, keepdims=True)
        attention_prob_low = (exp_scores / attention_row_sum).astype(jnp.bfloat16)
        attention_mixed_heads = jnp.einsum(
            "sgjpk,skgd->spgjd",
            attention_prob_low,
            attention_value_all,
            preferred_element_type=jnp.float32,
        )
        attention_mixed_heads = attention_mixed_heads.reshape(row_count, HEADS * HEAD_DIM).astype(
            jnp.bfloat16
        )
        attention_hidden = attention_inputs.reshape(row_count, model_width) + jnp.dot(
            attention_mixed_heads, attention_w_out, preferred_element_type=jnp.float32
        )
        attn_kept = (
            attention_inputs,
            attention_normed,
            attention_query_heads,
            attention_key_all,
            attention_value_all,
            attention_seg_mask,
            attention_row_max,
            attention_row_sum,
            attention_mixed_heads,
        )
        ffn_gain_two = lax.all_gather(ffn_gain, ("dp", "seq"), axis=0, tiled=True)
        ffn_w_gate = lax.all_gather(gate_weight, ("dp", "seq"), axis=0, tiled=True)
        ffn_w_up = lax.all_gather(up_weight, ("dp", "seq"), axis=0, tiled=True)
        ffn_w_down = lax.all_gather(down_weight, ("dp", "seq"), axis=0, tiled=True)
        ffn_normed_two = rms_norm(attention_hidden, ffn_gain_two.astype(jnp.float32)).astype(
            jnp.bfloat16
        )
        ffn_gate_act = jnp.dot(ffn_normed_two, ffn_w_gate, preferred_element_type=jnp.float32)
        ffn_up_act = jnp.dot(ffn_normed_two, ffn_w_up, preferred_element_type=jnp.float32)
        ffn_middle = silu_product(ffn_gate_act, ffn_up_act).astype(jnp.bfloat16)
        result = attention_hidden + contract_cols(ffn_middle, ffn_w_down)
        ffn_kept = (ffn_normed_two, ffn_gate_act, ffn_up_act, ffn_middle)
        output_list.append(result.astype(jnp.bfloat16).reshape(seq_local, piece_len, model_width))
        grad_out = cotangent[micro_index].reshape(row_count, model_width)
        gain_two = lax.all_gather(ffn_gain, ("dp", "seq"), axis=0, tiled=True)
        w_gate = lax.all_gather(gate_weight, ("dp", "seq"), axis=0, tiled=True)
        w_up = lax.all_gather(up_weight, ("dp", "seq"), axis=0, tiled=True)
        w_down = lax.all_gather(down_weight, ("dp", "seq"), axis=0, tiled=True)
        normed_two, gate_act, up_act, middle = ffn_kept
        grad_middle = jnp.dot(grad_out, w_down, preferred_element_type=jnp.float32)
        pull_gate = jax.vjp(silu_product, gate_act, up_act)[1]
        grad_gate, grad_up = pull_gate(grad_middle)
        gate_low = grad_gate.astype(jnp.bfloat16)
        up_low = grad_up.astype(jnp.bfloat16)
        ffn_grad_normed = contract_cols(gate_low, w_gate) + contract_cols(up_low, w_up)
        ffn_pull_norm = jax.vjp(rms_norm, attention_hidden, gain_two.astype(jnp.float32))[1]
        ffn_grad_hidden, ffn_grad_gain = ffn_pull_norm(ffn_grad_normed)
        saved_ffn = (normed_two, jnp.concatenate([gate_low, up_low], 1), grad_out, middle)
        grad_hidden, ffn_gain_term, saved_ffn = (
            grad_out.astype(jnp.float32) + ffn_grad_hidden,
            ffn_grad_gain,
            saved_ffn,
        )
        back_attn = (
            lax.all_gather(attn_gain, ("dp", "seq"), axis=0, tiled=True),
            lax.all_gather(query_weight, ("dp", "seq"), axis=0, tiled=True),
            lax.all_gather(key_weight, ("dp", "seq"), axis=0, tiled=True),
            lax.all_gather(value_weight, ("dp", "seq"), axis=0, tiled=True),
            lax.all_gather(out_weight, ("dp", "seq"), axis=0, tiled=True),
        )
        grad_inputs, attn_terms = attention_backward(back_attn, attn_kept, grad_hidden)
        input_list.append(grad_inputs.reshape(seq_local, piece_len, model_width))
        grad_parts = (
            attn_terms[0],
            ffn_gain_term,
            attn_terms[1],
            attn_terms[2],
            attn_terms[3],
            attn_terms[4],
        )
        sum_list.append(grad_parts)
        saved_list.append(saved_ffn)
    attn_sums = jax.tree.map(lambda *members: add_members(members), *sum_list)
    normed_all = jnp.concatenate([saved_item[0] for saved_item in saved_list], 0)
    gate_up = jnp.concatenate([saved_item[1] for saved_item in saved_list], 0)
    down_in = jnp.concatenate([saved_item[2] for saved_item in saved_list], 0)
    middle_all = jnp.concatenate([saved_item[3] for saved_item in saved_list], 0)
    gate_up_term = contract_rows(normed_all, gate_up)
    down_term = contract_rows(down_in, middle_all)
    ffn_total = (
        lax.psum_scatter(gate_up_term, ("dp", "seq"), scatter_dimension=0, tiled=True),
        lax.psum_scatter(down_term, ("dp", "seq"), scatter_dimension=0, tiled=True),
    )
    return (
        jnp.stack(output_list),
        jnp.stack(input_list),
        lax.psum_scatter(attn_sums[0], ("dp", "seq"), scatter_dimension=0, tiled=True),
        lax.psum_scatter(attn_sums[2], ("dp", "seq"), scatter_dimension=0, tiled=True),
        lax.psum_scatter(attn_sums[3], ("dp", "seq"), scatter_dimension=0, tiled=True),
        lax.psum_scatter(attn_sums[4], ("dp", "seq"), scatter_dimension=0, tiled=True),
        lax.psum_scatter(attn_sums[5], ("dp", "seq"), scatter_dimension=0, tiled=True),
        lax.psum_scatter(attn_sums[1], ("dp", "seq"), scatter_dimension=0, tiled=True),
        ffn_total[0][:, :ffn_width],
        ffn_total[0][:, ffn_width:],
        ffn_total[1],
    )


def solution(mesh):
    placed = (
        P(None, "dp", "seq", None),
        P(None, "dp", None),
        P(("dp", "seq")),
        P(("dp", "seq"), None),
        P(("dp", "seq"), None),
        P(("dp", "seq"), None),
        P(("dp", "seq"), None),
        P(("dp", "seq")),
        P(("dp", "seq"), None),
        P(("dp", "seq"), None),
        P(("dp", "seq"), None),
        P(None, "dp", "seq", None),
    )
    return jax.shard_map(
        shards,
        mesh=mesh,
        in_specs=placed,
        out_specs=(
            P(None, "dp", "seq", None),
            P(None, "dp", "seq", None),
            P(("dp", "seq")),
            P(("dp", "seq"), None),
            P(("dp", "seq"), None),
            P(("dp", "seq"), None),
            P(("dp", "seq"), None),
            P(("dp", "seq")),
            P(("dp", "seq"), None),
            P(("dp", "seq"), None),
            P(("dp", "seq"), None),
        ),
        check_vma=False,
    )
```

profile of v0, /device:TPU:29, one launch (start us, length us, event | category | flops | bytes accessed | tf_op | source)
XLA Modules:
  0.0 5825.0 jit_solution(3526860079647765976)
XLA Ops:
  11.2 38.3 all-reduce.6
  51.4 21.7 all-gather.16.cloned.1.call-done
  86.1 50.7 all-gather.12.cloned.1.call-done
  148.8 67.1 %all-gather.20.cloned.1.call-done = bf16[2048,2048]{1,0:T(8,128)(2,1)} async-done(((bf16[64,2048]{1,0:T(8,128)(2,1)}), bf16[2048,2048]{1,0:T(8,128)(2,1)}) %all-gather.20.cloned.1.call-update) | async-done | bytes 8388624 | tf_op jit(solution)/shard_map/all_gather | solution.py:196
  238.1 26.7 all-gather.18.cloned.1.call-done
  270.1 46.7 all-gather.14.cloned.1.call-done
  320.9 76.0 %all-gather.22.cloned.1.call-done = bf16[2048,2048]{1,0:T(8,128)(2,1)} async-done(((bf16[64,2048]{1,0:T(8,128)(2,1)}), bf16[2048,2048]{1,0:T(8,128)(2,1)}) %all-gather.22.cloned.1.call-update) | async-done | bytes 8388624 | tf_op jit(solution)/shard_map/all_gather | solution.py:199
  401.7 44.3 all-gather.32.cloned.1.call-done
  451.4 46.7 all-gather.30.cloned.1.call-done
  507.6 187.6 %all-gather.26.cloned.1.call-done = bf16[2048,8192]{1,0:T(8,128)(2,1)} async-done(((bf16[64,8192]{1,0:T(8,128)(2,1)}), bf16[2048,8192]{1,0:T(8,128)(2,1)}) %all-gather.26.cloned.1.call-update) | async-done | bytes 33554448 | tf_op jit(solution)/shard_map/all_gather | solution.py:260
  695.2 17.1 fusion.189
  712.3 178.7 %all-gather.24.cloned.1.call-done = bf16[2048,8192]{1,0:T(8,128)(2,1)} async-done(((bf16[64,8192]{1,0:T(8,128)(2,1)}), bf16[2048,8192]{1,0:T(8,128)(2,1)}) %all-gather.24.cloned.1.call-update) | async-done | bytes 33554448 | tf_op jit(solution)/shard_map/all_gather | solution.py:259
  908.1 179.0 %all-gather.28.cloned.1.call-done = bf16[2048,8192]{1,0:T(8,128)(2,1)} async-done(((bf16[64,8192]{1,0:T(8,128)(2,1)}), bf16[2048,8192]{1,0:T(8,128)(2,1)}) %all-gather.28.cloned.1.call-update) | async-done | bytes 33554448 | tf_op jit(solution)/shard_map/all_gather | solution.py:261
  1087.1 20.0 multiply_convert_fusion.1
  1107.1 17.3 fusion.192
  1124.4 20.1 multiply_reduce_fusion.1
  1144.5 17.3 fusion.191
  1161.7 17.0 fusion.190
  1178.8 19.8 multiply_convert_fusion
  1198.6 17.4 fusion.194
  1216.0 18.4 multiply_reduce_fusion
  1276.9 50.3 fusion
  1344.3 90.6 %reduce-scatter.10.cloned.1.call-done = bf16[128,1,8,256]{3,0,2,1:T(8,128)(2,1)} async-done(((bf16[1024,1,8,256]{3,0,2,1:T(8,128)(2,1)}), bf16[128,1,8,256]{3,0,2,1:T(8,128)(2,1)}) %reduce-scatter.10.cloned.1.call-update) | async-done | bytes 524304 | tf_op jit(solution)/shard_map/reduce_scatter | solution.py:151
  1495.1 27.3 fusion.14
  1540.6 17.5 fusion.36
  1580.7 41.0 all-reduce.5
  1626.5 1692.6 %all-reduce.9.cloned.1.call-done = f32[2048,16384]{1,0:T(8,128)} async-done(((f32[2048,16384]{1,0:T(8,128)}), f32[2048,16384]{1,0:T(8,128)}) %all-reduce.9.cloned.1.call-update) | async-done | bytes 134217744
  3324.0 181.6 %reduce-scatter.16.cloned.1.call-done = f32[64,1024]{1,0:T(8,128)} async-done(((f32[2048,1024]{1,0:T(8,128)}), f32[64,1024]{1,0:T(8,128)}) %reduce-scatter.16.cloned.1.call-update) | async-done | bytes 262160 | tf_op jit(solution)/shard_map/reduce_scatter | solution.py:327
  3505.6 186.8 %reduce-scatter.14.cloned.1.call-done = f32[64,1024]{1,0:T(8,128)} async-done(((f32[2048,1024]{1,0:T(8,128)}), f32[64,1024]{1,0:T(8,128)}) %reduce-scatter.14.cloned.1.call-update) | async-done | bytes 262160 | tf_op jit(solution)/shard_map/reduce_scatter | solution.py:326
  3692.4 360.4 %reduce-scatter.18.cloned.1.call-done = f32[64,2048]{1,0:T(8,128)} async-done(((f32[2048,2048]{1,0:T(8,128)}), f32[64,2048]{1,0:T(8,128)}) %reduce-scatter.18.cloned.1.call-update) | async-done | bytes 524304 | tf_op jit(solution)/shard_map/reduce_scatter | solution.py:328
  4052.7 360.1 %reduce-scatter.12.cloned.1.call-done = f32[64,2048]{1,0:T(8,128)} async-done(((f32[2048,2048]{1,0:T(8,128)}), f32[64,2048]{1,0:T(8,128)}) %reduce-scatter.12.cloned.1.call-update) | async-done | bytes 524304 | tf_op jit(solution)/shard_map/reduce_scatter | solution.py:325
  4412.8 1405.5 %reduce-scatter.20.cloned.1.call-done = f32[64,8192]{1,0:T(8,128)} async-done(((f32[2048,8192]{1,0:T(8,128)}), f32[64,8192]{1,0:T(8,128)}) %reduce-scatter.20.cloned.1.call-update) | async-done | bytes 2097168 | tf_op jit(solution)/shard_map/reduce_scatter | solution.py:319
  (304 shorter events, 268.0 us)
Async XLA Ops:
  7.2 66.0 %all-gather.16.cloned.1.call-start = ((), (), s32[]{:S(2)}) async-start(), calls=%async_computation.9 | async-start | bytes 4325376 | tf_op jit(solution)/shard_map/all_gather | solution.py:197
  7.9 129.0 %all-gather.12.cloned.1.call-start = ((), (), s32[]{:S(2)}) async-start(), calls=%async_computation.7 | async-start | bytes 4325376 | tf_op jit(solution)/shard_map/all_gather | solution.py:198
  8.7 207.2 %all-gather.20.cloned.1.call-start = ((), (), s32[]{:S(2)}) async-start(), calls=%async_computation.11 | async-start | bytes 8650752 | tf_op jit(solution)/shard_map/all_gather | solution.py:196
  9.4 255.4 %all-gather.18.cloned.1.call-start = ((), (), s32[]{:S(2)}) async-start(), calls=%async_computation.10 | async-start | bytes 2359296 | tf_op jit(solution)/shard_map/all_gather | solution.py:223
  49.5 185.3 %copy-start.39 = (f32[2048]{0:T(1024)}, f32[2048]{0:T(1024)S(1)}, u32[]{:S(2)}) copy-start(f32[2048]{0:T(1024)S(1)} %convert_element_type.364) | copy-start | bytes 24580
  51.1 177.3 %copy-start.68 = (f32[128]{0:T(128)}, f32[128]{0:T(128)S(1)}, u32[]{:S(2)}) copy-start(f32[128]{0:T(128)S(1)} %get-tuple-element.89) | copy-start | bytes 1540
  51.1 183.8 %copy-start.64 = (f32[128]{0:T(128)}, f32[128]{0:T(128)S(1)}, u32[]{:S(2)}) copy-start(f32[128]{0:T(128)S(1)} %get-tuple-element.90) | copy-start | bytes 1540
  51.4 186.4 %copy-start.47 = (f32[128,128]{1,0:T(8,128)}, f32[128,128]{1,0:T(8,128)S(1)}, u32[]{:S(2)}) copy-start(f32[128,128]{1,0:T(8,128)S(1)} %get-tuple-element.70) | copy-start | bytes 196612
  51.4 186.4 %copy-start.49 = (f32[128,128]{1,0:T(8,128)}, f32[128,128]{1,0:T(8,128)S(1)}, u32[]{:S(2)}) copy-start(f32[128,128]{1,0:T(8,128)S(1)} %get-tuple-element.71) | copy-start | bytes 196612
  86.1 230.7 %all-gather.14.cloned.1.call-start = ((), (), s32[]{:S(2)}) async-start(), calls=%async_computation.8 | async-start | bytes 2359296 | tf_op jit(solution)/shard_map/all_gather | solution.py:224
  140.7 256.2 %all-gather.22.cloned.1.call-start = ((), (), s32[]{:S(2)}) async-start(), calls=%async_computation.12 | async-start | bytes 8650752 | tf_op jit(solution)/shard_map/all_gather | solution.py:199
  141.3 304.7 %all-gather.32.cloned.1.call-start = ((), (), s32[]{:S(2)}) async-start(), calls=%async_computation.17 | async-start | bytes 2359296 | tf_op jit(solution)/shard_map/all_gather | solution.py:223
  142.1 356.0 %all-gather.30.cloned.1.call-start = ((), (), s32[]{:S(2)}) async-start(), calls=%async_computation.16 | async-start | bytes 2359296 | tf_op jit(solution)/shard_map/all_gather | solution.py:224
  146.0 549.3 %all-gather.26.cloned.1.call-start = ((), (), s32[]{:S(2)}) async-start(), calls=%async_computation.14 | async-start | bytes 34603008 | tf_op jit(solution)/shard_map/all_gather | solution.py:260
  146.7 744.4 %all-gather.24.cloned.1.call-start = ((), (), s32[]{:S(2)}) async-start(), calls=%async_computation.13 | async-start | bytes 34603008 | tf_op jit(solution)/shard_map/all_gather | solution.py:259
  147.3 939.8 %all-gather.28.cloned.1.call-start = ((), (), s32[]{:S(2)}) async-start(), calls=%async_computation.15 | async-start | bytes 34603008 | tf_op jit(solution)/shard_map/all_gather | solution.py:261
  148.0 1195.1 %reduce-scatter.8.cloned.1.call-start = ((), (), s32[]{:S(2)}) async-start(), calls=%async_computation.18 | async-start | bytes 4718592 | tf_op jit(solution)/shard_map/reduce_scatter | solution.py:151
  148.8 168.0 %copy-start.53 = (pred[128,1024]{0,1:T(8,128)(4,1)}, pred[128,1024]{0,1:T(8,128)(4,1)S(1)}, u32[]{:S(2)}) copy-start(pred[128,1024]{0,1:T(8,128)(4,1)S(1)} %get-tuple-element.72) | copy-start | bytes 393220
  148.8 349.3 %copy-start.51 = (pred[128,1024]{0,1:T(8,128)(4,1)}, pred[128,1024]{0,1:T(8,128)(4,1)S(1)}, u32[]{:S(2)}) copy-start(pred[128,1024]{0,1:T(8,128)(4,1)S(1)} %get-tuple-element.73) | copy-start | bytes 393220
  238.1 207.9 %copy-start.56 = (bf16[1,128,8,128]{3,1,2,0:T(8,128)(2,1)}, bf16[1,128,8,128]{3,1,2,0:T(8,128)(2,1)S(1)}, u32[]{:S(2)}) copy-start(bf16[1,128,8,128]{3,1,2,0:T(8,128)(2,1)S(1)} %get-tuple-element.63) | copy-start | bytes 786436
  238.1 207.9 %copy-start.58 = (bf16[1,128,8,128]{3,1,2,0:T(8,128)(2,1)}, bf16[1,128,8,128]{3,1,2,0:T(8,128)(2,1)S(1)}, u32[]{:S(2)}) copy-start(bf16[1,128,8,128]{3,1,2,0:T(8,128)(2,1)S(1)} %get-tuple-element.64) | copy-start | bytes 786436
  401.6 832.8 %copy-start.5 = (f32[128,2048]{1,0:T(8,128)}, f32[128,2048]{1,0:T(8,128)S(1)}, u32[]{:S(2)}) copy-start(f32[128,2048]{1,0:T(8,128)S(1)} %get-tuple-element.79) | copy-start | bytes 3145732
  507.4 727.0 %copy-start.7 = (f32[128,2048]{1,0:T(8,128)}, f32[128,2048]{1,0:T(8,128)S(1)}, u32[]{:S(2)}) copy-start(f32[128,2048]{1,0:T(8,128)S(1)} %get-tuple-element.81) | copy-start | bytes 3145732
  507.6 383.5 %copy-start.30 = (bf16[128,2048]{1,0:T(8,128)(2,1)}, bf16[128,2048]{1,0:T(8,128)(2,1)S(1)}, u32[]{:S(2)}) copy-start(bf16[128,2048]{1,0:T(8,128)(2,1)S(1)} %multiply_convert_fusion.5) | copy-start | bytes 1572868
  1256.1 178.7 %reduce-scatter.10.cloned.1.call-start = ((), (), s32[]{:S(2)}) async-start(), calls=%async_computation.19 | async-start | bytes 4718592 | tf_op jit(solution)/shard_map/reduce_scatter | solution.py:151
  1275.1 2044.0 %all-reduce.9.cloned.1.call-start = ((), (), s32[]{:S(2)}) async-start(), calls=%async_computation.25 | async-start | bytes 268435456
  1327.2 108.8 %copy-start.65 = (f32[128]{0:T(128)S(1)}, f32[128]{0:T(128)}, u32[]{:S(2)}) copy-start(f32[128]{0:T(128)} %copy-done.64) | copy-start | bytes 1540
  1327.3 2178.3 %reduce-scatter.16.cloned.1.call-start = ((), (), s32[]{:S(2)}) async-start(), calls=%async_computation.22 | async-start | bytes 8650752 | tf_op jit(solution)/shard_map/reduce_scatter | solution.py:327
  1442.1 2250.2 %reduce-scatter.14.cloned.1.call-start = ((), (), s32[]{:S(2)}) async-start(), calls=%async_computation.21 | async-start | bytes 8650752 | tf_op jit(solution)/shard_map/reduce_scatter | solution.py:326
  1452.9 2599.9 %reduce-scatter.18.cloned.1.call-start = ((), (), s32[]{:S(2)}) async-start(), calls=%async_computation.23 | async-start | bytes 17301504 | tf_op jit(solution)/shard_map/reduce_scatter | solution.py:328
  1465.9 2946.9 %reduce-scatter.12.cloned.1.call-start = ((), (), s32[]{:S(2)}) async-start(), calls=%async_computation.20 | async-start | bytes 17301504 | tf_op jit(solution)/shard_map/reduce_scatter | solution.py:325
  1492.3 4326.0 %reduce-scatter.20.cloned.1.call-start = ((), (), s32[]{:S(2)}) async-start(), calls=%async_computation.24 | async-start | bytes 69206016 | tf_op jit(solution)/shard_map/reduce_scatter | solution.py:319
  (67 other events, 1028.2 us)
Sparse Core Ops, SparseCore 0:
  11.1 62.0 all-gather.15
  76.2 60.6 all-gather.11
  139.9 75.9 all-gather.19
  218.5 46.3 all-gather.17
  267.3 49.4 all-gather.13
  319.6 77.2 all-gather.21
  399.6 46.3 all-gather.31
  448.6 49.4 all-gather.29
  501.1 194.1 all-gather.25
  698.1 192.9 all-gather.23
  894.1 192.9 all-gather.27
  1256.2 86.8 reduce-scatter.7
  1347.2 87.6 reduce-scatter.9
  1441.1 1877.9 all-reduce.8
  3321.8 183.7 reduce-scatter.15
  3508.3 183.9 reduce-scatter.13
  3695.1 357.6 reduce-scatter.17
  4055.5 357.2 reduce-scatter.11
  4415.7 1402.4 reduce-scatter.19
where the time goes:
time: 5830 us
  waiting for transfers between devices  5220 us (90%)
  matrix products  426 us (7%)
  blocking collectives  79.3 us (1%)
    unnamed x20, waiting for transfers between devices  1700 us
    reduce_scatter x1, waiting for transfers between devices, shards(): lax.psum_scatter(down_term, ('dp', 'seq'), scatter_dimension=0, tiled=True)  1410 us
    reduce_scatter x1, waiting for transfers between devices, shards(): lax.psum_scatter(attn_sums[5], ('dp', 'seq'), scatter_dimension=0, tiled=...  360 us
    reduce_scatter x1, waiting for transfers between devices, shards(): lax.psum_scatter(attn_sums[2], ('dp', 'seq'), scatter_dimension=0, tiled=...  360 us
    all_gather x1, waiting for transfers between devices, shards(): ffn_w_up = lax.all_gather(up_weight, ('dp', 'seq'), axis=0, tiled=True)  188 us
    reduce_scatter x1, waiting for transfers between devices, shards(): lax.psum_scatter(attn_sums[3], ('dp', 'seq'), scatter_dimension=0, tiled=...  187 us
    reduce_scatter x1, waiting for transfers between devices, shards(): lax.psum_scatter(attn_sums[4], ('dp', 'seq'), scatter_dimension=0, tiled=...  182 us
    all_gather x1, waiting for transfers between devices, shards(): ffn_w_down = lax.all_gather(down_weight, ('dp', 'seq'), axis=0, tiled=True)  179 us
  transfers between devices with their start and end apart: 19, of which 19 were waited for; matrix products, arithmetic and copies ran while one was open for 6% of the time, Pallas kernels for 0%

commit v1 on v0

v1 whole, which is shorter than its diff:
```python
import functools

import jax
import jax.numpy as jnp
from jax import lax
from jax.experimental import pallas as pl
from jax.experimental.pallas import tpu as pltpu
from jax.sharding import Mesh
from jax.sharding import PartitionSpec as P

HEADS = 8
KV_HEADS = 4
HEAD_DIM = 256
WINDOW = 1024
NORM_EPS = 1e-06
ROPE_BASE = 1000042.0
NEG_LARGE = -1e30
SCALE = HEAD_DIM**-0.5
PLANE = ("x", "core", "y")
EVERY = ("x", "core", "z", "y")
BF16 = jnp.bfloat16
F32 = jnp.float32


def dot_nn(a, b):
    return lax.dot_general(a, b, (((1,), (0,)), ((), ())), preferred_element_type=F32)


def dot_nt(a, b):
    return lax.dot_general(a, b, (((1,), (1,)), ((), ())), preferred_element_type=F32)


def dot_tn(a, b):
    return lax.dot_general(a, b, (((0,), (0,)), ((), ())), preferred_element_type=F32)


def rotate(values, cosine, sine):
    half = values.shape[-1] // 2
    a, b = values[:, :half], values[:, half:]
    return jnp.concatenate([a * cosine - b * sine, b * cosine + a * sine], -1)


def masked_prob(q, k, qinfo, kseg):
    scores = dot_nt(q, k) * SCALE
    qpos, qseg = qinfo[:, 0:1], qinfo[:, 1:2]
    kpos = lax.broadcasted_iota(jnp.int32, scores.shape, 1)
    allowed = (kpos <= qpos) & (qpos - kpos < WINDOW) & (qseg == kseg)
    masked = jnp.where(allowed, scores, NEG_LARGE)
    e = jnp.exp(masked - jnp.max(masked, -1, keepdims=True))
    return e / jnp.sum(e, -1, keepdims=True)


def attn_fwd_kernel(q_ref, k_ref, v_ref, qinfo_ref, kseg_ref, o_ref):
    hd = q_ref.shape[-1]
    q = q_ref[...].reshape(-1, hd)
    k = k_ref[...].reshape(-1, hd)
    v = v_ref[...].reshape(-1, hd)
    prob = masked_prob(q, k, qinfo_ref[0], kseg_ref[0])
    o_ref[...] = dot_nn(prob.astype(BF16), v).astype(BF16).reshape(o_ref.shape)


def attn_bwd_kernel(
    q_ref, k_ref, v_ref, do_ref, qinfo_ref, kseg_ref, dq_ref, dk_ref, dv_ref
):
    hd = q_ref.shape[-1]
    q = q_ref[...].reshape(-1, hd)
    k = k_ref[...].reshape(-1, hd)
    v = v_ref[...].reshape(-1, hd)
    do = do_ref[...].reshape(-1, hd)
    prob = masked_prob(q, k, qinfo_ref[0], kseg_ref[0])
    dprob = dot_nt(do, v)
    ds = prob * (dprob - jnp.sum(prob * dprob, -1, keepdims=True))
    dsb = ds.astype(BF16)
    dq_ref[...] = (dot_nn(dsb, k) * SCALE).reshape(dq_ref.shape)
    dk_ref[...] = (dot_tn(dsb, q) * SCALE).astype(BF16).reshape(dk_ref.shape)
    dv_ref[...] = dot_tn(prob.astype(BF16), do).astype(BF16).reshape(dv_ref.shape)


def attention_specs(dims):
    dp, ny, ms, pl_len, nz, hd = dims
    qspec = pl.BlockSpec((1, ny, 1, pl_len, hd), lambda d, m: (d, 0, m, 0, 0))
    kspec = pl.BlockSpec((nz, 1, ny, 1, pl_len, hd), lambda d, m: (0, d, 0, m, 0, 0))
    qi = pl.BlockSpec((1, ny * pl_len, 2), lambda d, m: (d * ms + m, 0, 0))
    ks = pl.BlockSpec((1, 1, nz * ny * pl_len), lambda d, m: (d * ms + m, 0, 0))
    return qspec, kspec, qi, ks


def attn_forward(q, k, v, qinfo, kseg, dims):
    dp, ny, ms, pl_len, nz, hd = dims
    qspec, kspec, qi, ks = attention_specs(dims)
    return pl.pallas_call(
        attn_fwd_kernel,
        grid=(dp, ms),
        in_specs=[qspec, kspec, kspec, qi, ks],
        out_specs=qspec,
        out_shape=jax.ShapeDtypeStruct((dp, ny, ms, pl_len, hd), BF16),
        compiler_params=pltpu.CompilerParams(vmem_limit_bytes=48 << 20),
        cost_estimate=pl.CostEstimate(
            flops=dp * ms * ny * pl_len * nz * ny * pl_len * hd * 4,
            bytes_accessed=4 * dp * ms * nz * ny * pl_len * hd,
            transcendentals=dp * ms * ny * pl_len * nz * ny * pl_len,
        ),
        name="attention_forward",
    )(q, k, v, qinfo, kseg)


def attn_backward(q, k, v, do, qinfo, kseg, dims):
    dp, ny, ms, pl_len, nz, hd = dims
    qspec, kspec, qi, ks = attention_specs(dims)
    kshape = (nz, dp, ny, ms, pl_len, hd)
    return pl.pallas_call(
        attn_bwd_kernel,
        grid=(dp, ms),
        in_specs=[qspec, kspec, kspec, qspec, qi, ks],
        out_specs=[qspec, kspec, kspec],
        out_shape=[
            jax.ShapeDtypeStruct((dp, ny, ms, pl_len, hd), F32),
            jax.ShapeDtypeStruct(kshape, BF16),
            jax.ShapeDtypeStruct(kshape, BF16),
        ],
        compiler_params=pltpu.CompilerParams(vmem_limit_bytes=48 << 20),
        cost_estimate=pl.CostEstimate(
            flops=dp * ms * ny * pl_len * nz * ny * pl_len * hd * 10,
            bytes_accessed=8 * dp * ms * nz * ny * pl_len * hd,
            transcendentals=dp * ms * ny * pl_len * nz * ny * pl_len,
        ),
        name="attention_backward",
    )(q, k, v, do, qinfo, kseg)


def plane_gather(a):
    return lax.all_gather(a, PLANE, axis=0, tiled=True)


def plane_scatter(a):
    return lax.psum_scatter(a, PLANE, scatter_dimension=0, tiled=True)


def weight_columns(w):
    part = lax.all_to_all(w, PLANE, split_axis=1, concat_axis=0, tiled=True)
    part = part.reshape(-1, w.shape[2])
    return lax.all_gather(part, "z", axis=0, tiled=True)


def weight_rows_back(g, rows):
    part = lax.psum_scatter(g, "z", scatter_dimension=0, tiled=True)
    part = part.reshape(8 * rows, 1, g.shape[1])
    return lax.all_to_all(part, PLANE, split_axis=0, concat_axis=1, tiled=True)


def shards(
    tokens,
    segments,
    attn_gain,
    query_weight,
    key_weight,
    value_weight,
    out_weight,
    ffn_gain,
    gate_weight,
    up_weight,
    down_weight,
    cotangent,
):
    micro, seq_local, pl_len, width = tokens.shape
    seq_len = segments.shape[2]
    ms = micro * seq_local
    rows_w = gate_weight.shape[0]
    ffn_width = gate_weight.shape[1]
    nx, nc, nz, ny = (lax.axis_size(a) for a in EVERY)
    dp = nx * nc
    n_own = ms * pl_len
    n_plane = 8 * n_own
    col_block = width // (dp * nz)
    dims = (dp, ny, ms, pl_len, nz, HEAD_DIM)
    z_index = lax.axis_index("z")
    core = lax.axis_index("core")

    def perm(a):
        lead = a.shape[:-1]
        return a.reshape(*lead, dp, nz, col_block).swapaxes(-3, -2).reshape(*lead, width)

    def unperm(a):
        lead = a.shape[:-1]
        return a.reshape(*lead, nz, dp, col_block).swapaxes(-3, -2).reshape(*lead, width)

    def by_head(a):
        return a.reshape(a.shape[0], 2, 2, 2, -1).swapaxes(2, 3).reshape(a.shape[0], 8, -1)

    def from_head(a):
        return a.reshape(a.shape[0], 2, 2, 2, -1).swapaxes(2, 3).reshape(a.shape[0], -1)

    heads_of = [(x * 2 + y) * 2 + c for x in range(2) for c in range(2) for y in range(2)]

    def place(x, c, z, y):
        return ((x * 2 + c) * nz + z) * 2 + y

    to_head, to_owner = [], []
    for x in range(2):
        for c in range(2):
            for y in range(2):
                head = (x * 2 + y) * 2 + c
                for k in range(nz):
                    to_head.append((head * nz + k, place(x, c, k, y)))
                    to_owner.append((place(x, c, k, y), head * nz + k))

    g1 = attn_gain.astype(F32)[:, None]
    g2 = ffn_gain.astype(F32)[:, None]

    def fold(w, g):
        return (w.astype(F32) * g).astype(BF16)

    wq_own = by_head(query_weight)
    wkv_own = jnp.stack(
        [key_weight.reshape(rows_w, KV_HEADS, HEAD_DIM), value_weight.reshape(rows_w, KV_HEADS, HEAD_DIM)], 2
    ).reshape(rows_w, 8 * HEAD_DIM)
    wkv_own = by_head(wkv_own)
    wqkv_own = jnp.concatenate([wq_own, wkv_own], 2)
    w_qkv = weight_columns((wqkv_own.astype(F32) * g1[:, :, None]).astype(BF16))
    w_out = lax.all_gather(
        lax.ppermute(perm(out_weight), EVERY, to_head), "z", axis=0, tiled=True
    )
    w_gate = weight_columns(fold(gate_weight, g2).reshape(rows_w, 8, -1))
    w_up = weight_columns(fold(up_weight, g2).reshape(rows_w, 8, -1))
    w_down = weight_columns(down_weight.reshape(rows_w, 8, -1))

    x = perm(tokens).reshape(n_own, width).astype(F32)
    r1 = lax.rsqrt(jnp.mean(x * x, -1, keepdims=True) + NORM_EPS)
    xhat = x * r1
    xa = plane_gather(xhat.astype(BF16))

    inv_freq = 1.0 / ROPE_BASE ** (jnp.arange(0, HEAD_DIM, 2, dtype=F32) / HEAD_DIM)
    pos = z_index * (ny * pl_len) + jnp.arange(ny * pl_len, dtype=jnp.int32)
    angles = pos.astype(F32)[:, None] * inv_freq[None, :]

    def spread(t):
        t = t.reshape(1, ny, 1, pl_len, HEAD_DIM // 2)
        return jnp.broadcast_to(t, (dp, ny, ms, pl_len, HEAD_DIM // 2)).reshape(n_plane, -1)

    cos_q, sin_q = spread(jnp.cos(angles)), spread(jnp.sin(angles))
    cos_k = jnp.where(core == 0, cos_q, 1.0)
    sin_k = jnp.where(core == 0, sin_q, 0.0)

    seg_all = lax.all_gather(segments, ("x", "core"), axis=0, tiled=False)
    seg_all = seg_all.reshape(dp * ms, seq_len)
    qseg = lax.dynamic_slice_in_dim(seg_all, z_index * (ny * pl_len), ny * pl_len, 1)
    qinfo = jnp.stack([jnp.broadcast_to(pos[None], qseg.shape), qseg], -1)
    kseg = seg_all[:, None, :]

    qkv = dot_nn(xa, w_qkv)
    qb = rotate(qkv[:, :HEAD_DIM], cos_q, sin_q).astype(BF16)
    kvb = rotate(qkv[:, HEAD_DIM:], cos_k, sin_k).astype(BF16)
    kv_all = lax.all_gather(lax.all_gather(kvb, "z", axis=0), "core", axis=0)
    k_all = kv_all[0].reshape(nz, dp, ny, ms, pl_len, HEAD_DIM)
    v_all = kv_all[1].reshape(nz, dp, ny, ms, pl_len, HEAD_DIM)
    q5 = qb.reshape(dp, ny, ms, pl_len, HEAD_DIM)
    ob = attn_forward(q5, k_all, v_all, qinfo, kseg, dims).reshape(n_plane, HEAD_DIM)
    h = x + plane_scatter(dot_nn(ob, w_out).astype(BF16)).astype(F32)

    r2 = lax.rsqrt(jnp.mean(h * h, -1, keepdims=True) + NORM_EPS)
    hhat = h * r2
    ha = plane_gather(hhat.astype(BF16))
    gate = dot_nn(ha, w_gate)
    up = dot_nn(ha, w_up)
    sig = jax.nn.sigmoid(gate)
    silu = gate * sig
    mid = (silu * up).astype(BF16)
    result = h + plane_scatter(dot_nt(mid, w_down).astype(BF16)).astype(F32)
    output = unperm(result.astype(BF16)).reshape(tokens.shape)

    cot = perm(cotangent).reshape(n_own, width)
    ca = plane_gather(cot)
    d_mid = dot_nn(ca, w_down)
    dgb = (d_mid * up * sig * (1.0 + gate * (1.0 - sig))).astype(BF16)
    dub = (d_mid * silu).astype(BF16)
    d_hhat = plane_scatter((dot_nt(dgb, w_gate) + dot_nt(dub, w_up)).astype(BF16)).astype(F32)
    dh = cot.astype(F32) + r2 * (d_hhat - hhat * jnp.mean(d_hhat * hhat, -1, keepdims=True))
    da = plane_gather(dh.astype(BF16))
    dob = dot_nt(da, w_out).astype(BF16)

    dq, dk_h, dv_h = attn_backward(
        q5, k_all, v_all, dob.reshape(q5.shape), qinfo, kseg, dims
    )
    dkv = lax.psum_scatter(jnp.stack([dk_h, dv_h]), "core", scatter_dimension=0)
    dkv = lax.psum_scatter(dkv, "z", scatter_dimension=0).reshape(n_plane, HEAD_DIM)
    dqb = rotate(dq.reshape(n_plane, HEAD_DIM), cos_q, -sin_q).astype(BF16)
    dkvb = rotate(dkv.astype(F32), cos_k, -sin_k).astype(BF16)
    dqkv = jnp.concatenate([dqb, dkvb], 1)
    d_xhat = plane_scatter(dot_nt(dqkv, w_qkv).astype(BF16)).astype(F32)
    input_grad = dh + r1 * (d_xhat - xhat * jnp.mean(d_xhat * xhat, -1, keepdims=True))
    input_grad = unperm(input_grad).reshape(tokens.shape)

    gate_back = weight_rows_back(dot_tn(ha, dgb).astype(BF16), rows_w).reshape(rows_w, -1).astype(F32)
    up_back = weight_rows_back(dot_tn(ha, dub).astype(BF16), rows_w).reshape(rows_w, -1).astype(F32)
    down_back = weight_rows_back(dot_tn(ca, mid).astype(BF16), rows_w).reshape(rows_w, -1).astype(F32)
    out_back = lax.psum_scatter(
        dot_tn(ob, da).astype(BF16), "z", scatter_dimension=0, tiled=True
    )
    out_back = unperm(lax.ppermute(out_back, EVERY, to_owner).astype(F32))
    qkv_back = weight_rows_back(dot_tn(xa, dqkv).astype(BF16), rows_w).astype(F32)
    q_back = from_head(qkv_back[:, :, :HEAD_DIM])
    kv_back = from_head(qkv_back[:, :, HEAD_DIM:]).reshape(rows_w, KV_HEADS, 2, HEAD_DIM)
    k_back = kv_back[:, :, 0].reshape(rows_w, -1)
    v_back = kv_back[:, :, 1].reshape(rows_w, -1)

    def gain_term(pairs):
        return sum(jnp.sum(w.astype(F32) * g, -1) for w, g in pairs)

    return (
        output,
        input_grad,
        gain_term([(query_weight, q_back), (key_weight, k_back), (value_weight, v_back)]),
        q_back * g1,
        k_back * g1,
        v_back * g1,
        out_back,
        gain_term([(gate_weight, gate_back), (up_weight, up_back)]),
        gate_back * g2,
        up_back * g2,
        down_back,
    )


def solution(mesh):
    dp, seq = mesh.shape["dp"], mesh.shape["seq"]
    fine = Mesh(mesh.devices.reshape(dp // 2, 2, seq // 2, 2), EVERY)
    dp_axes, seq_axes = ("x", "core"), ("z", "y")
    tok = P(None, dp_axes, seq_axes, None)
    vec, mat = P(EVERY), P(EVERY, None)
    return jax.shard_map(
        shards,
        mesh=fine,
        in_specs=(tok, P(None, dp_axes, None), vec, mat, mat, mat, mat, vec, mat, mat, mat, tok),
        out_specs=(tok, tok, vec, mat, mat, mat, mat, vec, mat, mat, mat),
        check_vma=False,
    )
```

time: 5830 us -> 1520 us (0.26)
  waiting for transfers between devices: 5220 us -> 1030 us
  matrix products: 426 us -> 184 us
    reduce_scatter x7 -> x11, waiting for transfers between devices: 2600 us -> 503 us  [the longest x4 236 us: plane_scatter(): return lax.psum_scatter(a, PLANE, scatter_dimension=0, tiled=True)]
    unnamed x20 -> x22, waiting for transfers between devices: 1700 us -> 0.36 us
    all_gather x11, waiting for transfers between devices: 925 us -> 524 us  [the longest x4 228 us: plane_gather(): return lax.all_gather(a, PLANE, axis=0, tiled=True)]
    dot_general x50 -> x15, matrix products: 426 us -> 184 us  [the longest x5 65.3 us: dot_nn(): lax.dot_general(a, b, (((1,), (0,)), ((), ())), preferred_element_type=F32)]
    unnamed x2 -> x0, blocking collectives: 79.3 us -> none
    all_to_all x0 -> x4, blocking collectives: none -> 65.1 us  [weight_columns(): part = lax.all_to_all(w, PLANE, split_axis=1, concat_axis=0, tiled=True)]
  transfers between devices with their start and end apart: 19 -> 28, of which waited for: 19 -> 22; matrix products, arithmetic and copies ran while one was open for 6% -> 14% of each run, Pallas kernels for 0% -> 1%
where the time goes in v1:
time: 1520 us; the launch traced here: 1500 us
  waiting for transfers between devices  1030 us (68%)
  matrix products  184 us (12%)
  local copies, waits for them, and re-layouts  86.5 us (6%)
  blocking collectives  80.9 us (5%)
  other arithmetic  59 us (4%)
  Pallas kernels  26.9 us (2%)
  starting transfers between devices  22.8 us (2%)
  between operations  15.5 us (1%)
    reduce_scatter x4, waiting for transfers between devices, plane_scatter(): return lax.psum_scatter(a, PLANE, scatter_dimension=0, tiled=True)  236 us
    all_gather x4, waiting for transfers between devices, plane_gather(): return lax.all_gather(a, PLANE, axis=0, tiled=True)  228 us
    reduce_scatter x4, waiting for transfers between devices, weight_rows_back(): part = lax.psum_scatter(g, 'z', scatter_dimension=0, tiled=True)  221 us
    all_gather x4, waiting for transfers between devices, weight_columns(): return lax.all_gather(part, 'z', axis=0, tiled=True)  201 us
    all_gather x2, waiting for transfers between devices, shards(): kv_all = lax.all_gather(lax.all_gather(kvb, 'z', axis=0), 'core', axis=0)  82.9 us
    dot_general x5, matrix products, dot_nn(): lax.dot_general(a, b, (((1,), (0,)), ((), ())), preferred_element_type=F32)  65.3 us
    all_to_all x4, blocking collectives, weight_columns(): part = lax.all_to_all(w, PLANE, split_axis=1, concat_axis=0, tiled=True)  65.1 us
    dot_general x5, matrix products, dot_nt(): lax.dot_general(a, b, (((1,), (1,)), ((), ())), preferred_element_type=F32)  59.3 us
  transfers between devices with their start and end apart: 28, of which 22 were waited for; matrix products, arithmetic and copies ran while one was open for 14% of the time, Pallas kernels for 1%

profile of v1, /device:TPU:29, one launch (start us, length us, event | category | flops | bytes accessed | tf_op | source)
XLA Modules:
  0.0 1503.2 jit_solution(13145317323335546868)
XLA Ops:
  32.8 35.6 %all-gather.16.cloned.1.call-done = bf16[2048,512]{1,0:T(8,128)(2,1)} async-done(((bf16[512,512]{1,0:T(8,128)(2,1)}), bf16[2048,512]{1,0:T(8,128)(2,1)}) %all-gather.16.cloned.1.call-update) | async-done | bytes 2097168 | tf_op jit(solution)/shard_map/all_gather | solution.py:142
  68.4 57.6 %all-gather.14.cloned.1.call-done = bf16[2048,2048]{1,0:T(8,128)(2,1)} async-done(((bf16[256,2048]{1,0:T(8,128)(2,1)}), bf16[2048,2048]{1,0:T(8,128)(2,1)}) %all-gather.14.cloned.1.call-update) | async-done | bytes 8388624 | tf_op jit(solution)/shard_map/all_gather | solution.py:132
  135.4 78.5 %all-gather.18.cloned.1.call-done = bf16[4,2048,256]{2,1,0:T(8,128)(2,1)} async-done(((bf16[1,2048,256]{2,1,0:T(8,128)(2,1)}), bf16[4,2048,256]{2,1,0:T(8,128)(2,1)}) %all-gather.18.cloned.1.call-update) | async-done | bytes 4194320 | tf_op jit(solution)/shard_map/all_gather | solution.py:253
  215.9 15.8 %all-gather.1.kseg_ref = s32[8,1,1024]{2,1,0:T(1,128)S(1)} all-gather(s32[2,1,1024]{2,1,0:T(1,128)S(1)} %copy-done.30), channel_id=3, replica_groups=mesh['x'=2,'core'=2,'z'=4,'y'=2] {'x','core'}, dimensions={0}, use_global_device_ids=true | all-gather | bytes 40960 | tf_op jit(solution)/shard_map/all_gather | solution.py:244
  275.4 17.6 %all_to_all.97 = bf16[64,8,1024]{2,0,1:T(8,128)(2,1)} all-to-all(bf16[64,8,1024]{2,0,1:T(8,128)(2,1)S(1)} %bitcast.268), channel_id=1, replica_groups=mesh['x'=2,'core'=2,'z'=4,'y'=2] {'x','core','y'}, dimensions={1} | all-to-all | bytes 2097152 | tf_op jit(solution)/shard_map/all_to_all | solution.py:140
  293.2 51.7 %reduce-scatter.12.cloned.1.call-done = bf16[256,2048]{1,0:T(8,128)(2,1)} async-done(((bf16[2048,2048]{1,0:T(8,128)(2,1)}), bf16[256,2048]{1,0:T(8,128)(2,1)}) %reduce-scatter.12.cloned.1.call-update) | async-done | bytes 1048592 | tf_op jit(solution)/shard_map/reduce_scatter | solution.py:136
  350.0 17.6 %all_to_all.98 = bf16[64,8,1024]{2,0,1:T(8,128)(2,1)} all-to-all(bf16[64,8,1024]{2,0,1:T(8,128)(2,1)S(1)} %bitcast.269), channel_id=1, replica_groups=mesh['x'=2,'core'=2,'z'=4,'y'=2] {'x','core','y'}, dimensions={1} | all-to-all | bytes 2097152 | tf_op jit(solution)/shard_map/all_to_all | solution.py:140
  369.1 17.6 %all_to_all.99 = bf16[64,8,1024]{2,0,1:T(8,128)(2,1)} all-to-all(bf16[64,8,1024]{2,0,1:T(8,128)(2,1)S(1)} %bitcast.273), channel_id=1, replica_groups=mesh['x'=2,'core'=2,'z'=4,'y'=2] {'x','core','y'}, dimensions={1} | all-to-all | bytes 2097152 | tf_op jit(solution)/shard_map/all_to_all | solution.py:140
  391.7 33.4 %all-gather.24.cloned.1.call-done = bf16[2048,1024]{1,0:T(8,128)(2,1)} async-done(((bf16[512,1024]{1,0:T(8,128)(2,1)}), bf16[2048,1024]{1,0:T(8,128)(2,1)}) %all-gather.24.cloned.1.call-update) | async-done | bytes 4194320 | tf_op jit(solution)/shard_map/all_gather | solution.py:142
  425.1 57.9 %all-gather.22.cloned.1.call-done = bf16[2048,2048]{1,0:T(8,128)(2,1)} async-done(((bf16[256,2048]{1,0:T(8,128)(2,1)}), bf16[2048,2048]{1,0:T(8,128)(2,1)}) %all-gather.22.cloned.1.call-update) | async-done | bytes 8388624 | tf_op jit(solution)/shard_map/all_gather | solution.py:132
  483.0 14.5 fusion.46
  497.5 65.7 %all-gather.26.cloned.1.call-done = bf16[2048,1024]{1,0:T(8,128)(2,1)} async-done(((bf16[512,1024]{1,0:T(8,128)(2,1)}), bf16[2048,1024]{1,0:T(8,128)(2,1)}) %all-gather.26.cloned.1.call-update) | async-done | bytes 4194320 | tf_op jit(solution)/shard_map/all_gather | solution.py:142
  563.1 14.4 fusion.47
  577.5 66.4 %all-gather.28.cloned.1.call-done = bf16[2048,1024]{1,0:T(8,128)(2,1)} async-done(((bf16[512,1024]{1,0:T(8,128)(2,1)}), bf16[2048,1024]{1,0:T(8,128)(2,1)}) %all-gather.28.cloned.1.call-update) | async-done | bytes 4194320 | tf_op jit(solution)/shard_map/all_gather | solution.py:142
  643.9 57.3 %all-gather.30.cloned.1.call-done = bf16[2048,2048]{1,0:T(8,128)(2,1)} async-done(((bf16[256,2048]{1,0:T(8,128)(2,1)}), bf16[2048,2048]{1,0:T(8,128)(2,1)}) %all-gather.30.cloned.1.call-update) | async-done | bytes 8388624 | tf_op jit(solution)/shard_map/all_gather | solution.py:132
  701.3 22.0 %multiply_convert_fusion = (bf16[2048,1024]{1,0:T(8,128)(2,1)}, bf16[2048,1024]{1,0:T(8,128)(2,1)}, bf16[2048,1024]{1,0:T(8,128)(2,1)}) fusion(f32[2048,1024]{1,0:T(8,128)} %fusion.46, f32[2048,1024]{1,0:T(8,128)} %fusion.47, bf16[2048,2048]{1,0:T(8,128)(2,1)} %all-gather.30.cloned.1.call-done, bf16[2048,1024]{1,0:T(8,128)(2,1)} %all-gather.28.cloned.1.call-done), kind=kOutput, calls=%fused_computation.2 | convolution fusion | flops 8621391872 | bytes 41943040 | tf_op jit(solution)/shard_map/dot_general | solution.py:26
  723.3 14.2 fusion.48
  737.5 16.4 %add_convert_fusion = bf16[2048,2048]{1,0:T(8,128)(2,1)} fusion(f32[2048,2048]{1,0:T(8,128)} %fusion.48, bf16[2048,1024]{1,0:T(8,128)(2,1)} %get-tuple-element.17, bf16[2048,1024]{1,0:T(8,128)(2,1)} %all-gather.26.cloned.1.call-done), kind=kOutput, calls=%fused_computation | convolution fusion | flops 8598323200 | bytes 33554432 | tf_op jit(solution)/shard_map/dot_general | solution.py:30
  754.0 71.2 %reduce-scatter.16.cloned.1.call-done = bf16[256,2048]{1,0:T(8,128)(2,1)} async-done(((bf16[2048,2048]{1,0:T(8,128)(2,1)}), bf16[256,2048]{1,0:T(8,128)(2,1)}) %reduce-scatter.16.cloned.1.call-update) | async-done | bytes 1048592 | tf_op jit(solution)/shard_map/reduce_scatter | solution.py:136
  830.1 54.7 %all-gather.32.cloned.1.call-done = bf16[2048,2048]{1,0:T(8,128)(2,1)} async-done(((bf16[256,2048]{1,0:T(8,128)(2,1)}), bf16[2048,2048]{1,0:T(8,128)(2,1)}) %all-gather.32.cloned.1.call-update) | async-done | bytes 8388624 | tf_op jit(solution)/shard_map/all_gather | solution.py:132
  890.7 15.7 %attention_backward.1 = (f32[4,2,2,128,256]{4,3,2,1,0:T(8,128)S(1)}, bf16[4,4,2,2,128,256]{5,4,3,2,1,0:T(8,128)(2,1)}, bf16[4,4,2,2,128,256]{5,4,3,2,1,0:T(8,128)(2,1)}) custom-call(bf16[4,2,2,128,256]{4,3,2,1,0:T(8,128)(2,1)S(1)} %pad_maximum_fusion.2.q_ref, bf16[4,4,2,2,128,256]{5,4,3,2,1,0:T(8,128)(2,1)} %bitcast.251, ...), custom_call_target="tpu_custom_call" | custom-call | flops 5368709120 | bytes 16777216 | tf_op jit(solution)/shard_map/attention_backward/pallas_call | solution.py:111
  915.4 17.6 %reduce-scatter.18.cloned.1.call-done = bf16[1,4,4,2,2,128,256]{6,5,4,3,2,1,0:T(8,128)(2,1)} async-done(((bf16[2,4,4,2,2,128,256]{6,5,4,3,2,1,0:T(8,128)(2,1)}), bf16[1,4,4,2,2,128,256]{6,5,4,3,2,1,0:T(8,128)(2,1)}) %reduce-scatter.18.cloned.1.call-update) | async-done | bytes 4194320 | tf_op jit(solution)/shard_map/reduce_scatter | solution.py:284
  947.1 14.1 convolution_convert_fusion.3
  961.3 14.5 convert_bitcast_fusion
  983.8 28.3 %reduce-scatter.20.cloned.1.call-done = bf16[1,4,2,2,128,256]{5,4,3,2,1,0:T(8,128)(2,1)} async-done(((bf16[4,4,2,2,128,256]{5,4,3,2,1,0:T(8,128)(2,1)}), bf16[1,4,2,2,128,256]{5,4,3,2,1,0:T(8,128)(2,1)}) %reduce-scatter.20.cloned.1.call-update) | async-done | bytes 1048592 | tf_op jit(solution)/shard_map/reduce_scatter | solution.py:285
  1033.9 14.3 convolution_convert_fusion.1
  1048.2 43.3 %reduce-scatter.28.cloned.1.call-done = bf16[512,1024]{1,0:T(8,128)(2,1)} async-done(((bf16[2048,1024]{1,0:T(8,128)(2,1)}), bf16[512,1024]{1,0:T(8,128)(2,1)}) %reduce-scatter.28.cloned.1.call-update) | async-done | bytes 1048592 | tf_op jit(solution)/shard_map/reduce_scatter | solution.py:146
  1100.7 70.3 %reduce-scatter.30.cloned.1.call-done = bf16[512,1024]{1,0:T(8,128)(2,1)} async-done(((bf16[2048,1024]{1,0:T(8,128)(2,1)}), bf16[512,1024]{1,0:T(8,128)(2,1)}) %reduce-scatter.30.cloned.1.call-update) | async-done | bytes 1048592 | tf_op jit(solution)/shard_map/reduce_scatter | solution.py:146
  1180.0 70.5 %reduce-scatter.32.cloned.1.call-done = bf16[512,1024]{0,1:T(8,128)(2,1)} async-done(((bf16[2048,1024]{0,1:T(8,128)(2,1)}), bf16[512,1024]{0,1:T(8,128)(2,1)}) %reduce-scatter.32.cloned.1.call-update) | async-done | bytes 1048592 | tf_op jit(solution)/shard_map/reduce_scatter | solution.py:146
  1290.8 37.2 %reduce-scatter.24.cloned.1.call-done = bf16[512,512]{1,0:T(8,128)(2,1)} async-done(((bf16[2048,512]{1,0:T(8,128)(2,1)}), bf16[512,512]{1,0:T(8,128)(2,1)}) %reduce-scatter.24.cloned.1.call-update) | async-done | bytes 524304 | tf_op jit(solution)/shard_map/reduce_scatter | solution.py:146
  1365.7 39.8 %reduce-scatter.22.cloned.1.call-done = bf16[256,2048]{1,0:T(8,128)(2,1)} async-done(((bf16[2048,2048]{1,0:T(8,128)(2,1)}), bf16[256,2048]{1,0:T(8,128)(2,1)}) %reduce-scatter.22.cloned.1.call-update) | async-done | bytes 1048592 | tf_op jit(solution)/shard_map/reduce_scatter | solution.py:136
  1407.2 73.1 %reduce-scatter.14.cloned.1.call-done = bf16[256,2048]{1,0:T(8,128)(2,1)} async-done(((bf16[2048,2048]{1,0:T(8,128)(2,1)}), bf16[256,2048]{1,0:T(8,128)(2,1)}) %reduce-scatter.14.cloned.1.call-update) | async-done | bytes 1048592 | tf_op jit(solution)/shard_map/reduce_scatter | solution.py:136
  (241 shorter events, 268.9 us)
Async XLA Ops:
  7.2 61.2 %all-gather.16.cloned.1.call-start = ((), (), s32[]{:S(2)}) async-start(), calls=%async_computation.20 | async-start | bytes 2621440 | tf_op jit(solution)/shard_map/all_gather | solution.py:142
  24.1 101.9 %all-gather.14.cloned.1.call-start = ((), (), s32[]{:S(2)}) async-start(), calls=%async_computation.19 | async-start | bytes 9437184 | tf_op jit(solution)/shard_map/all_gather | solution.py:132
  29.8 103.7 %copy-start.4 = (f32[256,2048]{1,0:T(8,128)}, f32[256,2048]{1,0:T(8,128)S(1)}, u32[]{:S(2)}) copy-start(f32[256,2048]{1,0:T(8,128)S(1)} %reshape.300) | copy-start | bytes 6291460
  32.1 181.8 %all-gather.18.cloned.1.call-start = ((), (), s32[]{:S(2)}) async-start(), calls=%async_computation.21 | async-start | bytes 5242880 | tf_op jit(solution)/shard_map/all_gather | solution.py:253
  32.7 100.8 %copy-start.15 = (f32[2,128,128]{2,1,0:T(8,128)}, f32[2,128,128]{2,1,0:T(8,128)S(1)}, u32[]{:S(2)}) copy-start(f32[2,128,128]{2,1,0:T(8,128)S(1)} %get-tuple-element.48) | copy-start | bytes 393220
  32.8 100.8 %copy-start.17 = (f32[2,128,128]{2,1,0:T(8,128)}, f32[2,128,128]{2,1,0:T(8,128)S(1)}, u32[]{:S(2)}) copy-start(f32[2,128,128]{2,1,0:T(8,128)S(1)} %get-tuple-element.49) | copy-start | bytes 393220
  134.2 81.7 %copy-start.30 = (s32[2,1,1024]{2,1,0:T(1,128)S(1)}, s32[2,1,1024]{2,1,0:T(1,128)}, u32[]{:S(2)}) copy-start(s32[2,1,1024]{2,1,0:T(1,128)} %param.13) | copy-start | bytes 24580
  135.3 101.4 %all-gather.34.cloned.1.call-start = ((), (), s32[]{:S(2)}) async-start(), calls=%async_computation.40 | async-start | bytes 12582912 | tf_op jit(solution)/shard_map/all_gather | solution.py:253
  213.9 51.9 %all-gather.20.cloned.1.call-start = ((), (), s32[]{:S(2)}) async-start(), calls=%async_computation.22 | async-start | bytes 1310720 | tf_op jit(solution)/shard_map/all_gather | solution.py:220
  214.5 0.7 collective-permute-start
  215.9 128.9 %reduce-scatter.12.cloned.1.call-start = ((), (), s32[]{:S(2)}) async-start(), calls=%async_computation.23 | async-start | bytes 9437184 | tf_op jit(solution)/shard_map/reduce_scatter | solution.py:136
  272.8 152.3 %all-gather.24.cloned.1.call-start = ((), (), s32[]{:S(2)}) async-start(), calls=%async_computation.25 | async-start | bytes 5242880 | tf_op jit(solution)/shard_map/all_gather | solution.py:142
  293.1 189.9 %all-gather.22.cloned.1.call-start = ((), (), s32[]{:S(2)}) async-start(), calls=%async_computation.24 | async-start | bytes 9437184 | tf_op jit(solution)/shard_map/all_gather | solution.py:132
  349.9 213.2 %all-gather.26.cloned.1.call-start = ((), (), s32[]{:S(2)}) async-start(), calls=%async_computation.26 | async-start | bytes 5242880 | tf_op jit(solution)/shard_map/all_gather | solution.py:142
  367.7 276.2 %all-gather.28.cloned.1.call-start = ((), (), s32[]{:S(2)}) async-start(), calls=%async_computation.27 | async-start | bytes 5242880 | tf_op jit(solution)/shard_map/all_gather | solution.py:142
  386.7 314.6 %all-gather.30.cloned.1.call-start = ((), (), s32[]{:S(2)}) async-start(), calls=%async_computation.29 | async-start | bytes 9437184 | tf_op jit(solution)/shard_map/all_gather | solution.py:132
  391.7 433.5 %reduce-scatter.16.cloned.1.call-start = ((), (), s32[]{:S(2)}) async-start(), calls=%async_computation.30 | async-start | bytes 9437184 | tf_op jit(solution)/shard_map/reduce_scatter | solution.py:136
  753.9 130.8 %all-gather.32.cloned.1.call-start = ((), (), s32[]{:S(2)}) async-start(), calls=%async_computation.31 | async-start | bytes 9437184 | tf_op jit(solution)/shard_map/all_gather | solution.py:132
  830.0 102.9 %reduce-scatter.18.cloned.1.call-start = ((), (), s32[]{:S(2)}) async-start(), calls=%async_computation.32 | async-start | bytes 12582912 | tf_op jit(solution)/shard_map/reduce_scatter | solution.py:284
  915.3 96.7 %reduce-scatter.20.cloned.1.call-start = ((), (), s32[]{:S(2)}) async-start(), calls=%async_computation.33 | async-start | bytes 5242880 | tf_op jit(solution)/shard_map/reduce_scatter | solution.py:285
  933.0 158.5 %reduce-scatter.28.cloned.1.call-start = ((), (), s32[]{:S(2)}) async-start(), calls=%async_computation.37 | async-start | bytes 5242880 | tf_op jit(solution)/shard_map/reduce_scatter | solution.py:146
  947.1 224.0 %reduce-scatter.30.cloned.1.call-start = ((), (), s32[]{:S(2)}) async-start(), calls=%async_computation.38 | async-start | bytes 5242880 | tf_op jit(solution)/shard_map/reduce_scatter | solution.py:146
  961.2 289.3 %reduce-scatter.32.cloned.1.call-start = ((), (), s32[]{:S(2)}) async-start(), calls=%async_computation.39 | async-start | bytes 5242880 | tf_op jit(solution)/shard_map/reduce_scatter | solution.py:146
  975.8 313.3 %reduce-scatter.26.cloned.1.call-start = ((), (), s32[]{:S(2)}) async-start(), calls=%async_computation.36 | async-start | bytes 1310720 | tf_op jit(solution)/shard_map/reduce_scatter | solution.py:296
  983.7 344.3 %reduce-scatter.24.cloned.1.call-start = ((), (), s32[]{:S(2)}) async-start(), calls=%async_computation.35 | async-start | bytes 2621440 | tf_op jit(solution)/shard_map/reduce_scatter | solution.py:146
  1025.4 380.2 %reduce-scatter.22.cloned.1.call-start = ((), (), s32[]{:S(2)}) async-start(), calls=%async_computation.34 | async-start | bytes 9437184 | tf_op jit(solution)/shard_map/reduce_scatter | solution.py:136
  1033.9 446.4 %reduce-scatter.14.cloned.1.call-start = ((), (), s32[]{:S(2)}) async-start(), calls=%async_computation.28 | async-start | bytes 9437184 | tf_op jit(solution)/shard_map/reduce_scatter | solution.py:136
  1096.3 79.0 %all-to-all-start.5 = ((bf16[8,2,32768]{2,1,0:T(2,128)(2,1)}), bf16[8,2,32768]{2,1,0:T(2,128)(2,1)S(1)}, u32[]{:S(2)}, u32[]{:S(2)}) async-start(bf16[8,2,32768]{2,1,0:T(2,128)(2,1)} %reshape.328), calls=%async_computation.14 | async-start | bytes 2097152 | tf_op jit(solution)/shard_map/all_to_all | solution.py:148
  1175.3 86.2 %all-to-all-start.6 = ((bf16[8,2,32768]{2,1,0:T(2,128)(2,1)}), bf16[8,2,32768]{2,1,0:T(2,128)(2,1)}, u32[]{:S(2)}, u32[]{:S(2)}) async-start(bf16[8,2,32768]{2,1,0:T(2,128)(2,1)} %reshape.330), calls=%async_computation.16 | async-start | bytes 2097152 | tf_op jit(solution)/shard_map/all_to_all | solution.py:148
  1261.5 21.1 %all-to-all-start.7 = ((bf16[8,2,32768]{2,1,0:T(2,128)(2,1)}), bf16[8,2,32768]{2,1,0:T(2,128)(2,1)}, u32[]{:S(2)}, u32[]{:S(2)}) async-start(bf16[8,2,32768]{2,1,0:T(2,128)(2,1)} %reshape.332), calls=%async_computation.18 | async-start | bytes 2097152 | tf_op jit(solution)/shard_map/all_to_all | solution.py:148
  1289.1 54.4 %collective-permute-start.1 = (bf16[64,2048]{1,0:T(8,128)(2,1)}, bf16[64,2048]{1,0:T(8,128)(2,1)S(1)}, u32[]{:S(2)}, u32[]{:S(2)}) collective-permute-start(bf16[64,2048]{1,0:T(8,128)(2,1)} %reduce-scatter.26.cloned.1.call-done), channel_id=1, source_target_pairs={{0,0},{2,1},{4,2},{6,3},{1,8},{3,9},{5,10},{7,11},{8,4},{10,5},{12... | collective-permute-start | bytes 786440 | tf_op jit(solution)/shard_map/ppermute | solution.py:299
  1333.0 12.9 all-to-all-start.4
  (34 other events, 730.0 us)
Sparse Core Ops, SparseCore 0:
  24.2 44.1 all-gather.15
  70.8 55.1 all-gather.13
  135.5 78.3 all-gather.17
  215.3 21.3 all-gather.33
  238.7 27.1 all-gather.19
  272.9 71.8 reduce-scatter.11
  346.5 78.5 all-gather.23
  427.7 55.2 all-gather.21
  484.7 78.4 all-gather.25
  564.6 79.2 all-gather.27
  646.0 55.2 all-gather.29
  754.0 71.0 reduce-scatter.15
  830.1 54.5 all-gather.31
  915.4 17.4 reduce-scatter.17
  935.2 76.8 reduce-scatter.19
  1014.2 77.2 reduce-scatter.27
  1093.8 77.2 reduce-scatter.29
  1173.2 77.2 reduce-scatter.31
  1253.5 25.4 reduce-scatter.25
  1281.7 46.3 reduce-scatter.23
  1331.9 73.5 reduce-scatter.21
  1409.0 71.2 reduce-scatter.13

commit v2 on v1

v2 whole, which is shorter than its diff:
```python
import functools

import jax
import jax.numpy as jnp
from jax import lax
from jax.experimental import pallas as pl
from jax.experimental.pallas import tpu as pltpu
from jax.sharding import Mesh
from jax.sharding import PartitionSpec as P

HEADS = 8
KV_HEADS = 4
HEAD_DIM = 256
WINDOW = 1024
NORM_EPS = 1e-06
ROPE_BASE = 1000042.0
NEG_LARGE = -1e30
SCALE = HEAD_DIM**-0.5
PLANE = ("x", "core", "y")
EVERY = ("x", "core", "z", "y")
BF16 = jnp.bfloat16
F32 = jnp.float32
MESH = pl.DeviceIdType.MESH
GATHER_PARTS = 4
SCATTER_PARTS = 4
CORE_PARTS = 4


def dot_nn(a, b):
    return lax.dot_general(a, b, (((1,), (0,)), ((), ())), preferred_element_type=F32)


def dot_nt(a, b):
    return lax.dot_general(a, b, (((1,), (1,)), ((), ())), preferred_element_type=F32)


def dot_tn(a, b):
    return lax.dot_general(a, b, (((0,), (0,)), ((), ())), preferred_element_type=F32)


def rotate(values, cosine, sine):
    half = values.shape[-1] // 2
    a, b = values[:, :half], values[:, half:]
    return jnp.concatenate([a * cosine - b * sine, b * cosine + a * sine], -1)


QUERY_ROWS = 256


def query_blocks(seq_len):
    out = []
    for first in range(0, seq_len, QUERY_ROWS):
        low = max(0, first - WINDOW + 1) // 128 * 128
        out.append((first, low, min(seq_len, first + QUERY_ROWS)))
    return out


def masked_prob(q, k, first, low, qseg, kseg):
    scores = dot_nt(q, k) * SCALE
    qpos = first + lax.broadcasted_iota(jnp.int32, scores.shape, 0)
    kpos = low + lax.broadcasted_iota(jnp.int32, scores.shape, 1)
    allowed = (kpos <= qpos) & (qpos - kpos < WINDOW) & (qseg == kseg)
    masked = jnp.where(allowed, scores, NEG_LARGE)
    e = jnp.exp(masked - jnp.max(masked, -1, keepdims=True))
    return e / jnp.sum(e, -1, keepdims=True)


def attn_fwd_kernel(q_ref, k_ref, v_ref, qseg_ref, kseg_ref, o_ref):
    for first, low, end in query_blocks(q_ref.shape[0]):
        rows, keys = pl.ds(first, QUERY_ROWS), pl.ds(low, end - low)
        prob = masked_prob(q_ref[rows, :], k_ref[keys, :], first, low, qseg_ref[rows, :], kseg_ref[:, keys])
        o_ref[rows, :] = dot_nn(prob.astype(BF16), v_ref[keys, :]).astype(BF16)


def attn_bwd_kernel(q_ref, k_ref, v_ref, do_ref, qseg_ref, kseg_ref, *refs):
    dq_ref, dkv_ref, dk_sum, dv_sum = refs[-4:]
    dk_sum[...] = jnp.zeros_like(dk_sum)
    dv_sum[...] = jnp.zeros_like(dv_sum)
    for first, low, end in query_blocks(q_ref.shape[0]):
        rows, keys = pl.ds(first, QUERY_ROWS), pl.ds(low, end - low)
        q, k, v, do = q_ref[rows, :], k_ref[keys, :], v_ref[keys, :], do_ref[rows, :]
        prob = masked_prob(q, k, first, low, qseg_ref[rows, :], kseg_ref[:, keys])
        dprob = dot_nt(do, v)
        ds = prob * (dprob - jnp.sum(prob * dprob, -1, keepdims=True))
        dsb = ds.astype(BF16)
        dq_ref[rows, :] = dot_nn(dsb, k) * SCALE
        dk_sum[keys, :] += dot_tn(dsb, q)
        dv_sum[keys, :] += dot_tn(prob.astype(BF16), do)
    dkv_ref[0] = (dk_sum[...] * SCALE).astype(BF16)
    dkv_ref[1] = dv_sum[...].astype(BF16)


def attention_specs(seq_len):
    qspec = pl.BlockSpec((None, seq_len, HEAD_DIM), lambda s: (s, 0, 0))
    kspec = pl.BlockSpec((None, None, seq_len, HEAD_DIM), lambda s: (0, s, 0, 0))
    vspec = pl.BlockSpec((None, None, seq_len, HEAD_DIM), lambda s: (1, s, 0, 0))
    qseg = pl.BlockSpec((None, seq_len, 1), lambda s: (s, 0, 0))
    kseg = pl.BlockSpec((None, 1, seq_len), lambda s: (s, 0, 0))
    return qspec, kspec, vspec, qseg, kseg


def attn_forward(q, kv, qseg, kseg):
    seqs, seq_len, _ = q.shape
    qspec, kspec, vspec, qi, ks = attention_specs(seq_len)
    return pl.pallas_call(
        attn_fwd_kernel,
        grid=(seqs,),
        in_specs=[qspec, kspec, vspec, qi, ks],
        out_specs=qspec,
        out_shape=jax.ShapeDtypeStruct(q.shape, BF16),
        compiler_params=pltpu.CompilerParams(vmem_limit_bytes=48 << 20),
        cost_estimate=light(),
        name="attention_forward",
    )(q, kv, kv, qseg, kseg)


def attn_backward(q, kv, do, qseg, kseg, *earlier):
    seqs, seq_len, _ = q.shape
    qspec, kspec, vspec, qi, ks = attention_specs(seq_len)
    return pl.pallas_call(
        attn_bwd_kernel,
        grid=(seqs,),
        in_specs=[qspec, kspec, vspec, qspec, qi, ks] + [ANY] * len(earlier),
        out_specs=[qspec, pl.BlockSpec((2, None, seq_len, HEAD_DIM), lambda s: (0, s, 0, 0))],
        out_shape=[
            jax.ShapeDtypeStruct(q.shape, F32),
            jax.ShapeDtypeStruct((2, *q.shape), BF16),
        ],
        scratch_shapes=[pltpu.VMEM((seq_len, HEAD_DIM), F32)] * 2,
        compiler_params=pltpu.CompilerParams(vmem_limit_bytes=48 << 20),
        cost_estimate=light(),
        name="attention_backward",
    )(q, kv, kv, do, qseg, kseg, *earlier)


NUMBERS = [0]


def fresh():
    NUMBERS[0] += 1
    return NUMBERS[0] - 1


def flips():
    x, c, y = (lax.axis_index(a) for a in PLANE)
    return x, c, y, {"x": 1 - x}, {"y": 1 - y}, {"core": 1 - c}


def greet(*targets):
    barrier = pltpu.get_barrier_semaphore()
    for target in targets:
        pl.semaphore_signal(barrier, 1, device_id=target, device_id_type=MESH)
    pl.semaphore_wait(barrier, len(targets))


def pieces_at(ref, split, px, pc, py):
    return ref.at[pc, :, px, py] if split == 2 else ref.at[:, pc, px, py]


def plane_shape(split, slots, *rest):
    return (2, slots, 2, 2, *rest) if split == 2 else (slots, 2, 2, 2, *rest)


def gather_kernel(split, a_ref, *refs):
    o_ref, own_sem, send_sem, recv_sem = refs[-4:]
    x, c, y, to_x, to_y, to_c = flips()
    slots, piece, _ = a_ref.shape
    per_slot = GATHER_PARTS // slots
    step = piece // per_slot
    greet(to_x, to_y, to_c)

    def rows_of(i):
        return i // per_slot, pl.ds(i % per_slot * step, step)

    def part(px, pc, py, i):
        return pieces_at(o_ref, split, px, pc, py).at[rows_of(i)]

    def send(kind, i, src, dst, target):
        copy = pltpu.make_async_remote_copy(
            src_ref=src, dst_ref=dst, send_sem=send_sem.at[kind, i], recv_sem=recv_sem.at[kind, i],
            device_id=target, device_id_type=MESH,
        )
        copy.start()
        return copy

    own_copy = pltpu.make_async_copy(a_ref, pieces_at(o_ref, split, x, c, y), own_sem)
    own_copy.start()
    copies = {}
    for i in range(GATHER_PARTS):
        own = a_ref.at[rows_of(i)]
        for kind, target in enumerate((to_x, to_y, to_c)):
            copies[kind, i] = send(kind, i, own, part(x, c, y, i), target)
    src_x, src_y = jnp.where(c == 0, x, 1 - x), jnp.where(c == 0, 1 - y, y)
    dst_x, dst_y = jnp.where(c == 0, 1 - x, x), jnp.where(c == 0, y, 1 - y)
    for i in range(GATHER_PARTS):
        for kind, (px, py) in enumerate(((1 - x, y), (x, 1 - y))):
            copies[kind, i].wait_recv()
            block = part(px, c, py, i)
            copies[3 + kind, i] = send(3 + kind, i, block, block, to_c)
        block = part(src_x, c, src_y, i)
        copies[5, i] = send(5, i, block, block, {"x": dst_x, "y": dst_y})
    for i in range(GATHER_PARTS):
        copies[5, i].wait_recv()
        block = part(1 - x, c, 1 - y, i)
        copies[6, i] = send(6, i, block, block, to_c)
    for i in range(GATHER_PARTS):
        for kind in (2, 3, 4, 6):
            copies[kind, i].wait_recv()
    own_copy.wait()
    for i in range(GATHER_PARTS):
        for kind in range(7):
            copies[kind, i].wait_send()


ANY = pl.BlockSpec(memory_space=pl.ANY)
WHOLE = pl.BlockSpec(memory_space=pltpu.VMEM)


def light(bytes_accessed=1024):
    return pl.CostEstimate(flops=0, bytes_accessed=bytes_accessed, transcendentals=0)


def plane_gather(a, split, *earlier):
    slots, piece, width = a.shape
    out = pl.pallas_call(
        functools.partial(gather_kernel, split),
        out_shape=jax.ShapeDtypeStruct(plane_shape(split, slots, piece, width), a.dtype),
        in_specs=[WHOLE] + [ANY] * len(earlier),
        out_specs=ANY,
        scratch_shapes=[
            pltpu.SemaphoreType.DMA,
            pltpu.SemaphoreType.DMA((7, GATHER_PARTS)),
            pltpu.SemaphoreType.DMA((7, GATHER_PARTS)),
        ],
        compiler_params=pltpu.CompilerParams(collective_id=fresh(), has_side_effects=True),
        cost_estimate=light(),
        name="plane_gather",
    )(a, *earlier)
    return out.reshape(-1, width)


def scatter_kernel(split, p_ref, *refs):
    o_ref, own, got_c, put_x, put_y, got_x, got_y, fin_x, fin_y, end_x, end_y, own_sem, send_sem, recv_sem = refs[-14:]
    x, c, y, to_x, to_y, to_c = flips()
    parts, _, _, step, width = own.shape
    slots, piece, _ = o_ref.shape
    per_slot = parts // slots
    half = width // 2
    left, right = pl.ds(0, half), pl.ds(half, half)
    greet(to_x, to_y, to_c)

    def send(kind, i, src, dst, target):
        copy = pltpu.make_async_remote_copy(
            src_ref=src.at[i] if kind else src, dst_ref=dst.at[i],
            send_sem=send_sem.at[kind, i], recv_sem=recv_sem.at[kind, i],
            device_id=target, device_id_type=MESH,
        )
        copy.start()
        return copy

    loads, first, second, third = [], [], [], []
    def rows_of(i):
        return i // per_slot, pl.ds(i % per_slot * step, step)

    def blocks(pc, i):
        slot, rows = rows_of(i)
        return p_ref.at[pc, slot, :, :, rows, :] if split == 2 else p_ref.at[slot, pc, :, :, rows, :]

    for i in range(parts):
        first.append(send(0, i, blocks(1 - c, i), got_c, to_c))
        load = pltpu.make_async_copy(blocks(c, i), own.at[i], own_sem.at[i])
        load.start()
        loads.append(load)

    def f32(ref, *index):
        return ref[index].astype(F32)

    for i in range(parts):
        loads[i].wait()
        first[i].wait_recv()
        for j in range(2):
            put_x[i, j] = (f32(own, i, 1 - x, j, slice(None), left) + f32(got_c, i, 1 - x, j, slice(None), left)).astype(BF16)
            put_y[i, j] = (f32(own, i, j, 1 - y, slice(None), right) + f32(got_c, i, j, 1 - y, slice(None), right)).astype(BF16)
        second.append((send(1, i, put_x, got_x, to_x), send(2, i, put_y, got_y, to_y)))
    for i in range(parts):
        for copy in second[i]:
            copy.wait_recv()
        fin_y[i] = (
            f32(own, i, x, 1 - y, slice(None), left) + f32(got_c, i, x, 1 - y, slice(None), left) + f32(got_x, i, 1 - y)
        ).astype(BF16)
        fin_x[i] = (
            f32(own, i, 1 - x, y, slice(None), right) + f32(got_c, i, 1 - x, y, slice(None), right) + f32(got_y, i, 1 - x)
        ).astype(BF16)
        third.append((send(3, i, fin_y, end_y, to_y), send(4, i, fin_x, end_x, to_x)))
    for i in range(parts):
        for copy in third[i]:
            copy.wait_recv()
        slot, rows = rows_of(i)
        o_ref[slot, rows, left] = (
            f32(own, i, x, y, slice(None), left) + f32(got_c, i, x, y, slice(None), left)
            + f32(got_x, i, y) + f32(end_y, i)
        )
        o_ref[slot, rows, right] = (
            f32(own, i, x, y, slice(None), right) + f32(got_c, i, x, y, slice(None), right)
            + f32(got_y, i, x) + f32(end_x, i)
        )
    for i in range(parts):
        for copy in (first[i], *second[i], *third[i]):
            copy.wait_send()


def plane_scatter(a, split, slots, *earlier):
    rows, width = a.shape[0] // 8, a.shape[1]
    piece = rows // slots
    n = SCATTER_PARTS
    step, half = rows // n, width // 2
    return pl.pallas_call(
        functools.partial(scatter_kernel, split),
        out_shape=jax.ShapeDtypeStruct((slots, piece, width), F32),
        in_specs=[ANY] * (1 + len(earlier)),
        out_specs=WHOLE,
        scratch_shapes=[
            pltpu.VMEM((n, 2, 2, step, width), BF16),
            pltpu.VMEM((n, 2, 2, step, width), BF16),
            pltpu.VMEM((n, 2, step, half), BF16),
            pltpu.VMEM((n, 2, step, half), BF16),
            pltpu.VMEM((n, 2, step, half), BF16),
            pltpu.VMEM((n, 2, step, half), BF16),
            pltpu.VMEM((n, step, half), BF16),
            pltpu.VMEM((n, step, half), BF16),
            pltpu.VMEM((n, step, half), BF16),
            pltpu.VMEM((n, step, half), BF16),
            pltpu.SemaphoreType.DMA((n,)),
            pltpu.SemaphoreType.DMA((5, n)),
            pltpu.SemaphoreType.DMA((5, n)),
        ],
        compiler_params=pltpu.CompilerParams(
            collective_id=fresh(), has_side_effects=True, vmem_limit_bytes=32 << 20
        ),
        cost_estimate=light(),
        name="plane_scatter",
    )(a.reshape(plane_shape(split, slots, piece, width)), *earlier)


def pair_kernel(a_ref, *refs):
    o_ref, own_sem, send_sem, recv_sem = refs[-4:]
    c = lax.axis_index("core")
    greet({"core": 1 - c})
    keep = pltpu.make_async_copy(a_ref, o_ref.at[c], own_sem)
    keep.start()
    copy = pltpu.make_async_remote_copy(
        src_ref=a_ref, dst_ref=o_ref.at[c], send_sem=send_sem, recv_sem=recv_sem,
        device_id={"core": 1 - c}, device_id_type=MESH,
    )
    copy.start()
    keep.wait()
    copy.wait()


def core_gather(a, *earlier):
    return pl.pallas_call(
        pair_kernel,
        out_shape=jax.ShapeDtypeStruct((2, *a.shape), a.dtype),
        in_specs=[WHOLE] + [ANY] * len(earlier),
        out_specs=ANY,
        scratch_shapes=[pltpu.SemaphoreType.DMA] * 3,
        compiler_params=pltpu.CompilerParams(
            collective_id=fresh(), has_side_effects=True, vmem_limit_bytes=32 << 20
        ),
        cost_estimate=light(),
        name="core_gather",
    )(a, *earlier)


def pair_sum_kernel(a_ref, *refs):
    o_ref, own, got, out, own_sem, out_sem, send_sem, recv_sem = refs[-8:]
    c = lax.axis_index("core")
    parts, step, _ = own.shape
    greet({"core": 1 - c})
    copies, loads, stores = [], [], []
    for i in range(parts):
        rows = pl.ds(i * step, step)
        copy = pltpu.make_async_remote_copy(
            src_ref=a_ref.at[1 - c, rows, :], dst_ref=got.at[i], send_sem=send_sem.at[i], recv_sem=recv_sem.at[i],
            device_id={"core": 1 - c}, device_id_type=MESH,
        )
        copy.start()
        copies.append(copy)
        load = pltpu.make_async_copy(a_ref.at[c, rows, :], own.at[i], own_sem.at[i])
        load.start()
        loads.append(load)
    for i in range(parts):
        loads[i].wait()
        copies[i].wait_recv()
        out[i] = own[i].astype(F32) + got[i].astype(F32)
        store = pltpu.make_async_copy(out.at[i], o_ref.at[pl.ds(i * step, step), :], out_sem.at[i])
        store.start()
        stores.append(store)
    for i in range(parts):
        stores[i].wait()
        copies[i].wait_send()


def core_scatter(a, *earlier):
    _, rows, width = a.shape
    n = CORE_PARTS
    return pl.pallas_call(
        pair_sum_kernel,
        out_shape=jax.ShapeDtypeStruct((rows, width), F32),
        in_specs=[ANY] * (1 + len(earlier)),
        out_specs=ANY,
        scratch_shapes=[pltpu.VMEM((n, rows // n, width), BF16)] * 2
        + [pltpu.VMEM((n, rows // n, width), F32)]
        + [pltpu.SemaphoreType.DMA((n,))] * 4,
        compiler_params=pltpu.CompilerParams(
            collective_id=fresh(), has_side_effects=True, vmem_limit_bytes=32 << 20
        ),
        cost_estimate=light(),
        name="core_scatter",
    )(a, *earlier)


def others():
    x, c, y, *_ = flips()
    out = []
    for dx, dc, dy in ((1, 0, 1), (1, 1, 1), (1, 0, 0), (0, 0, 1), (1, 1, 0), (0, 1, 1), (0, 1, 0)):
        px, pc, py = (1 - x if dx else x), (1 - c if dc else c), (1 - y if dy else y)
        out.append(((px * 2 + pc) * 2 + py, {"x": px, "core": pc, "y": py}))
    return (x * 2 + c) * 2 + y, out


def token_moves(split, ms):
    x, c, y, *_ = flips()
    z = lax.axis_index("z")
    if split == 2:
        slot, group = z // 2, z // 2
        to = [(z % 2, c, 2 * j + x) for j in range(ms)]
        of = [(z % 2, c, 2 * k + x) for k in range(ms)]
    else:
        slot, group = z // 4, z // 4
        to = [(z % 2, z // 2 % 2, (2 * j + x) * 2 + c) for j in range(ms)]
        of = [(z // 2 % 2, z % 2, 4 * k + 2 * c + x) for k in range(ms)]
    me = (x * 2 + c) * 64 + z
    places = [[{"x": px, "core": pc, "z": pz}, (px * 2 + pc) * 64 + pz != me] for px, pc, pz in to]
    sources = [[{"x": px, "core": pc, "z": pz}, (px * 2 + pc) * 64 + pz != me] for px, pc, pz in of]
    return slot, group, places, sources


def token_kernel(split, t_ref, *refs):
    o_ref, send_sem, recv_sem = refs[-3:]
    finish = start_tokens(split, t_ref, o_ref, send_sem, recv_sem, [])
    finish()


def start_tokens(split, t_ref, o_ref, send_sem, recv_sem, targets):
    ms = t_ref.shape[0]
    slot, group, places, sources = token_moves(split, ms)
    barrier = pltpu.get_barrier_semaphore()
    for target, remote in sources:
        @pl.when(remote)
        def _(target=target):
            pl.semaphore_signal(barrier, 1, device_id=target, device_id_type=MESH)
    for target in targets:
        pl.semaphore_signal(barrier, 1, device_id=target, device_id_type=MESH)
    count = len(targets)
    for _, remote in places:
        count = count + remote.astype(jnp.int32)
    pl.semaphore_wait(barrier, count)

    def local(j):
        return pltpu.make_async_copy(t_ref.at[j], o_ref.at[slot], recv_sem.at[slot])

    def away(j):
        return pltpu.make_async_remote_copy(
            src_ref=t_ref.at[j], dst_ref=o_ref.at[slot], send_sem=send_sem.at[j], recv_sem=recv_sem.at[slot],
            device_id=places[j][0], device_id_type=MESH,
        )

    for j in range(ms):
        pl.when(places[j][1])(lambda j=j: away(j).start())
        pl.when(jnp.logical_not(places[j][1]))(lambda j=j: local(j).start())

    def finish():
        for k in range(ms):
            pltpu.make_async_copy(t_ref.at[0], o_ref.at[k], recv_sem.at[k]).wait()
        for j in range(ms):
            pl.when(places[j][1])(lambda j=j: away(j).wait_send())

    return finish


def spread_kernel(with_gain, with_seg, w_ref, *refs):
    refs = list(refs)
    g_ref = refs.pop(0) if with_gain else None
    seg_ref, tok_ref = (refs.pop(0), refs.pop(0)) if with_seg else (None, None)
    scaled, own_sem, send_sem, recv_sem, tok_send, tok_recv = refs[-6:]
    o_ref, seg_out, tok_out = refs[-9:-6] if with_seg else (refs[-7], None, None)
    rows, width = w_ref.shape
    cols = width // 8
    me, peers = others()
    if with_seg:
        finish = start_tokens(with_seg, tok_ref, tok_out, tok_send, tok_recv, [target for _, target in peers])
    else:
        greet(*(target for _, target in peers))

    def place(p):
        return o_ref.at[pl.ds(pl.multiple_of(p * rows, rows), rows), :]

    copies = []

    def send(kind, src, dst, target):
        copy = pltpu.make_async_remote_copy(
            src_ref=src, dst_ref=dst, send_sem=send_sem.at[kind], recv_sem=recv_sem.at[kind],
            device_id=target, device_id_type=MESH,
        )
        copy.start()
        copies.append(copy)

    def columns(p):
        return pl.ds(pl.multiple_of(p * cols, cols), cols)

    def piece(p):
        if with_gain:
            scaled[p] = (w_ref[:, columns(p)].astype(F32) * g_ref[...]).astype(BF16)
            return scaled.at[p]
        return w_ref.at[:, columns(p)]

    for kind, (p, target) in enumerate(peers):
        send(kind, piece(p), place(me), target)
        if with_seg:
            send(7 + kind, seg_ref, seg_out.at[me], target)
    keeps = [pltpu.make_async_copy(piece(me), place(me), own_sem.at[0])]
    if with_seg:
        keeps.append(pltpu.make_async_copy(seg_ref, seg_out.at[me], own_sem.at[1]))
    for keep in keeps:
        keep.start()
    for keep in keeps:
        keep.wait()
    for copy in copies:
        copy.wait()
    if with_seg:
        finish()


def to_columns(w, gain, seg, *earlier, split=0, tokens=None):
    rows, width = w.shape
    cols = width // 8
    operands = [w] + ([gain] if gain is not None else []) + ([seg, tokens] if seg is not None else [])
    ms = tokens.shape[0] if seg is not None else 1
    out_shape = [jax.ShapeDtypeStruct((8 * rows, cols), BF16)]
    if seg is not None:
        out_shape.append(jax.ShapeDtypeStruct((8, *seg.shape), seg.dtype))
        out_shape.append(jax.ShapeDtypeStruct(tokens.shape, tokens.dtype))
    return pl.pallas_call(
        functools.partial(spread_kernel, gain is not None, split),
        out_shape=out_shape,
        in_specs=[WHOLE] * len(operands) + [ANY] * len(earlier),
        out_specs=[ANY] * len(out_shape),
        scratch_shapes=[
            pltpu.VMEM((8, rows, cols), BF16),
            pltpu.SemaphoreType.DMA((2,)),
            pltpu.SemaphoreType.DMA((14,)),
            pltpu.SemaphoreType.DMA((14,)),
            pltpu.SemaphoreType.DMA((ms,)),
            pltpu.SemaphoreType.DMA((ms,)),
        ],
        compiler_params=pltpu.CompilerParams(collective_id=fresh(), has_side_effects=True),
        cost_estimate=light(),
        name="weight_columns",
    )(*operands, *earlier)


def return_kernel(with_gain, p_ref, *refs):
    refs = list(refs)
    w_ref, g_ref = (refs.pop(0), refs.pop(0)) if with_gain else (None, None)
    got, own_sem, send_sem, recv_sem = refs[-4:]
    o_ref = refs[-6] if with_gain else refs[-5]
    _, rows, cols = got.shape
    me, peers = others()
    greet(*(target for _, target in peers))

    def block(p):
        return p_ref.at[pl.ds(pl.multiple_of(p * rows, rows), rows), :]

    copies = []
    for kind, (p, target) in enumerate(peers):
        copy = pltpu.make_async_remote_copy(
            src_ref=block(p), dst_ref=got.at[me], send_sem=send_sem.at[kind], recv_sem=recv_sem.at[kind],
            device_id=target, device_id_type=MESH,
        )
        copy.start()
        copies.append(copy)
    keep = pltpu.make_async_copy(block(me), got.at[me], own_sem)
    keep.start()
    total = jnp.zeros((rows, 1), F32)

    def finish(p, total):
        columns = pl.ds(pl.multiple_of(p * cols, cols), cols)
        grad = got[p].astype(F32)
        if with_gain:
            total = total + jnp.sum(w_ref[:, columns].astype(F32) * grad, -1, keepdims=True)
            grad = grad * g_ref[...]
        o_ref[:, columns] = grad
        return total

    keep.wait()
    total = finish(me, total)
    for kind in (6, 2, 3, 4, 5, 0, 1):
        copies[kind].wait_recv()
        total = finish(peers[kind][0], total)
    if with_gain:
        refs[-5][...] = total
    for copy in copies:
        copy.wait_send()


def to_rows(part, w, gain, *earlier):
    cols = part.shape[1]
    rows = part.shape[0] // 8
    operands = [part] + ([w, gain] if gain is not None else [])
    out_shape = [jax.ShapeDtypeStruct((rows, 8 * cols), F32)]
    if gain is not None:
        out_shape.append(jax.ShapeDtypeStruct((rows, 1), F32))
    return pl.pallas_call(
        functools.partial(return_kernel, gain is not None),
        out_shape=out_shape,
        in_specs=[ANY] + [WHOLE] * (len(operands) - 1) + [ANY] * len(earlier),
        out_specs=[WHOLE] * len(out_shape),
        scratch_shapes=[
            pltpu.VMEM((8, rows, cols), BF16),
            pltpu.SemaphoreType.DMA,
            pltpu.SemaphoreType.DMA((7,)),
            pltpu.SemaphoreType.DMA((7,)),
        ],
        compiler_params=pltpu.CompilerParams(
            collective_id=fresh(), has_side_effects=True, vmem_limit_bytes=24 << 20
        ),
        cost_estimate=light(),
        name="weight_rows",
    )(*operands, *earlier)


def tie_kernel(a_ref, *refs):
    pass


def tie(a, *earlier):
    return pl.pallas_call(
        tie_kernel,
        out_shape=jax.ShapeDtypeStruct(a.shape, a.dtype),
        in_specs=[ANY] * (1 + len(earlier)),
        out_specs=ANY,
        input_output_aliases={0: 0},
        cost_estimate=light(),
        name="tie",
    )(a, *earlier)


def along_z(part):
    return lax.all_gather(part, "z", axis=0, tiled=True)


def sum_along_z(g):
    return lax.psum_scatter(g, "z", scatter_dimension=0, tiled=True)


def shards(
    tokens,
    segments,
    attn_gain,
    query_weight,
    key_weight,
    value_weight,
    out_weight,
    ffn_gain,
    gate_weight,
    up_weight,
    down_weight,
    cotangent,
):
    NUMBERS[0] = 0
    micro, seq_local, pl_len, width = tokens.shape
    seq_len = segments.shape[2]
    ms = micro * seq_local
    rows_w = gate_weight.shape[0]
    nx, nc, nz, ny = (lax.axis_size(a) for a in EVERY)
    dp = nx * nc
    n_plane = 8 * ms * pl_len
    col_block = width // (dp * nz)
    z_index = lax.axis_index("z")
    core = lax.axis_index("core")
    split = dp * ms // nz

    def perm(a):
        lead = a.shape[:-1]
        return a.reshape(*lead, dp, nz, col_block).swapaxes(-3, -2).reshape(*lead, width)

    def unperm(a):
        lead = a.shape[:-1]
        return a.reshape(*lead, nz, dp, col_block).swapaxes(-3, -2).reshape(*lead, width)

    def by_head(a):
        return a.reshape(a.shape[0], 2, 2, 2, -1).swapaxes(2, 3).reshape(a.shape[0], 8, -1)

    def from_head(a):
        return a.reshape(a.shape[0], 2, 2, 2, -1).swapaxes(2, 3).reshape(a.shape[0], -1)

    heads_of = [(x * 2 + y) * 2 + c for x in range(2) for c in range(2) for y in range(2)]

    def place(x, c, z, y):
        return ((x * 2 + c) * nz + z) * 2 + y

    to_head, to_owner = [], []
    for x in range(2):
        for c in range(2):
            for y in range(2):
                head = (x * 2 + y) * 2 + c
                for k in range(nz):
                    to_head.append((head * nz + k, place(x, c, k, y)))
                    to_owner.append((place(x, c, k, y), head * nz + k))

    def slot_of(z):
        return z // 2 if split == 2 else z // 4

    def group_of(z):
        return z // 2 if split == 2 else z // 4

    rounds = []
    for k in range(ms):
        moves = []
        for ox in range(2):
            for oc in range(2):
                for oz in range(nz):
                    j = (k + slot_of(oz)) % ms
                    if split == 2:
                        to = (oz % 2, oc, 2 * j + ox)
                    else:
                        to = (oz % 2, oz // 2 % 2, (2 * j + ox) * 2 + oc)
                    moves += [(place(ox, oc, oz, oy), place(*to, oy)) for oy in range(2)]
        rounds.append(moves)

    def pick(a, index):
        return lax.dynamic_index_in_dim(a, index, 0, keepdims=False)

    def to_planes(a):
        got = jnp.stack([
            lax.ppermute(pick(a, (k + slot_of(z_index)) % ms), EVERY, rounds[k]) for k in range(ms)
        ])
        return jnp.stack([pick(got, (group_of(z_index) - slot + ms) % ms) for slot in range(ms)])

    def from_planes(a):
        got = jnp.stack([
            lax.ppermute(
                pick(a, (group_of(z_index) - k + ms) % ms), EVERY, [(to, of) for of, to in rounds[k]]
            )
            for k in range(ms)
        ])
        return jnp.stack([pick(got, (j - slot_of(z_index) + ms) % ms) for j in range(ms)])

    g1 = attn_gain.astype(F32)[:, None]
    g2 = ffn_gain.astype(F32)[:, None]

    wq_own = by_head(query_weight)
    wkv_own = jnp.stack(
        [key_weight.reshape(rows_w, KV_HEADS, HEAD_DIM), value_weight.reshape(rows_w, KV_HEADS, HEAD_DIM)], 2
    ).reshape(rows_w, 8 * HEAD_DIM)
    wkv_own = by_head(wkv_own)
    wqkv_own = jnp.concatenate([wq_own, wkv_own], 2).reshape(rows_w, -1)
    wqkv_part, seg_all, x = to_columns(
        wqkv_own, g1, segments.reshape(ms, seq_len), split=split, tokens=tokens.reshape(ms, pl_len, width)
    )
    (gate_part,) = to_columns(gate_weight, g2, None, wqkv_part)
    w_qkv = along_z(wqkv_part)
    w_out = along_z(lax.ppermute(perm(out_weight), EVERY, to_head))

    seg_all = seg_all.reshape(2, 2, 2, ms, seq_len)[:, :, 0]
    if split == 2:
        seg = pick(pick(seg_all, z_index % 2).swapaxes(0, 1), z_index // 2)
    else:
        seg = pick(pick(pick(seg_all, z_index // 2 % 2), z_index % 2), z_index // 4)[None]
    qseg, kseg = seg[:, :, None], seg[:, None, :]

    x = perm(x).astype(F32)
    r1 = lax.rsqrt(jnp.mean(x * x, -1, keepdims=True) + NORM_EPS)
    xhat = x * r1
    xa = plane_gather(xhat.astype(BF16), split, gate_part)
    (down_part,) = to_columns(down_weight, None, None, xa)

    inv_freq = 1.0 / ROPE_BASE ** (jnp.arange(0, HEAD_DIM, 2, dtype=F32) / HEAD_DIM)
    angles = jnp.arange(seq_len, dtype=jnp.int32).astype(F32)[:, None] * inv_freq[None, :]
    cos_q, sin_q = (jnp.tile(t, (split, 1)) for t in (jnp.cos(angles), jnp.sin(angles)))
    cos_k = jnp.where(core == 0, cos_q, 1.0)
    sin_k = jnp.where(core == 0, sin_q, 0.0)

    qkv = dot_nn(xa, w_qkv)
    qb = rotate(qkv[:, :HEAD_DIM], cos_q, sin_q).astype(BF16).reshape(split, seq_len, HEAD_DIM)
    kvb = rotate(qkv[:, HEAD_DIM:], cos_k, sin_k).astype(BF16)
    kv_all = core_gather(kvb, down_part).reshape(2, split, seq_len, HEAD_DIM)

    w_gate = along_z(gate_part)
    w_down = along_z(down_part)
    ob = attn_forward(qb, kv_all, qseg, kseg).reshape(n_plane, HEAD_DIM)
    cot = perm(to_planes(tie(cotangent.reshape(ms, pl_len, width), ob)))
    h = x + plane_scatter(dot_nn(ob, w_out).astype(BF16), split, ms)

    r2 = lax.rsqrt(jnp.mean(h * h, -1, keepdims=True) + NORM_EPS)
    hhat = h * r2
    ha = plane_gather(hhat.astype(BF16), split)
    (up_part,) = to_columns(up_weight, g2, None, ha)
    w_up = along_z(up_part)
    ca = plane_gather(cot, split, up_part)
    gate = dot_nn(ha, w_gate)
    sig = jax.nn.sigmoid(gate)
    silu = gate * sig
    d_mid = dot_nn(ca, w_down)
    dub = (d_mid * silu).astype(BF16)
    d_up = dot_tn(ha, dub).astype(BF16)
    w_up = tie(w_up, d_up)
    up = dot_nn(ha, w_up)
    dgb = (d_mid * up * sig * (1.0 + gate * (1.0 - sig))).astype(BF16)
    mid = (silu * up).astype(BF16)
    part_hhat = (dot_nt(dgb, w_gate) + dot_nt(dub, w_up)).astype(BF16)
    d_gate = dot_tn(ha, dgb).astype(BF16)
    up_z = sum_along_z(d_up)
    gate_z = sum_along_z(d_gate)
    d_hhat = plane_scatter(part_hhat, split, ms, d_gate)
    dh = cot.astype(F32) + r2 * (d_hhat - hhat * jnp.mean(d_hhat * hhat, -1, keepdims=True))
    da = plane_gather(dh.astype(BF16), split)
    dob = dot_nt(da, w_out).astype(BF16)

    dq, dkv_h = attn_backward(qb, kv_all, dob.reshape(qb.shape), qseg, kseg, up_z)
    dkv = core_scatter(dkv_h.reshape(2, n_plane, HEAD_DIM), gate_z)
    dqb = rotate(dq.reshape(n_plane, HEAD_DIM), cos_q, -sin_q).astype(BF16)
    dkvb = rotate(dkv, cos_k, -sin_k).astype(BF16)
    dqkv = jnp.concatenate([dqb, dkvb], 1)
    d_down = dot_tn(ca, mid).astype(BF16)
    d_qkv = dot_tn(xa, dqkv).astype(BF16)
    d_out = dot_tn(ob, da).astype(BF16)
    down_z = sum_along_z(d_down)
    out_z = sum_along_z(d_out)
    qkv_z = sum_along_z(d_qkv)
    part_xhat = dot_nt(dqkv, w_qkv).astype(BF16)
    d_xhat = plane_scatter(part_xhat, split, ms, d_down, d_qkv)
    input_grad = dh + r1 * (d_xhat - xhat * jnp.mean(d_xhat * xhat, -1, keepdims=True))
    input_grad = from_planes(unperm(input_grad).astype(BF16)).astype(F32).reshape(tokens.shape)

    up_back, up_gain = to_rows(up_z, up_weight, g2, d_xhat)
    part_out = dot_nt(mid, w_down).astype(BF16)
    result = h + plane_scatter(part_out, split, ms, up_back)
    output = from_planes(unperm(result.astype(BF16))).reshape(tokens.shape)
    gate_back, gate_gain = to_rows(gate_z, gate_weight, g2, result)

    (down_back,) = to_rows(down_z, None, None, gate_back)
    out_back = unperm(lax.ppermute(out_z, EVERY, to_owner).astype(F32))
    qkv_back, attn_gain_term = to_rows(qkv_z, wqkv_own, g1, down_back)
    qkv_back = qkv_back.reshape(rows_w, 8, -1)
    q_back = from_head(qkv_back[:, :, :HEAD_DIM])
    kv_back = from_head(qkv_back[:, :, HEAD_DIM:]).reshape(rows_w, KV_HEADS, 2, HEAD_DIM)
    k_back = kv_back[:, :, 0].reshape(rows_w, -1)
    v_back = kv_back[:, :, 1].reshape(rows_w, -1)

    return (
        output,
        input_grad,
        attn_gain_term.reshape(-1),
        q_back,
        k_back,
        v_back,
        out_back,
        (gate_gain + up_gain).reshape(-1),
        gate_back,
        up_back,
        down_back,
    )


def solution(mesh):
    dp, seq = mesh.shape["dp"], mesh.shape["seq"]
    fine = Mesh(mesh.devices.reshape(dp // 2, 2, seq // 2, 2), EVERY)
    dp_axes, seq_axes = ("x", "core"), ("z", "y")
    tok = P(None, dp_axes, seq_axes, None)
    vec, mat = P(EVERY), P(EVERY, None)
    return jax.shard_map(
        shards,
        mesh=fine,
        in_specs=(tok, P(None, dp_axes, None), vec, mat, mat, mat, mat, vec, mat, mat, mat, tok),
        out_specs=(tok, tok, vec, mat, mat, mat, mat, vec, mat, mat, mat),
        check_vma=False,
    )
```

time: 1520 us -> 902 us (0.59)
  waiting for transfers between devices: 1030 us -> 11.8 us
  Pallas kernels: 26.9 us -> 551 us
  blocking collectives: 80.9 us -> 0 us
  other arithmetic: 59 us -> 23.4 us
    pallas_call x2 -> x22, Pallas kernels: 26.9 us -> 551 us  [the longest x4 182 us: plane_scatter(): pl.pallas_call(functools.partial(scatter_kernel, split), out_shape=jax.Sh...]
    all_gather x11 -> x5, waiting for transfers between devices: 524 us -> 11.6 us  [along_z(): return lax.all_gather(part, 'z', axis=0, tiled=True)]
    reduce_scatter x11 -> x5, waiting for transfers between devices: 503 us -> 0.01 us  [sum_along_z(): return lax.psum_scatter(g, 'z', scatter_dimension=0, tiled=True)]
    all_to_all x4 -> x0, blocking collectives: 65.1 us -> none  [weight_columns(): part = lax.all_to_all(w, PLANE, split_axis=1, concat_axis=0, tiled=True)]
    all_to_all x4 -> x0, starting transfers between devices: 19.2 us -> none  [weight_rows_back(): return lax.all_to_all(part, PLANE, split_axis=0, concat_axis=1, tiled=True)]
    ppermute x2 -> x8, starting transfers between devices: 2.41 us -> 19.2 us  [the longest x4 10.9 us: from_planes(): lax.ppermute(pick(a, (group_of(z_index) - k + ms) % ms), EVERY, [(to, of)...]
    all_gather x1 -> x0, blocking collectives: 15.8 us -> none  [shards(): seg_all = lax.all_gather(segments, ('x', 'core'), axis=0, tiled=False)]
    unnamed x92 -> x138, local copies, waits for them, and re-layouts: 39 us -> 43.5 us
  transfers between devices with their start and end apart: 28 -> 18, of which waited for: 22 -> 1; matrix products, arithmetic and copies ran while one was open for 14% -> 27% of each run, Pallas kernels for 1% -> 57%
where the time goes in v2:
time: 902 us; the launch traced here: 889 us
  Pallas kernels  551 us (61%)
  matrix products  181 us (20%)
  local copies, waits for them, and re-layouts  86.6 us (10%)
  other arithmetic  23.4 us (3%)
  starting transfers between devices  20.2 us (2%)
  between operations  15.8 us (2%)
  waiting for transfers between devices  11.8 us (1%)
    pallas_call x4, Pallas kernels, plane_scatter(): pl.pallas_call(functools.partial(scatter_kernel, split), out_shape=jax.Sh...  182 us
    pallas_call x4, Pallas kernels, plane_gather(): pl.pallas_call(functools.partial(gather_kernel, split), out_shape=jax.Sha...  160 us
    pallas_call x4, Pallas kernels, to_columns(): pl.pallas_call(functools.partial(spread_kernel, gain is not None, split),...  102 us
    pallas_call x4, Pallas kernels, to_rows(): pl.pallas_call(functools.partial(return_kernel, gain is not None), out_sh...  86.9 us
    dot_general x5, matrix products, dot_nt(): lax.dot_general(a, b, (((1,), (1,)), ((), ())), preferred_element_type=F32)  62.6 us
    dot_general x5, matrix products, dot_nn(): lax.dot_general(a, b, (((1,), (0,)), ((), ())), preferred_element_type=F32)  61.6 us
    dot_general x5, matrix products, dot_tn(): lax.dot_general(a, b, (((0,), (0,)), ((), ())), preferred_element_type=F32)  56.4 us
    unnamed x138, local copies, waits for them, and re-layouts  43.5 us
  transfers between devices with their start and end apart: 18, of which 1 were waited for; matrix products, arithmetic and copies ran while one was open for 27% of the time, Pallas kernels for 57%

profile of v2, /device:TPU:29, one launch (start us, length us, event | category | flops | bytes accessed | tf_op | source)
XLA Modules:
  0.0 889.5 jit_solution(6360906051111373302)
XLA Ops:
  15.2 38.1 %weight_columns.4 = (bf16[512,512]{1,0:T(8,128)(2,1)}, s32[8,2,1024]{2,1,0:T(2,128)}, bf16[2,128,2048]{2,1,0:T(8,128)(2,1)}) custom-call(bf16[64,4096]{1,0:T(8,128)(2,1)} %bitcast.213, f32[64,1]{1,0:T(8,128)} %copy.61.refs_0_.refs_1_, s32[2,1024]{1,0:T(2,128)} %bitcast.254, bf16[2,128,2048]{2,1,0:T(8,128)(2,1)} %bitcast.245), custom_call_target="tpu_custom_call" | custom-call | bytes 1024 | tf_op jit(solution)/shard_map/weight_columns/pallas_call | solution.py:554
  56.0 30.8 %weight_columns.5.refs_0_ = bf16[512,1024]{1,0:T(8,128)(2,1)} custom-call(bf16[64,8192]{1,0:T(8,128)(2,1)} %refs_0_.3, f32[64,1]{1,0:T(8,128)} %copy.63.refs_0_.refs_1_, bf16[512,512]{1,0:T(8,128)(2,1)} %get-tuple-element.23.refs_1_), custom_call_target="tpu_custom_call" | custom-call | bytes 1024 | tf_op jit(solution)/shard_map/weight_columns/pallas_call | solution.py:554
  94.9 40.1 %plane_gather.4 = bf16[2,2,2,2,128,2048]{5,4,3,2,1,0:T(8,128)(2,1)} custom-call(bf16[2,128,2048]{2,1,0:T(8,128)(2,1)} %multiply_convert_fusion.4.a_ref, bf16[512,1024]{1,0:T(8,128)(2,1)} %weight_columns.5.refs_0_), custom_call_target="tpu_custom_call" | custom-call | bytes 1024 | tf_op jit(solution)/shard_map/plane_gather/pallas_call | solution.py:225
  135.0 16.4 %weight_columns.6.refs_0_ = bf16[512,1024]{1,0:T(8,128)(2,1)} custom-call(bf16[64,8192]{1,0:T(8,128)(2,1)} %w_ref.4, bf16[2048,2048]{1,0:T(8,128)(2,1)} %bitcast.220), custom_call_target="tpu_custom_call" | custom-call | bytes 1024 | tf_op jit(solution)/shard_map/weight_columns/pallas_call | solution.py:554
  155.3 7.7 fusion.40
  184.1 62.3 %plane_scatter.4 = f32[2,128,2048]{2,1,0:T(8,128)S(1)} custom-call(bf16[2,2,2,2,128,2048]{5,4,3,2,1,0:T(8,128)(2,1)S(1)} %bitcast.204), custom_call_target="tpu_custom_call" | custom-call | bytes 1024 | tf_op jit(solution)/shard_map/plane_scatter/pallas_call | solution.py:317
  249.2 40.1 %plane_gather.5 = bf16[2,2,2,2,128,2048]{5,4,3,2,1,0:T(8,128)(2,1)} custom-call(bf16[2,128,2048]{2,1,0:T(8,128)(2,1)} %multiply_convert_fusion.3.a_ref), custom_call_target="tpu_custom_call" | custom-call | bytes 1024 | tf_op jit(solution)/shard_map/plane_gather/pallas_call | solution.py:225
  289.3 16.6 %weight_columns.7.refs_0_ = bf16[512,1024]{1,0:T(8,128)(2,1)} custom-call(bf16[64,8192]{1,0:T(8,128)(2,1)} %refs_0_.2, f32[64,1]{1,0:T(8,128)} %copy.63.refs_0_.refs_1_, bf16[2048,2048]{1,0:T(8,128)(2,1)} %bitcast.223), custom_call_target="tpu_custom_call" | custom-call | bytes 1024 | tf_op jit(solution)/shard_map/weight_columns/pallas_call | solution.py:554
  311.4 40.1 %plane_gather.6 = bf16[2,2,2,2,128,2048]{5,4,3,2,1,0:T(8,128)(2,1)} custom-call(bf16[2,128,2048]{2,1,0:T(8,128)(2,1)} %reshape.304.a_ref, bf16[512,1024]{1,0:T(8,128)(2,1)} %weight_columns.7.refs_0_), custom_call_target="tpu_custom_call" | custom-call | bytes 1024 | tf_op jit(solution)/shard_map/plane_gather/pallas_call | solution.py:225
  351.5 14.5 %fusion.41 = f32[2048,1024]{1,0:T(8,128)} fusion(bf16[2048,2048]{1,0:T(8,128)(2,1)} %bitcast.224, bf16[2048,1024]{1,0:T(8,128)(2,1)} %all-gather.10.cloned.1.call-done), kind=kOutput, calls=%fused_computation.115 | convolution fusion | flops 8589934592 | bytes 20971520 | tf_op jit(solution)/shard_map/dot_general | solution.py:30
  365.9 16.2 %multiply_convert_fusion.2 = (bf16[2048,1024]{1,0:T(8,128)(2,1)S(1)}, f32[2048,1024]{1,0:T(8,128)}) fusion(f32[2048,1024]{1,0:T(8,128)} %fusion.41, bf16[2048,2048]{1,0:T(8,128)(2,1)} %bitcast.229, bf16[2048,1024]{1,0:T(8,128)(2,1)} %all-gather.14.cloned.1.call-done), kind=kOutput, calls=%fused_computation.3 | convolution fusion | flops 8602517504 | bytes 33554432 | tf_op jit(solution)/shard_map/dot_general | solution.py:30
  384.1 13.0 %convolution_convert_fusion.5.refs_0_ = bf16[2048,1024]{1,0:T(8,128)(2,1)} fusion(bf16[2048,2048]{1,0:T(8,128)(2,1)} %bitcast.225, bf16[2048,1024]{1,0:T(8,128)(2,1)S(1)} %get-tuple-element.79), kind=kOutput, calls=%fused_computation.11 | convolution fusion | flops 8592031744 | bytes 16777216 | tf_op jit(solution)/shard_map/dot_general | solution.py:38
  397.2 11.6 %all-gather.12.cloned.1.call-done.a_ref = bf16[2048,1024]{1,0:T(8,128)(2,1)} async-done(((bf16[512,1024]{1,0:T(8,128)(2,1)}), bf16[2048,1024]{1,0:T(8,128)(2,1)}) %all-gather.12.cloned.1.call-update) | async-done | bytes 4194320 | tf_op jit(solution)/shard_map/all_gather | solution.py:660
  408.8 19.7 %multiply_convert_fusion = (bf16[2048,1024]{1,0:T(8,128)(2,1)S(1)}, bf16[2048,1024]{1,0:T(8,128)(2,1)}) fusion(f32[2048,1024]{1,0:T(8,128)} %fusion.41, f32[2048,1024]{1,0:T(8,128)} %get-tuple-element.80, bf16[2048,2048]{1,0:T(8,128)(2,1)} %bitcast.226, bf16[2048,1024]{1,0:T(8,128)(2,1)} %tie.3), kind=kOutput, calls=%fused_computation.1 | convolution fusion | flops 8617197568 | bytes 37748736 | tf_op jit(solution)/shard_map/dot_general | solution.py:30
  430.5 12.9 %convolution_convert_fusion.4.refs_0_ = bf16[2048,1024]{1,0:T(8,128)(2,1)} fusion(bf16[2048,2048]{1,0:T(8,128)(2,1)} %bitcast.227, bf16[2048,1024]{1,0:T(8,128)(2,1)S(1)} %get-tuple-element.48), kind=kOutput, calls=%fused_computation.10 | convolution fusion | flops 8592031744 | bytes 16777216 | tf_op jit(solution)/shard_map/dot_general | solution.py:38
  443.4 15.6 %fusion.42 = f32[2048,2048]{1,0:T(8,128)} fusion(bf16[2048,1024]{1,0:T(8,128)(2,1)} %copy-done.61, bf16[2048,1024]{1,0:T(8,128)(2,1)} %all-gather.10.cloned.1.call-done), kind=kOutput, calls=%fused_computation.116 | convolution fusion | flops 8589934592 | bytes 25165824 | tf_op jit(solution)/shard_map/dot_general | solution.py:34
  459.0 16.0 %add_convert_fusion = bf16[2048,2048]{1,0:T(8,128)(2,1)} fusion(f32[2048,2048]{1,0:T(8,128)} %fusion.42, bf16[2048,1024]{1,0:T(8,128)(2,1)} %copy-done.60, bf16[2048,1024]{1,0:T(8,128)(2,1)S(1)} %copy-done.43), kind=kOutput, calls=%fused_computation | convolution fusion | flops 8598323200 | bytes 33554432 | tf_op jit(solution)/shard_map/dot_general | solution.py:34
  478.5 40.0 %plane_scatter.5 = f32[2,128,2048]{2,1,0:T(8,128)S(1)} custom-call(bf16[2,2,2,2,128,2048]{5,4,3,2,1,0:T(8,128)(2,1)S(1)} %bitcast.208, bf16[2048,1024]{1,0:T(8,128)(2,1)S(1)} %copy-done.4), custom_call_target="tpu_custom_call" | custom-call | bytes 1024 | tf_op jit(solution)/shard_map/plane_scatter/pallas_call | solution.py:317
  521.3 40.1 %plane_gather.7 = bf16[2,2,2,2,128,2048]{5,4,3,2,1,0:T(8,128)(2,1)} custom-call(bf16[2,128,2048]{2,1,0:T(8,128)(2,1)} %fusion.28.a_ref), custom_call_target="tpu_custom_call" | custom-call | bytes 1024 | tf_op jit(solution)/shard_map/plane_gather/pallas_call | solution.py:225
  561.5 6.8 convolution_convert_fusion.7
  568.3 14.0 %convolution_convert_fusion.3.refs_0_ = bf16[2048,1024]{1,0:T(8,128)(2,1)} fusion(bf16[2048,2048]{1,0:T(8,128)(2,1)} %bitcast.230, bf16[2048,1024]{1,0:T(8,128)(2,1)} %get-tuple-element.49), kind=kOutput, calls=%fused_computation.9 | convolution fusion | flops 8592031744 | bytes 16777216 | tf_op jit(solution)/shard_map/dot_general | solution.py:38
  582.4 7.1 convolution_convert_fusion.8
  593.2 9.9 %attention_backward.1 = (f32[2,1024,256]{2,1,0:T(8,128)}, bf16[2,2,1024,256]{3,2,1,0:T(8,128)(2,1)}) custom-call(bf16[2,1024,256]{2,1,0:T(8,128)(2,1)S(1)} %copy-done.10, bf16[2,2,1024,256]{3,2,1,0:T(8,128)(2,1)} %bitcast.202, bf16[2,2,1024,256]{3,2,1,0:T(8,128)(2,1)} %bitcast.203, bf16[2,1024,256]{2,1,0:T(8,128)(2,1)S(1)} %bitcast.216, ...), custom_call_target="tpu_custom_call" | custom-call | bytes 1024 | tf_op jit(solution)/shard_map/attention_backward/pallas_call | solution.py:120
  611.7 9.8 %convolution_convert_fusion.6.refs_1_ = bf16[2048,512]{1,0:T(8,128)(2,1)} fusion(bf16[2048,2048]{1,0:T(8,128)(2,1)} %bitcast.222, bf16[2048,128]{1,0:T(8,128)(2,1)S(1)} %get-tuple-element.69, bf16[2048,128]{1,0:T(8,128)(2,1)S(1)} %get-tuple-element.70, bf16[2048,128]{1,0:T(8,128)(2,1)S(1)} %get-tuple-element.55, bf16[2048,128]{1,0:T(8,128)(2,1)S(1)} %get-tuple-element.54), kind=kOutput, calls=%fused_computation.17 | convolution fusion | flops 4304404480 | bytes 12582912 | tf_op jit(solution)/shard_map/dot_general | solution.py:38
  621.5 14.1 %convolution_convert_fusion.1 = bf16[2048,2048]{1,0:T(8,128)(2,1)} fusion(bf16[2048,1024]{1,0:T(8,128)(2,1)} %get-tuple-element.49, bf16[2048,1024]{1,0:T(8,128)(2,1)} %all-gather.14.cloned.1.call-done), kind=kOutput, calls=%fused_computation.7 | convolution fusion | flops 8594128896 | bytes 16777216 | tf_op jit(solution)/shard_map/dot_general | solution.py:34
  638.0 9.8 %convolution_convert_fusion = bf16[2048,2048]{1,0:T(8,128)(2,1)} fusion(bf16[2048,512]{1,0:T(8,128)(2,1)} %all-gather.6.cloned.1.call-done, bf16[2048,128]{1,0:T(8,128)(2,1)} %copy-done.47, bf16[2048,128]{1,0:T(8,128)(2,1)} %copy-done.48, bf16[2048,128]{1,0:T(8,128)(2,1)S(1)} %get-tuple-element.55, bf16[2048,128]{1,0:T(8,128)(2,1)S(1)} %get-tuple-element.54), kind=kOutput, calls=%fused_computation.6 | convolution fusion | flops 4307550208 | bytes 12582912 | tf_op jit(solution)/shard_map/dot_general | solution.py:34
  651.4 40.6 %plane_scatter.6.refs_2_ = f32[2,128,2048]{2,1,0:T(8,128)S(1)} custom-call(bf16[2,2,2,2,128,2048]{5,4,3,2,1,0:T(8,128)(2,1)S(1)} %bitcast.212, bf16[2048,1024]{1,0:T(8,128)(2,1)S(1)} %copy-done.5, bf16[2048,512]{1,0:T(8,128)(2,1)S(1)} %copy-done.18), custom_call_target="tpu_custom_call" | custom-call | bytes 1024 | tf_op jit(solution)/shard_map/plane_scatter/pallas_call | solution.py:317
  692.1 15.7 %weight_rows.4 = (f32[64,8192]{1,0:T(8,128)S(1)}, f32[64,1]{1,0:T(8,128)S(1)}) custom-call(bf16[512,1024]{1,0:T(8,128)(2,1)S(1)} %copy-done.24, bf16[64,8192]{1,0:T(8,128)(2,1)S(1)} %copy-done.20, f32[64,1]{1,0:T(8,128)S(1)} %copy-done.29, f32[2,128,2048]{2,1,0:T(8,128)S(1)} %plane_scatter.6.refs_2_), custom_call_target="tpu_custom_call" | custom-call | bytes 1024 | tf_op jit(solution)/shard_map/weight_rows/pallas_call | solution.py:624
  707.8 38.8 %plane_scatter.7 = f32[2,128,2048]{2,1,0:T(8,128)S(1)} custom-call(bf16[2,2,2,2,128,2048]{5,4,3,2,1,0:T(8,128)(2,1)S(1)} %bitcast.211, f32[64,8192]{1,0:T(8,128)S(1)} %get-tuple-element.101.refs_0_), custom_call_target="tpu_custom_call" | custom-call | bytes 1024 | tf_op jit(solution)/shard_map/plane_scatter/pallas_call | solution.py:317
  783.0 47.0 %weight_rows.5 = (f32[64,8192]{1,0:T(8,128)S(1)}, f32[64,1]{1,0:T(8,128)S(1)}) custom-call(bf16[512,1024]{1,0:T(8,128)(2,1)S(1)} %copy-done.22, bf16[64,8192]{1,0:T(8,128)(2,1)S(1)} %copy-done.25, f32[64,1]{1,0:T(8,128)S(1)} %copy-done.29, f32[2,128,2048]{2,1,0:T(8,128)S(1)} %copy-done.12), custom_call_target="tpu_custom_call" | custom-call | bytes 1024 | tf_op jit(solution)/shard_map/weight_rows/pallas_call | solution.py:624
  834.1 15.0 %weight_rows.6.refs_2_ = f32[64,8192]{1,0:T(8,128)S(1)} custom-call(bf16[512,1024]{1,0:T(8,128)(2,1)S(1)} %copy-done.27, f32[64,8192]{1,0:T(8,128)S(1)} %copy-done.15), custom_call_target="tpu_custom_call" | custom-call | bytes 1024 | tf_op jit(solution)/shard_map/weight_rows/pallas_call | solution.py:624
  859.7 9.2 %weight_rows.7 = (f32[64,4096]{1,0:T(8,128)S(1)}, f32[64,1]{1,0:T(8,128)S(1)}) custom-call(bf16[512,512]{1,0:T(8,128)(2,1)S(1)} %copy-done.30, bf16[64,4096]{1,0:T(8,128)(2,1)S(1)} %bitcast.214, f32[64,1]{1,0:T(8,128)S(1)} %copy-done.31, f32[64,8192]{1,0:T(8,128)S(1)} %weight_rows.6.refs_2_), custom_call_target="tpu_custom_call" | custom-call | bytes 1024 | tf_op jit(solution)/shard_map/weight_rows/pallas_call | solution.py:624
  (265 shorter events, 144.2 us)
Async XLA Ops:
  7.2 148.1 %all-gather.6.cloned.1.call-start = ((), (), s32[]{:S(2)}) async-start(), calls=%async_computation.5 | async-start | bytes 2621440 | tf_op jit(solution)/shard_map/all_gather | solution.py:660
  9.6 43.8 %copy-start.50 = (bf16[64,2048]{1,0:T(8,128)(2,1)S(1)}, bf16[64,2048]{1,0:T(8,128)(2,1)}, u32[]{:S(2)}) copy-start(bf16[64,2048]{1,0:T(8,128)(2,1)} %param.18) | copy-start | bytes 786436
  12.2 43.1 %copy-start.59 = (bf16[64]{0:T(256)(128)(2,1)S(1)}, bf16[64]{0:T(256)(128)(2,1)}, u32[]{:S(2)}) copy-start(bf16[64]{0:T(256)(128)(2,1)} %param.19) | copy-start | bytes 388
  53.3 127.2 %all-gather.8.cloned.1.call-start = ((), (), s32[]{:S(2)}) async-start(), calls=%async_computation.6 | async-start | bytes 1310720 | tf_op jit(solution)/shard_map/all_gather | solution.py:660
  53.8 0.7 collective-permute-start
  55.3 296.2 %all-gather.10.cloned.1.call-start = ((), (), s32[]{:S(2)}) async-start(), calls=%async_computation.7 | async-start | bytes 5242880 | tf_op jit(solution)/shard_map/all_gather | solution.py:660
  86.8 279.1 %all-gather.14.cloned.1.call-start = ((), (), s32[]{:S(2)}) async-start(), calls=%async_computation.9 | async-start | bytes 5242880 | tf_op jit(solution)/shard_map/all_gather | solution.py:660
  92.6 153.8 %copy-start.34 = (f32[2,128,2048]{2,1,0:T(8,128)}, f32[2,128,2048]{2,1,0:T(8,128)S(1)}, u32[]{:S(2)}) copy-start(f32[2,128,2048]{2,1,0:T(8,128)S(1)} %reshape.326) | copy-start | bytes 6291460
  151.4 257.4 %all-gather.12.cloned.1.call-start = ((), (), s32[]{:S(2)}) async-start(), calls=%async_computation.8 | async-start | bytes 5242880 | tf_op jit(solution)/shard_map/all_gather | solution.py:660
  175.1 131.2 %collective-permute-start.1 = (bf16[128,2048]{1,0:T(8,128)(2,1)}, bf16[128,2048]{1,0:T(8,128)(2,1)}, u32[]{:S(2)}, u32[]{:S(2)}) collective-permute-start(bf16[128,2048]{1,0:T(8,128)(2,1)} %get-tuple-element.74), channel_id=1, source_target_pairs={{0,0},{1,1},{2,16},{3,17},{4,4},{5,5},{6,20},{7,21},{8,8},{9,9},{1... | collective-permute-start | bytes 1572872 | tf_op jit(solution)/shard_map/ppermute | solution.py:747
  177.1 129.3 %collective-permute-start.2 = (bf16[128,2048]{1,0:T(8,128)(2,1)}, bf16[128,2048]{1,0:T(8,128)(2,1)}, u32[]{:S(2)}, u32[]{:S(2)}) collective-permute-start(bf16[128,2048]{1,0:T(8,128)(2,1)} %get-tuple-element.73), channel_id=1, source_target_pairs={{0,4},{1,5},{2,20},{3,21},{4,0},{5,1},{6,16},{7,17},{8,12},{9,13},... | collective-permute-start | bytes 1572872 | tf_op jit(solution)/shard_map/ppermute | solution.py:747
  305.9 283.6 %reduce-scatter.6.cloned.1.call-start = ((), (), s32[]{:S(2)}) async-start(), calls=%async_computation.10 | async-start | bytes 5242880 | tf_op jit(solution)/shard_map/reduce_scatter | solution.py:664
  397.2 205.9 %reduce-scatter.8.cloned.1.call-start = ((), (), s32[]{:S(2)}) async-start(), calls=%async_computation.11 | async-start | bytes 5242880 | tf_op jit(solution)/shard_map/reduce_scatter | solution.py:664
  443.4 192.3 %reduce-scatter.14.cloned.1.call-start = ((), (), s32[]{:S(2)}) async-start(), calls=%async_computation.14 | async-start | bytes 1310720 | tf_op jit(solution)/shard_map/reduce_scatter | solution.py:664
  478.5 40.0 %copy-start.37 = (f32[2,128,2048]{2,1,0:T(8,128)S(1)}, f32[2,128,2048]{2,1,0:T(8,128)}, u32[]{:S(2)}) copy-start(f32[2,128,2048]{2,1,0:T(8,128)} %copy-done.36) | copy-start | bytes 6291460
  478.5 40.1 %copy-start.53 = (f32[2,128]{1,0:T(2,128)S(1)}, f32[2,128]{1,0:T(2,128)}, u32[]{:S(2)}) copy-start(f32[2,128]{1,0:T(2,128)} %copy-done.52) | copy-start | bytes 3076
  521.3 40.2 %copy-start.3 = (bf16[2,1024,256]{2,1,0:T(8,128)(2,1)S(1)}, bf16[2,1024,256]{2,1,0:T(8,128)(2,1)}, u32[]{:S(2)}) copy-start(bf16[2,1024,256]{2,1,0:T(8,128)(2,1)} %copy-done.1) | copy-start | bytes 3145732
  568.3 263.0 %reduce-scatter.12.cloned.1.call-start = ((), (), s32[]{:S(2)}) async-start(), calls=%async_computation.13 | async-start | bytes 5242880 | tf_op jit(solution)/shard_map/reduce_scatter | solution.py:664
  582.4 276.3 %reduce-scatter.10.cloned.1.call-start = ((), (), s32[]{:S(2)}) async-start(), calls=%async_computation.12 | async-start | bytes 2621440 | tf_op jit(solution)/shard_map/reduce_scatter | solution.py:664
  635.6 140.9 %collective-permute-start.7 = (bf16[64,2048]{1,0:T(8,128)(2,1)}, bf16[64,2048]{1,0:T(8,128)(2,1)S(1)}, u32[]{:S(2)}, u32[]{:S(2)}) collective-permute-start(bf16[64,2048]{1,0:T(8,128)(2,1)} %reduce-scatter.14.cloned.1.call-done), channel_id=1, source_target_pairs={{0,0},{2,1},{4,2},{6,3},{1,8},{3,9},{5,10},{7,11},{8,4},{10,5},{12... | collective-permute-start | bytes 786440 | tf_op jit(solution)/shard_map/ppermute | solution.py:854
  647.8 60.0 %slice-start = ((s8[8388608]{0:T(1024)(128)(4,1)}), s8[4194304]{0:T(1024)(128)(4,1)S(1)}, s32[]{:S(2)}) async-start(s8[8388608]{0:T(1024)(128)(4,1)} %bitcast.209), calls=%async_computation.15 | async-start | bytes 8388608
  651.4 40.7 %copy-start.20 = (bf16[64,8192]{1,0:T(8,128)(2,1)S(1)}, bf16[64,8192]{1,0:T(8,128)(2,1)}, u32[]{:S(2)}) copy-start(bf16[64,8192]{1,0:T(8,128)(2,1)} %refs_0_.2) | copy-start | bytes 3145732
  651.4 40.7 %copy-start.24 = (bf16[512,1024]{1,0:T(8,128)(2,1)S(1)}, bf16[512,1024]{1,0:T(8,128)(2,1)}, u32[]{:S(2)}) copy-start(bf16[512,1024]{1,0:T(8,128)(2,1)} %reduce-scatter.6.cloned.1.call-done.refs_0_.p_ref) | copy-start | bytes 3145732
  651.4 40.7 %copy-start.29 = (f32[64,1]{1,0:T(8,128)S(1)}, f32[64,1]{1,0:T(8,128)}, u32[]{:S(2)}) copy-start(f32[64,1]{1,0:T(8,128)} %copy.63.refs_0_.refs_1_) | copy-start | bytes 772
  651.4 56.4 %slice-start.1 = ((s8[8388608]{0:T(1024)(128)(4,1)}), s8[4194304]{0:T(1024)(128)(4,1)S(1)}, s32[]{:S(2)}) async-start(s8[8388608]{0:T(1024)(128)(4,1)} %bitcast.209), calls=%async_computation.16 | async-start | bytes 8388608
  707.8 38.9 %copy-start.16 = (f32[64,8192]{1,0:T(8,128)}, f32[64,8192]{1,0:T(8,128)S(1)}, u32[]{:S(2)}) copy-start(f32[64,8192]{1,0:T(8,128)S(1)} %get-tuple-element.101.refs_0_) | copy-start | bytes 6291460
  707.8 38.9 %copy-start.35 = (f32[2,128,2048]{2,1,0:T(8,128)S(1)}, f32[2,128,2048]{2,1,0:T(8,128)}, u32[]{:S(2)}) copy-start(f32[2,128,2048]{2,1,0:T(8,128)} %copy-done.34) | copy-start | bytes 6291460
  707.8 38.9 %copy-start.56 = (f32[2,128]{1,0:T(2,128)S(1)}, f32[2,128]{1,0:T(2,128)}, u32[]{:S(2)}) copy-start(f32[2,128]{1,0:T(2,128)} %copy-done.55) | copy-start | bytes 3076
  755.0 94.8 %collective-permute-start.5 = (bf16[128,2048]{0,1:T(8,128)(2,1)}, bf16[128,2048]{0,1:T(8,128)(2,1)}, u32[]{:S(2)}, u32[]{:S(2)}) collective-permute-start(bf16[128,2048]{0,1:T(8,128)(2,1)} %get-tuple-element.64), channel_id=1, source_target_pairs={{0,0},{1,1},{16,2},{17,3},{4,4},{5,5},{20,6},{21,7},{8,8},{9,9},{2... | collective-permute-start | bytes 1572872 | tf_op jit(solution)/shard_map/ppermute | solution.py:753
  759.5 90.3 %collective-permute-start.6 = (bf16[128,2048]{0,1:T(8,128)(2,1)}, bf16[128,2048]{0,1:T(8,128)(2,1)}, u32[]{:S(2)}, u32[]{:S(2)}) collective-permute-start(bf16[128,2048]{0,1:T(8,128)(2,1)} %get-tuple-element.63), channel_id=1, source_target_pairs={{4,0},{5,1},{20,2},{21,3},{0,4},{1,5},{16,6},{17,7},{12,8},{13,9},... | collective-permute-start | bytes 1572872 | tf_op jit(solution)/shard_map/ppermute | solution.py:753
  771.3 83.1 %collective-permute-start.3 = (bf16[128,2048]{1,0:T(8,128)(2,1)}, bf16[128,2048]{1,0:T(8,128)(2,1)}, u32[]{:S(2)}, u32[]{:S(2)}) collective-permute-start(bf16[128,2048]{1,0:T(8,128)(2,1)} %bitcast.250), channel_id=1, source_target_pairs={{0,0},{1,1},{16,2},{17,3},{4,4},{5,5},{20,6},{21,7},{8,8},{9,9},{2... | collective-permute-start | bytes 1572872 | tf_op jit(solution)/shard_map/ppermute | solution.py:753
  775.6 78.9 %collective-permute-start.4 = (bf16[128,2048]{1,0:T(8,128)(2,1)}, bf16[128,2048]{1,0:T(8,128)(2,1)}, u32[]{:S(2)}, u32[]{:S(2)}) collective-permute-start(bf16[128,2048]{1,0:T(8,128)(2,1)} %bitcast.251), channel_id=1, source_target_pairs={{4,0},{5,1},{20,2},{21,3},{0,4},{1,5},{16,6},{17,7},{12,8},{13,9},... | collective-permute-start | bytes 1572872 | tf_op jit(solution)/shard_map/ppermute | solution.py:753
  (50 other events, 296.3 us)
Sparse Core Ops, SparseCore 0:
  53.4 50.8 all-gather.5
  106.4 26.8 all-gather.7
  134.9 101.4 all-gather.9
  237.9 90.1 all-gather.13
  329.5 79.2 all-gather.11
  411.0 77.0 reduce-scatter.5
  490.5 77.2 reduce-scatter.7
  570.1 25.4 reduce-scatter.13
  598.0 80.3 reduce-scatter.11
  681.2 44.5 reduce-scatter.9

commit v3 on v2

--- a/solution.py
+++ b/solution.py
@@ -1,4 +1,5 @@
 import functools
+import itertools
 
 import jax
 import jax.numpy as jnp
@@ -42,6 +43,18 @@
     half = values.shape[-1] // 2
     a, b = values[:, :half], values[:, half:]
     return jnp.concatenate([a * cosine - b * sine, b * cosine + a * sine], -1)
+
+
+def reorder(values, outer, inner):
+    block = values.shape[-1] // (outer * inner)
+    return jnp.concatenate(
+        [
+            values[..., (o * inner + i) * block : (o * inner + i + 1) * block]
+            for i in range(inner)
+            for o in range(outer)
+        ],
+        -1,
+    )
 
 
 QUERY_ROWS = 256
@@ -154,20 +167,128 @@
 
 
 def pieces_at(ref, split, px, pc, py):
-    return ref.at[pc, :, px, py] if split == 2 else ref.at[:, pc, px, py]
+    return ref.at[px, :, pc, py] if split == 2 else ref.at[:, pc, px, py]
 
 
 def plane_shape(split, slots, *rest):
     return (2, slots, 2, 2, *rest) if split == 2 else (slots, 2, 2, 2, *rest)
 
 
-def gather_kernel(split, a_ref, *refs):
-    o_ref, own_sem, send_sem, recv_sem = refs[-4:]
+ANY = pl.BlockSpec(memory_space=pl.ANY)
+WHOLE = pl.BlockSpec(memory_space=pltpu.VMEM)
+
+
+def light(bytes_accessed=1024):
+    return pl.CostEstimate(flops=0, bytes_accessed=bytes_accessed, transcendentals=0)
+
+
+FORMS = {"nn": dot_nn, "nt": dot_nt, "tn": dot_tn}
+
+
+class Matmul:
+    def __init__(self, form, a, b, dtype=BF16):
+        self.form, self.operands = form, [a, b]
+        rows = a.shape[1] if form == "tn" else a.shape[0]
+        cols = b.shape[0] if form == "nt" else b.shape[1]
+        self.out = jax.ShapeDtypeStruct((rows, cols), dtype)
+        self.parts = max(1, rows // 256)
+        self.scratch = [
+            pltpu.VMEM(a.shape, a.dtype),
+            pltpu.VMEM(b.shape, b.dtype),
+            pltpu.VMEM(self.out.shape, dtype),
+            pltpu.SemaphoreType.DMA((2,)),
+            pltpu.SemaphoreType.DMA((self.parts,)),
+        ]
+
+    def steps(self, a_ref, b_ref, o_ref, a, b, out, load_sem, store_sem):
+        loads = [
+            pltpu.make_async_copy(a_ref, a, load_sem.at[0]),
+            pltpu.make_async_copy(b_ref, b, load_sem.at[1]),
+        ]
+        for load in loads:
+            load.start()
+        yield
+        for load in loads:
+            load.wait()
+        step = out.shape[0] // self.parts
+        stores = []
+        for i in range(self.parts):
+            rows = pl.ds(i * step, step)
+            left = a[:, rows] if self.form == "tn" else a[rows, :]
+            out[rows, :] = FORMS[self.form](left, b[...]).astype(out.dtype)
+            store = pltpu.make_async_copy(out.at[rows, :], o_ref.at[rows, :], store_sem.at[i])
+            store.start()
+            stores.append(store)
+            yield
+        for store in stores:
+            store.wait()
+
+
+def interleave(main, side):
+    for matmul in side:
+        next(matmul)
+    rest = itertools.chain(*side)
+    for _ in main:
+        next(rest, None)
+    for _ in rest:
+        pass
+
+
+def communicate(name, steps, operands, earlier, out, scratch, matmuls, vmem, specs=None, moves=None):
+    n_in = len(operands)
+    n_scratch = len(scratch)
+    split, back, tokens = moves or (0, False, None)
+    moved = [] if moves is None else [tokens]
+    side_in = [a for m in matmuls for a in m.operands]
+
+    def kernel(*refs):
+        refs = list(refs)
+        ins, refs = refs[:n_in], refs[n_in:]
+        before, refs = refs[: len(moved)], refs[len(moved) :]
+        side_ins, refs = refs[: len(side_in)], refs[len(side_in) + len(earlier) :]
+        outs, refs = refs[: 1 + len(matmuls)], refs[1 + len(matmuls) :]
+        behind, refs = refs[: len(moved)], refs[len(moved) :]
+        own, refs = refs[:n_scratch], refs[n_scratch:]
+        finish = []
+
+        def meet(*targets):
+            if moved:
+                finish.append(start_tokens(split, back, before[0], behind[0], refs[-2], refs[-1], targets))
+            else:
+                greet(*targets)
+
+        side = []
+        for i, m in enumerate(matmuls):
+            side.append(m.steps(*side_ins[2 * i : 2 * i + 2], outs[1 + i], *refs[5 * i : 5 * i + 5]))
+        interleave(steps(meet, *ins, outs[0], *own), side)
+        for wait in finish:
+            wait()
+
+    shape, spec = out
+    result = pl.pallas_call(
+        kernel,
+        out_shape=[shape] + [m.out for m in matmuls] + [jax.ShapeDtypeStruct(t.shape, t.dtype) for t in moved],
+        in_specs=(specs or [ANY] * n_in) + [ANY] * (len(moved) + len(side_in) + len(earlier)),
+        out_specs=[spec] + [ANY] * (len(matmuls) + len(moved)),
+        scratch_shapes=scratch
+        + [t for m in matmuls for t in m.scratch]
+        + [pltpu.SemaphoreType.DMA((t.shape[0],)) for t in moved for _ in range(2)],
+        compiler_params=pltpu.CompilerParams(
+            collective_id=fresh(), has_side_effects=True, vmem_limit_bytes=vmem << 20
+        ),
+        cost_estimate=light(),
+        name=name,
+    )(*operands, *moved, *side_in, *earlier)
+    return result
+
+
+def gather_steps(split, prepare, meet, *refs):
+    sources, (o_ref, a_ref, own_sem, send_sem, recv_sem) = refs[:-5], refs[-5:]
     x, c, y, to_x, to_y, to_c = flips()
     slots, piece, _ = a_ref.shape
     per_slot = GATHER_PARTS // slots
     step = piece // per_slot
-    greet(to_x, to_y, to_c)
+    meet(to_x, to_y, to_c)
 
     def rows_of(i):
         return i // per_slot, pl.ds(i % per_slot * step, step)
@@ -183,13 +304,15 @@
         copy.start()
         return copy
 
-    own_copy = pltpu.make_async_copy(a_ref, pieces_at(o_ref, split, x, c, y), own_sem)
-    own_copy.start()
     copies = {}
     for i in range(GATHER_PARTS):
+        a_ref[rows_of(i)] = prepare(*(source[rows_of(i)] for source in sources)).astype(BF16)
         own = a_ref.at[rows_of(i)]
         for kind, target in enumerate((to_x, to_y, to_c)):
             copies[kind, i] = send(kind, i, own, part(x, c, y, i), target)
+    own_copy = pltpu.make_async_copy(a_ref, pieces_at(o_ref, split, x, c, y), own_sem)
+    own_copy.start()
+    yield
     src_x, src_y = jnp.where(c == 0, x, 1 - x), jnp.where(c == 0, 1 - y, y)
     dst_x, dst_y = jnp.where(c == 0, 1 - x, x), jnp.where(c == 0, y, 1 - y)
     for i in range(GATHER_PARTS):
@@ -199,10 +322,13 @@
             copies[3 + kind, i] = send(3 + kind, i, block, block, to_c)
         block = part(src_x, c, src_y, i)
         copies[5, i] = send(5, i, block, block, {"x": dst_x, "y": dst_y})
+        yield
+        yield
     for i in range(GATHER_PARTS):
         copies[5, i].wait_recv()
         block = part(1 - x, c, 1 - y, i)
         copies[6, i] = send(6, i, block, block, to_c)
+        yield
     for i in range(GATHER_PARTS):
         for kind in (2, 3, 4, 6):
             copies[kind, i].wait_recv()
@@ -212,76 +338,90 @@
             copies[kind, i].wait_send()
 
 
-ANY = pl.BlockSpec(memory_space=pl.ANY)
-WHOLE = pl.BlockSpec(memory_space=pltpu.VMEM)
-
-
-def light(bytes_accessed=1024):
-    return pl.CostEstimate(flops=0, bytes_accessed=bytes_accessed, transcendentals=0)
-
-
-def plane_gather(a, split, *earlier):
-    slots, piece, width = a.shape
-    out = pl.pallas_call(
-        functools.partial(gather_kernel, split),
-        out_shape=jax.ShapeDtypeStruct(plane_shape(split, slots, piece, width), a.dtype),
-        in_specs=[WHOLE] + [ANY] * len(earlier),
-        out_specs=ANY,
-        scratch_shapes=[
-            pltpu.SemaphoreType.DMA,
-            pltpu.SemaphoreType.DMA((7, GATHER_PARTS)),
-            pltpu.SemaphoreType.DMA((7, GATHER_PARTS)),
-        ],
-        compiler_params=pltpu.CompilerParams(collective_id=fresh(), has_side_effects=True),
-        cost_estimate=light(),
-        name="plane_gather",
-    )(a, *earlier)
-    return out.reshape(-1, width)
-
-
-def scatter_kernel(split, p_ref, *refs):
-    o_ref, own, got_c, put_x, put_y, got_x, got_y, fin_x, fin_y, end_x, end_y, own_sem, send_sem, recv_sem = refs[-14:]
+def plane_gather(sources, prepare, split, *earlier, matmuls=()):
+    slots, piece, width = sources[0].shape
+    out = jax.ShapeDtypeStruct(plane_shape(split, slots, piece, width), BF16)
+    scratch = [
+        pltpu.VMEM((slots, piece, width), BF16),
+        pltpu.SemaphoreType.DMA,
+        pltpu.SemaphoreType.DMA((7, GATHER_PARTS)),
+        pltpu.SemaphoreType.DMA((7, GATHER_PARTS)),
+    ]
+    result = communicate(
+        "plane_gather", functools.partial(gather_steps, split, prepare), list(sources), earlier, (out, ANY), scratch,
+        matmuls, 40 if matmuls else 16, [WHOLE] * len(sources),
+    )
+    got = result[0].reshape(-1, width)
+    return (got, *result[1:]) if matmuls else got
+
+
+def scatter_steps(split, forms, finish, n_sources, meet, *refs):
+    n = len(forms)
+    hbm, refs = refs[: 2 * n], refs[2 * n :]
+    sources, refs = refs[:n_sources], refs[n_sources:]
+    o_ref, refs = refs[0], refs[1:]
+    held, refs = refs[: 2 * n], refs[2 * n :]
+    own, put_c, got_c, put_x, put_y, got_x, got_y, fin_x, fin_y, end_x, end_y, load_sem, send_sem, recv_sem = refs
     x, c, y, to_x, to_y, to_c = flips()
     parts, _, _, step, width = own.shape
-    slots, piece, _ = o_ref.shape
+    slots = o_ref.shape[0]
     per_slot = parts // slots
     half = width // 2
     left, right = pl.ds(0, half), pl.ds(half, half)
-    greet(to_x, to_y, to_c)
+    loads = [pltpu.make_async_copy(of, to, load_sem.at[i]) for i, (of, to) in enumerate(zip(hbm, held))]
+    for load in loads:
+        load.start()
+    meet(to_x, to_y, to_c)
+    for load in loads:
+        load.wait()
+
+    def rows_of(i):
+        return i // per_slot, pl.ds(i % per_slot * step, step)
+
+    def partial_sums(pc, i, columns):
+        slot, rows = rows_of(i)
+        total = None
+        for form, a, b in zip(forms, held[::2], held[1::2]):
+            if split == 2:
+                block = a[:, slot, pc, :, rows, :]
+            else:
+                block = a[slot, pc, :, :, rows, :]
+            block = block.reshape(4 * step, block.shape[-1])
+            term = dot_nn(block, b[:, columns]) if form == "nn" else dot_nt(block, b[columns, :])
+            total = term if total is None else total + term
+        return total.astype(BF16).reshape(2, 2, step, half)
 
     def send(kind, i, src, dst, target):
         copy = pltpu.make_async_remote_copy(
-            src_ref=src.at[i] if kind else src, dst_ref=dst.at[i],
-            send_sem=send_sem.at[kind, i], recv_sem=recv_sem.at[kind, i],
+            src_ref=src.at[i], dst_ref=dst.at[i], send_sem=send_sem.at[kind, i], recv_sem=recv_sem.at[kind, i],
             device_id=target, device_id_type=MESH,
         )
         copy.start()
         return copy
 
-    loads, first, second, third = [], [], [], []
-    def rows_of(i):
-        return i // per_slot, pl.ds(i % per_slot * step, step)
-
-    def blocks(pc, i):
-        slot, rows = rows_of(i)
-        return p_ref.at[pc, slot, :, :, rows, :] if split == 2 else p_ref.at[slot, pc, :, :, rows, :]
-
-    for i in range(parts):
-        first.append(send(0, i, blocks(1 - c, i), got_c, to_c))
-        load = pltpu.make_async_copy(blocks(c, i), own.at[i], own_sem.at[i])
-        load.start()
-        loads.append(load)
-
     def f32(ref, *index):
         return ref[index].astype(F32)
 
-    for i in range(parts):
-        loads[i].wait()
+    first, second, third = [], [], []
+
+    def along_first_axis(i):
         first[i].wait_recv()
         for j in range(2):
             put_x[i, j] = (f32(own, i, 1 - x, j, slice(None), left) + f32(got_c, i, 1 - x, j, slice(None), left)).astype(BF16)
             put_y[i, j] = (f32(own, i, j, 1 - y, slice(None), right) + f32(got_c, i, j, 1 - y, slice(None), right)).astype(BF16)
         second.append((send(1, i, put_x, got_x, to_x), send(2, i, put_y, got_y, to_y)))
+
+    for i in range(parts):
+        for columns in (left, right):
+            put_c[i, :, :, :, columns] = partial_sums(1 - c, i, columns)
+        first.append(send(0, i, put_c, got_c, to_c))
+        for columns in (left, right):
+            own[i, :, :, :, columns] = partial_sums(c, i, columns)
+        if i:
+            along_first_axis(i - 1)
+    along_first_axis(parts - 1)
+    yield
+    yield
     for i in range(parts):
         for copy in second[i]:
             copy.wait_recv()
@@ -292,54 +432,57 @@
             f32(own, i, 1 - x, y, slice(None), right) + f32(got_c, i, 1 - x, y, slice(None), right) + f32(got_y, i, 1 - x)
         ).astype(BF16)
         third.append((send(3, i, fin_y, end_y, to_y), send(4, i, fin_x, end_x, to_x)))
+        yield
+        yield
     for i in range(parts):
         for copy in third[i]:
             copy.wait_recv()
         slot, rows = rows_of(i)
-        o_ref[slot, rows, left] = (
-            f32(own, i, x, y, slice(None), left) + f32(got_c, i, x, y, slice(None), left)
-            + f32(got_x, i, y) + f32(end_y, i)
+        total = jnp.concatenate(
+            [
+                f32(own, i, x, y, slice(None), left) + f32(got_c, i, x, y, slice(None), left)
+                + f32(got_x, i, y) + f32(end_y, i),
+                f32(own, i, x, y, slice(None), right) + f32(got_c, i, x, y, slice(None), right)
+                + f32(got_y, i, x) + f32(end_x, i),
+            ],
+            -1,
         )
-        o_ref[slot, rows, right] = (
-            f32(own, i, x, y, slice(None), right) + f32(got_c, i, x, y, slice(None), right)
-            + f32(got_y, i, x) + f32(end_x, i)
-        )
+        o_ref[slot, rows, :] = finish(total, *(source[slot, rows, :] for source in sources)).astype(o_ref.dtype)
+        yield
     for i in range(parts):
         for copy in (first[i], *second[i], *third[i]):
             copy.wait_send()
 
 
-def plane_scatter(a, split, slots, *earlier):
-    rows, width = a.shape[0] // 8, a.shape[1]
+def plane_scatter(products, sources, finish, dtype, split, slots, *earlier, matmuls=(), moves=None):
+    forms = [form for form, _, _ in products]
+    _, a, b = products[0]
+    rows, width = a.shape[0] // 8, (b.shape[1] if forms[0] == "nn" else b.shape[0])
     piece = rows // slots
     n = SCATTER_PARTS
     step, half = rows // n, width // 2
-    return pl.pallas_call(
-        functools.partial(scatter_kernel, split),
-        out_shape=jax.ShapeDtypeStruct((slots, piece, width), F32),
-        in_specs=[ANY] * (1 + len(earlier)),
-        out_specs=WHOLE,
-        scratch_shapes=[
-            pltpu.VMEM((n, 2, 2, step, width), BF16),
-            pltpu.VMEM((n, 2, 2, step, width), BF16),
-            pltpu.VMEM((n, 2, step, half), BF16),
-            pltpu.VMEM((n, 2, step, half), BF16),
-            pltpu.VMEM((n, 2, step, half), BF16),
-            pltpu.VMEM((n, 2, step, half), BF16),
-            pltpu.VMEM((n, step, half), BF16),
-            pltpu.VMEM((n, step, half), BF16),
-            pltpu.VMEM((n, step, half), BF16),
-            pltpu.VMEM((n, step, half), BF16),
-            pltpu.SemaphoreType.DMA((n,)),
-            pltpu.SemaphoreType.DMA((5, n)),
-            pltpu.SemaphoreType.DMA((5, n)),
-        ],
-        compiler_params=pltpu.CompilerParams(
-            collective_id=fresh(), has_side_effects=True, vmem_limit_bytes=32 << 20
-        ),
-        cost_estimate=light(),
-        name="plane_scatter",
-    )(a.reshape(plane_shape(split, slots, piece, width)), *earlier)
+    operands = []
+    for _, a, b in products:
+        operands += [a.reshape(plane_shape(split, slots, piece, a.shape[1])), b]
+    whole, two, one = (
+        pltpu.VMEM((n, 2, 2, step, width), BF16),
+        pltpu.VMEM((n, 2, step, half), BF16),
+        pltpu.VMEM((n, step, half), BF16),
+    )
+    scratch = [pltpu.VMEM(t.shape, t.dtype) for t in operands]
+    scratch += [whole] * 3 + [two] * 4 + [one] * 4
+    scratch += [
+        pltpu.SemaphoreType.DMA((len(operands),)),
+        pltpu.SemaphoreType.DMA((5, n)),
+        pltpu.SemaphoreType.DMA((5, n)),
+    ]
+    out = jax.ShapeDtypeStruct((slots, piece, width), dtype)
+    result = communicate(
+        "plane_scatter", functools.partial(scatter_steps, split, forms, finish, len(sources)),
+        operands + list(sources), earlier, (out, WHOLE), scratch, matmuls, 62,
+        [ANY] * len(operands) + [WHOLE] * len(sources), moves,
+    )
+    return result if matmuls or moves else result[0]
 
 
 def pair_kernel(a_ref, *refs):
@@ -434,8 +577,8 @@
     z = lax.axis_index("z")
     if split == 2:
         slot, group = z // 2, z // 2
-        to = [(z % 2, c, 2 * j + x) for j in range(ms)]
-        of = [(z % 2, c, 2 * k + x) for k in range(ms)]
+        to = [(x, z % 2, 2 * j + c) for j in range(ms)]
+        of = [(x, z % 2, 2 * k + c) for k in range(ms)]
     else:
         slot, group = z // 4, z // 4
         to = [(z % 2, z // 2 % 2, (2 * j + x) * 2 + c) for j in range(ms)]
@@ -446,15 +589,11 @@
     return slot, group, places, sources
 
 
-def token_kernel(split, t_ref, *refs):
-    o_ref, send_sem, recv_sem = refs[-3:]
-    finish = start_tokens(split, t_ref, o_ref, send_sem, recv_sem, [])
-    finish()
-
-
-def start_tokens(split, t_ref, o_ref, send_sem, recv_sem, targets):
+def start_tokens(split, back, t_ref, o_ref, send_sem, recv_sem, targets):
     ms = t_ref.shape[0]
     slot, group, places, sources = token_moves(split, ms)
+    if back:
+        slot, places, sources = group, sources, places
     barrier = pltpu.get_barrier_semaphore()
     for target, remote in sources:
         @pl.when(remote)
@@ -489,17 +628,22 @@
     return finish
 
 
-def spread_kernel(with_gain, with_seg, w_ref, *refs):
+def head_columns(px, pc, py):
+    return tuple(pl.ds(pl.multiple_of(h * HEAD_DIM, HEAD_DIM), HEAD_DIM) for h in (4 * px + 2 * py + pc, 2 * px + py))
+
+
+def spread_kernel(heads, with_gain, split, *refs):
     refs = list(refs)
+    w_refs = [refs.pop(0) for _ in range(3 if heads else 1)]
     g_ref = refs.pop(0) if with_gain else None
-    seg_ref, tok_ref = (refs.pop(0), refs.pop(0)) if with_seg else (None, None)
+    seg_ref, tok_ref = (refs.pop(0), refs.pop(0)) if split else (None, None)
     scaled, own_sem, send_sem, recv_sem, tok_send, tok_recv = refs[-6:]
-    o_ref, seg_out, tok_out = refs[-9:-6] if with_seg else (refs[-7], None, None)
-    rows, width = w_ref.shape
-    cols = width // 8
+    o_ref, seg_out, tok_out = refs[-9:-6] if split else (refs[-7], None, None)
+    _, rows, cols = scaled.shape
     me, peers = others()
-    if with_seg:
-        finish = start_tokens(with_seg, tok_ref, tok_out, tok_send, tok_recv, [target for _, target in peers])
+    x, c, y, *_ = flips()
+    if split:
+        finish = start_tokens(split, False, tok_ref, tok_out, tok_send, tok_recv, [target for _, target in peers])
     else:
         greet(*(target for _, target in peers))
 
@@ -519,18 +663,24 @@
     def columns(p):
         return pl.ds(pl.multiple_of(p * cols, cols), cols)
 
-    def piece(p):
+    def piece(p, px, pc, py):
+        if heads:
+            q_cols, kv_cols = head_columns(px, pc, py)
+            key, value = (w[:, kv_cols].astype(F32) for w in w_refs[1:])
+            scaled[p, :, :HEAD_DIM] = (w_refs[0][:, q_cols].astype(F32) * g_ref[...]).astype(BF16)
+            scaled[p, :, HEAD_DIM:] = (jnp.where(pc == 0, key, value) * g_ref[...]).astype(BF16)
+            return scaled.at[p]
         if with_gain:
-            scaled[p] = (w_ref[:, columns(p)].astype(F32) * g_ref[...]).astype(BF16)
+            scaled[p] = (w_refs[0][:, columns(p)].astype(F32) * g_ref[...]).astype(BF16)
             return scaled.at[p]
-        return w_ref.at[:, columns(p)]
+        return w_refs[0].at[:, columns(p)]
 
     for kind, (p, target) in enumerate(peers):
-        send(kind, piece(p), place(me), target)
-        if with_seg:
+        send(kind, piece(p, target["x"], target["core"], target["y"]), place(me), target)
+        if split:
             send(7 + kind, seg_ref, seg_out.at[me], target)
-    keeps = [pltpu.make_async_copy(piece(me), place(me), own_sem.at[0])]
-    if with_seg:
+    keeps = [pltpu.make_async_copy(piece(me, x, c, y), place(me), own_sem.at[0])]
+    if split:
         keeps.append(pltpu.make_async_copy(seg_ref, seg_out.at[me], own_sem.at[1]))
     for keep in keeps:
         keep.start()
@@ -538,21 +688,22 @@
         keep.wait()
     for copy in copies:
         copy.wait()
-    if with_seg:
+    if split:
         finish()
 
 
-def to_columns(w, gain, seg, *earlier, split=0, tokens=None):
-    rows, width = w.shape
-    cols = width // 8
-    operands = [w] + ([gain] if gain is not None else []) + ([seg, tokens] if seg is not None else [])
-    ms = tokens.shape[0] if seg is not None else 1
+def to_columns(weights, gain, seg, *earlier, split=0, tokens=None):
+    rows = weights[0].shape[0]
+    heads = len(weights) == 3
+    cols = 2 * HEAD_DIM if heads else weights[0].shape[1] // 8
+    operands = list(weights) + ([gain] if gain is not None else []) + ([seg, tokens] if split else [])
+    ms = tokens.shape[0] if split else 1
     out_shape = [jax.ShapeDtypeStruct((8 * rows, cols), BF16)]
-    if seg is not None:
+    if split:
         out_shape.append(jax.ShapeDtypeStruct((8, *seg.shape), seg.dtype))
         out_shape.append(jax.ShapeDtypeStruct(tokens.shape, tokens.dtype))
     return pl.pallas_call(
-        functools.partial(spread_kernel, gain is not None, split),
+        functools.partial(spread_kernel, heads, gain is not None, split),
         out_shape=out_shape,
         in_specs=[WHOLE] * len(operands) + [ANY] * len(earlier),
         out_specs=[ANY] * len(out_shape),
@@ -570,74 +721,119 @@
     )(*operands, *earlier)
 
 
-def return_kernel(with_gain, p_ref, *refs):
-    refs = list(refs)
-    w_ref, g_ref = (refs.pop(0), refs.pop(0)) if with_gain else (None, None)
-    got, own_sem, send_sem, recv_sem = refs[-4:]
-    o_ref = refs[-6] if with_gain else refs[-5]
-    _, rows, cols = got.shape
-    me, peers = others()
-    greet(*(target for _, target in peers))
-
-    def block(p):
-        return p_ref.at[pl.ds(pl.multiple_of(p * rows, rows), rows), :]
-
-    copies = []
-    for kind, (p, target) in enumerate(peers):
-        copy = pltpu.make_async_remote_copy(
-            src_ref=block(p), dst_ref=got.at[me], send_sem=send_sem.at[kind], recv_sem=recv_sem.at[kind],
-            device_id=target, device_id_type=MESH,
-        )
-        copy.start()
-        copies.append(copy)
-    keep = pltpu.make_async_copy(block(me), got.at[me], own_sem)
-    keep.start()
-    total = jnp.zeros((rows, 1), F32)
-
-    def finish(p, total):
-        columns = pl.ds(pl.multiple_of(p * cols, cols), cols)
-        grad = got[p].astype(F32)
-        if with_gain:
-            total = total + jnp.sum(w_ref[:, columns].astype(F32) * grad, -1, keepdims=True)
-            grad = grad * g_ref[...]
-        o_ref[:, columns] = grad
-        return total
-
-    keep.wait()
-    total = finish(me, total)
-    for kind in (6, 2, 3, 4, 5, 0, 1):
-        copies[kind].wait_recv()
-        total = finish(peers[kind][0], total)
-    if with_gain:
-        refs[-5][...] = total
-    for copy in copies:
-        copy.wait_send()
-
-
-def to_rows(part, w, gain, *earlier):
-    cols = part.shape[1]
-    rows = part.shape[0] // 8
-    operands = [part] + ([w, gain] if gain is not None else [])
-    out_shape = [jax.ShapeDtypeStruct((rows, 8 * cols), F32)]
-    if gain is not None:
-        out_shape.append(jax.ShapeDtypeStruct((rows, 1), F32))
-    return pl.pallas_call(
-        functools.partial(return_kernel, gain is not None),
-        out_shape=out_shape,
-        in_specs=[ANY] + [WHOLE] * (len(operands) - 1) + [ANY] * len(earlier),
-        out_specs=[WHOLE] * len(out_shape),
-        scratch_shapes=[
-            pltpu.VMEM((8, rows, cols), BF16),
+class Rows:
+    def __init__(self, part, weights=(), gain=None):
+        self.cols, rows = part.shape[1], part.shape[0] // 8
+        self.heads, self.scaled = len(weights) == 3, gain is not None
+        self.operands = [part, *weights] + ([gain] if self.scaled else [])
+        widths = [w.shape[1] for w in weights] if self.heads else [8 * self.cols]
+        self.out = [jax.ShapeDtypeStruct((rows, n), F32) for n in widths + ([1] if self.scaled else [])]
+        self.scratch = [
+            pltpu.VMEM((8, rows, self.cols), BF16),
             pltpu.SemaphoreType.DMA,
             pltpu.SemaphoreType.DMA((7,)),
             pltpu.SemaphoreType.DMA((7,)),
-        ],
+        ]
+
+    def start(self, me, peers, p_ref, got, own_sem, send_sem, recv_sem):
+        rows = got.shape[1]
+
+        def block(p):
+            return p_ref.at[pl.ds(pl.multiple_of(p * rows, rows), rows), :]
+
+        copies = []
+        for kind, (p, target) in enumerate(peers):
+            copy = pltpu.make_async_remote_copy(
+                src_ref=block(p), dst_ref=got.at[me], send_sem=send_sem.at[kind], recv_sem=recv_sem.at[kind],
+                device_id=target, device_id_type=MESH,
+            )
+            copy.start()
+            copies.append(copy)
+        keep = pltpu.make_async_copy(block(me), got.at[me], own_sem)
+        keep.start()
+        return copies, keep
+
+    def store(self, p, place, got, ins, outs, total):
+        grad = got[p].astype(F32)
+        if self.heads:
+            q_cols, kv_cols = head_columns(*place)
+            wq, wk, wv, gain = ins
+            q_out, k_out, v_out, _ = outs
+            for_q, for_kv = grad[:, :HEAD_DIM], grad[:, HEAD_DIM:]
+            is_key = place[1] == 0
+            w_kv = jnp.where(is_key, wk[:, kv_cols].astype(F32), wv[:, kv_cols].astype(F32))
+            q_out[:, q_cols] = for_q * gain[...]
+
+            @pl.when(is_key)
+            def _():
+                k_out[:, kv_cols] = for_kv * gain[...]
+
+            @pl.when(jnp.logical_not(is_key))
+            def _():
+                v_out[:, kv_cols] = for_kv * gain[...]
+
+            terms = wq[:, q_cols].astype(F32) * for_q + w_kv * for_kv
+            return total + jnp.sum(terms, -1, keepdims=True)
+        columns = pl.ds(pl.multiple_of(p * self.cols, self.cols), self.cols)
+        if self.scaled:
+            total = total + jnp.sum(ins[0][:, columns].astype(F32) * grad, -1, keepdims=True)
+            grad = grad * ins[1][...]
+        outs[0][:, columns] = grad
+        return total
+
+
+def to_rows(items, *earlier, moves=None):
+    split, tokens = moves or (0, None)
+    moved = [tokens] if moves else []
+    operands = [a for item in items for a in item.operands]
+    specs = [spec for item in items for spec in [ANY] + [WHOLE] * (len(item.operands) - 1)]
+    outs = [o for item in items for o in item.out]
+    ms = tokens.shape[0] if moves else 1
+
+    def kernel(*refs):
+        refs = list(refs)
+        ins = [[refs.pop(0) for _ in item.operands] for item in items]
+        before = [refs.pop(0) for _ in moved]
+        refs = refs[len(earlier) :]
+        results = [[refs.pop(0) for _ in item.out] for item in items]
+        behind = [refs.pop(0) for _ in moved]
+        held = [[refs.pop(0) for _ in item.scratch] for item in items]
+        me, peers = others()
+        x, c, y, *_ = flips()
+        targets = [target for _, target in peers]
+        if moved:
+            finish = start_tokens(split, True, before[0], behind[0], *refs, targets)
+        else:
+            greet(*targets)
+        started = [item.start(me, peers, i[0], *h) for item, i, h in zip(items, ins, held)]
+        for item, i, o, h, (copies, keep) in zip(items, ins, results, held, started):
+            total = jnp.zeros((h[0].shape[1], 1), F32)
+            keep.wait()
+            total = item.store(me, (x, c, y), h[0], i[1:], o, total)
+            for kind in (6, 2, 3, 4, 5, 0, 1):
+                copies[kind].wait_recv()
+                p, target = peers[kind]
+                total = item.store(p, (target["x"], target["core"], target["y"]), h[0], i[1:], o, total)
+            if item.scaled:
+                o[-1][...] = total
+        for copies, _ in started:
+            for copy in copies:
+                copy.wait_send()
+        if moved:
+            finish()
+
+    return pl.pallas_call(
+        kernel,
+        out_shape=outs + [jax.ShapeDtypeStruct(t.shape, t.dtype) for t in moved],
+        in_specs=specs + [ANY] * (len(moved) + len(earlier)),
+        out_specs=[WHOLE] * len(outs) + [ANY] * len(moved),
+        scratch_shapes=[t for item in items for t in item.scratch] + [pltpu.SemaphoreType.DMA((ms,))] * 2 * len(moved),
         compiler_params=pltpu.CompilerParams(
-            collective_id=fresh(), has_side_effects=True, vmem_limit_bytes=24 << 20
+            collective_id=fresh(), has_side_effects=True, vmem_limit_bytes=32 << 20
         ),
         cost_estimate=light(),
         name="weight_rows",
-    )(*operands, *earlier)
+    )(*operands, *moved, *earlier)
 
 
 def tie_kernel(a_ref, *refs):
@@ -699,13 +895,27 @@
         lead = a.shape[:-1]
         return a.reshape(*lead, nz, dp, col_block).swapaxes(-3, -2).reshape(*lead, width)
 
-    def by_head(a):
-        return a.reshape(a.shape[0], 2, 2, 2, -1).swapaxes(2, 3).reshape(a.shape[0], 8, -1)
-
-    def from_head(a):
-        return a.reshape(a.shape[0], 2, 2, 2, -1).swapaxes(2, 3).reshape(a.shape[0], -1)
-
-    heads_of = [(x * 2 + y) * 2 + c for x in range(2) for c in range(2) for y in range(2)]
+    whole_lanes = col_block % 128 == 0
+
+    def inward(v):
+        return reorder(v, dp, nz) if whole_lanes else v
+
+    def outward(v):
+        return reorder(v, nz, dp) if whole_lanes else v
+
+    def inside(a):
+        return a if whole_lanes else perm(a)
+
+    def outside(a):
+        return a if whole_lanes else unperm(a)
+
+    def scale_of(v):
+        return lax.rsqrt(jnp.mean(v * v, -1, keepdims=True) + NORM_EPS)
+
+    def norm_back(v, d_hat):
+        scale = scale_of(v)
+        hat = v * scale
+        return scale * (d_hat - hat * jnp.mean(d_hat * hat, -1, keepdims=True))
 
     def place(x, c, z, y):
         return ((x * 2 + c) * nz + z) * 2 + y
@@ -719,72 +929,34 @@
                     to_head.append((head * nz + k, place(x, c, k, y)))
                     to_owner.append((place(x, c, k, y), head * nz + k))
 
-    def slot_of(z):
-        return z // 2 if split == 2 else z // 4
-
-    def group_of(z):
-        return z // 2 if split == 2 else z // 4
-
-    rounds = []
-    for k in range(ms):
-        moves = []
-        for ox in range(2):
-            for oc in range(2):
-                for oz in range(nz):
-                    j = (k + slot_of(oz)) % ms
-                    if split == 2:
-                        to = (oz % 2, oc, 2 * j + ox)
-                    else:
-                        to = (oz % 2, oz // 2 % 2, (2 * j + ox) * 2 + oc)
-                    moves += [(place(ox, oc, oz, oy), place(*to, oy)) for oy in range(2)]
-        rounds.append(moves)
-
     def pick(a, index):
         return lax.dynamic_index_in_dim(a, index, 0, keepdims=False)
 
-    def to_planes(a):
-        got = jnp.stack([
-            lax.ppermute(pick(a, (k + slot_of(z_index)) % ms), EVERY, rounds[k]) for k in range(ms)
-        ])
-        return jnp.stack([pick(got, (group_of(z_index) - slot + ms) % ms) for slot in range(ms)])
-
-    def from_planes(a):
-        got = jnp.stack([
-            lax.ppermute(
-                pick(a, (group_of(z_index) - k + ms) % ms), EVERY, [(to, of) for of, to in rounds[k]]
-            )
-            for k in range(ms)
-        ])
-        return jnp.stack([pick(got, (j - slot_of(z_index) + ms) % ms) for j in range(ms)])
-
     g1 = attn_gain.astype(F32)[:, None]
     g2 = ffn_gain.astype(F32)[:, None]
 
-    wq_own = by_head(query_weight)
-    wkv_own = jnp.stack(
-        [key_weight.reshape(rows_w, KV_HEADS, HEAD_DIM), value_weight.reshape(rows_w, KV_HEADS, HEAD_DIM)], 2
-    ).reshape(rows_w, 8 * HEAD_DIM)
-    wkv_own = by_head(wkv_own)
-    wqkv_own = jnp.concatenate([wq_own, wkv_own], 2).reshape(rows_w, -1)
+    wqkv = (query_weight, key_weight, value_weight)
     wqkv_part, seg_all, x = to_columns(
-        wqkv_own, g1, segments.reshape(ms, seq_len), split=split, tokens=tokens.reshape(ms, pl_len, width)
-    )
-    (gate_part,) = to_columns(gate_weight, g2, None, wqkv_part)
+        wqkv, g1, segments.reshape(ms, seq_len), split=split, tokens=tokens.reshape(ms, pl_len, width)
+    )
     w_qkv = along_z(wqkv_part)
     w_out = along_z(lax.ppermute(perm(out_weight), EVERY, to_head))
 
     seg_all = seg_all.reshape(2, 2, 2, ms, seq_len)[:, :, 0]
     if split == 2:
-        seg = pick(pick(seg_all, z_index % 2).swapaxes(0, 1), z_index // 2)
+        seg = pick(pick(seg_all.swapaxes(0, 1), z_index % 2).swapaxes(0, 1), z_index // 2)
     else:
         seg = pick(pick(pick(seg_all, z_index // 2 % 2), z_index % 2), z_index // 4)[None]
     qseg, kseg = seg[:, :, None], seg[:, None, :]
 
-    x = perm(x).astype(F32)
-    r1 = lax.rsqrt(jnp.mean(x * x, -1, keepdims=True) + NORM_EPS)
-    xhat = x * r1
-    xa = plane_gather(xhat.astype(BF16), split, gate_part)
-    (down_part,) = to_columns(down_weight, None, None, xa)
+    x = inside(x)
+
+    def norm_in(v):
+        v = inward(v.astype(F32))
+        return v * scale_of(v)
+
+    xa = plane_gather([x], norm_in, split, wqkv_part)
+    (gate_part,) = to_columns([gate_weight], g2, None, xa)
 
     inv_freq = 1.0 / ROPE_BASE ** (jnp.arange(0, HEAD_DIM, 2, dtype=F32) / HEAD_DIM)
     angles = jnp.arange(seq_len, dtype=jnp.int32).astype(F32)[:, None] * inv_freq[None, :]
@@ -795,21 +967,22 @@
     qkv = dot_nn(xa, w_qkv)
     qb = rotate(qkv[:, :HEAD_DIM], cos_q, sin_q).astype(BF16).reshape(split, seq_len, HEAD_DIM)
     kvb = rotate(qkv[:, HEAD_DIM:], cos_k, sin_k).astype(BF16)
-    kv_all = core_gather(kvb, down_part).reshape(2, split, seq_len, HEAD_DIM)
+    kv_all = core_gather(kvb, gate_part).reshape(2, split, seq_len, HEAD_DIM)
 
     w_gate = along_z(gate_part)
+    ob = attn_forward(qb, kv_all, qseg, kseg).reshape(n_plane, HEAD_DIM)
+    (down_part,) = to_columns([down_weight], None, None, ob)
     w_down = along_z(down_part)
-    ob = attn_forward(qb, kv_all, qseg, kseg).reshape(n_plane, HEAD_DIM)
-    cot = perm(to_planes(tie(cotangent.reshape(ms, pl_len, width), ob)))
-    h = x + plane_scatter(dot_nn(ob, w_out).astype(BF16), split, ms)
-
-    r2 = lax.rsqrt(jnp.mean(h * h, -1, keepdims=True) + NORM_EPS)
-    hhat = h * r2
-    ha = plane_gather(hhat.astype(BF16), split)
-    (up_part,) = to_columns(up_weight, g2, None, ha)
+    h, cot = plane_scatter(
+        [("nn", ob, w_out)], [x], lambda total, v: inward(v.astype(F32)) + total, F32, split, ms, down_part,
+        moves=(split, False, cotangent.reshape(ms, pl_len, width)),
+    )
+    cot = inside(cot)
+
+    ha = plane_gather([h], lambda v: v * scale_of(v), split)
+    (up_part,) = to_columns([up_weight], g2, None, ha)
     w_up = along_z(up_part)
-    ca = plane_gather(cot, split, up_part)
-    gate = dot_nn(ha, w_gate)
+    ca, gate = plane_gather([cot], inward, split, up_part, matmuls=[Matmul("nn", ha, w_gate, F32)])
     sig = jax.nn.sigmoid(gate)
     silu = gate * sig
     d_mid = dot_nn(ca, w_down)
@@ -819,13 +992,15 @@
     up = dot_nn(ha, w_up)
     dgb = (d_mid * up * sig * (1.0 + gate * (1.0 - sig))).astype(BF16)
     mid = (silu * up).astype(BF16)
-    part_hhat = (dot_nt(dgb, w_gate) + dot_nt(dub, w_up)).astype(BF16)
-    d_gate = dot_tn(ha, dgb).astype(BF16)
+    dh, d_gate = plane_scatter(
+        [("nt", dgb, w_gate), ("nt", dub, w_up)],
+        [h, cot],
+        lambda total, v, dy: inward(dy.astype(F32)) + norm_back(v, total),
+        F32, split, ms, matmuls=[Matmul("tn", ha, dgb)],
+    )
     up_z = sum_along_z(d_up)
     gate_z = sum_along_z(d_gate)
-    d_hhat = plane_scatter(part_hhat, split, ms, d_gate)
-    dh = cot.astype(F32) + r2 * (d_hhat - hhat * jnp.mean(d_hhat * hhat, -1, keepdims=True))
-    da = plane_gather(dh.astype(BF16), split)
+    da, d_down = plane_gather([dh], lambda v: v, split, matmuls=[Matmul("tn", ca, mid)])
     dob = dot_nt(da, w_out).astype(BF16)
 
     dq, dkv_h = attn_backward(qb, kv_all, dob.reshape(qb.shape), qseg, kseg, up_z)
@@ -833,31 +1008,27 @@
     dqb = rotate(dq.reshape(n_plane, HEAD_DIM), cos_q, -sin_q).astype(BF16)
     dkvb = rotate(dkv, cos_k, -sin_k).astype(BF16)
     dqkv = jnp.concatenate([dqb, dkvb], 1)
-    d_down = dot_tn(ca, mid).astype(BF16)
-    d_qkv = dot_tn(xa, dqkv).astype(BF16)
-    d_out = dot_tn(ob, da).astype(BF16)
     down_z = sum_along_z(d_down)
+    input_grad, d_qkv, d_out = plane_scatter(
+        [("nt", dqkv, w_qkv)],
+        [x, dh],
+        lambda total, v, direct: outward(direct + norm_back(inward(v.astype(F32)), total)),
+        BF16, split, ms, matmuls=[Matmul("tn", xa, dqkv), Matmul("tn", ob, da)],
+    )
+    qkv_z = sum_along_z(d_qkv)
     out_z = sum_along_z(d_out)
-    qkv_z = sum_along_z(d_qkv)
-    part_xhat = dot_nt(dqkv, w_qkv).astype(BF16)
-    d_xhat = plane_scatter(part_xhat, split, ms, d_down, d_qkv)
-    input_grad = dh + r1 * (d_xhat - xhat * jnp.mean(d_xhat * xhat, -1, keepdims=True))
-    input_grad = from_planes(unperm(input_grad).astype(BF16)).astype(F32).reshape(tokens.shape)
-
-    up_back, up_gain = to_rows(up_z, up_weight, g2, d_xhat)
-    part_out = dot_nt(mid, w_down).astype(BF16)
-    result = h + plane_scatter(part_out, split, ms, up_back)
-    output = from_planes(unperm(result.astype(BF16))).reshape(tokens.shape)
-    gate_back, gate_gain = to_rows(gate_z, gate_weight, g2, result)
-
-    (down_back,) = to_rows(down_z, None, None, gate_back)
+    up_back, up_gain, gate_back, gate_gain, input_grad = to_rows(
+        [Rows(up_z, [up_weight], g2), Rows(gate_z, [gate_weight], g2)], moves=(split, outside(input_grad))
+    )
+    input_grad = input_grad.astype(F32).reshape(tokens.shape)
+    output = plane_scatter(
+        [("nt", mid, w_down)], [h], lambda total, v: outward(v + total), BF16, split, ms, up_back, down_z
+    )
+    out_z = tie(out_z, output)
+    down_back, output = to_rows([Rows(down_z)], moves=(split, outside(output)))
+    output = output.reshape(tokens.shape)
     out_back = unperm(lax.ppermute(out_z, EVERY, to_owner).astype(F32))
-    qkv_back, attn_gain_term = to_rows(qkv_z, wqkv_own, g1, down_back)
-    qkv_back = qkv_back.reshape(rows_w, 8, -1)
-    q_back = from_head(qkv_back[:, :, :HEAD_DIM])
-    kv_back = from_head(qkv_back[:, :, HEAD_DIM:]).reshape(rows_w, KV_HEADS, 2, HEAD_DIM)
-    k_back = kv_back[:, :, 0].reshape(rows_w, -1)
-    v_back = kv_back[:, :, 1].reshape(rows_w, -1)
+    q_back, k_back, v_back, attn_gain_term = to_rows([Rows(qkv_z, wqkv, g1)], down_back, out_back)
 
     return (
         output,

time: 902 us -> 786 us (0.87)
  matrix products: 181 us -> 65.1 us
  waiting for transfers between devices: 11.8 us -> 53.4 us
  local copies, waits for them, and re-layouts: 86.6 us -> 64.6 us
  starting transfers between devices: 20.2 us -> 5.06 us
    dot_general x5 -> x1, matrix products: 62.6 us -> 7.06 us  [dot_nt(): lax.dot_general(a, b, (((1,), (1,)), ((), ())), preferred_element_type=F32)]
    dot_general x5 -> x1, matrix products: 56.4 us -> 13.3 us  [dot_tn(): lax.dot_general(a, b, (((0,), (0,)), ((), ())), preferred_element_type=F32)]
    all_gather x5, waiting for transfers between devices: 11.6 us -> 37.4 us  [along_z(): return lax.all_gather(part, 'z', axis=0, tiled=True)]
    dot_general x5 -> x3, matrix products: 61.6 us -> 44.7 us  [dot_nn(): lax.dot_general(a, b, (((1,), (0,)), ((), ())), preferred_element_type=F32)]
    ppermute x6 -> x0, starting transfers between devices: 16.2 us -> none  [the longest x4 10.9 us: from_planes(): lax.ppermute(pick(a, (group_of(z_index) - k + ms) % ms), EVERY, [(to, of)...]
    unnamed x138 -> x107, local copies, waits for them, and re-layouts: 43.5 us -> 59.6 us
    reduce_scatter x5, waiting for transfers between devices: 0.01 us -> 15.4 us  [sum_along_z(): return lax.psum_scatter(g, 'z', scatter_dimension=0, tiled=True)]
    pallas_call x16 -> x15, Pallas kernels: 531 us -> 535 us  [the longest x8 382 us: communicate(): pl.pallas_call(kernel, out_shape=[shape] + [m.out for m in matmuls] + [ja...]
  transfers between devices with their start and end apart: 18 -> 12, of which waited for: 1 -> 2; matrix products, arithmetic and copies ran while one was open for 27% -> 11% of each run, Pallas kernels for 57% -> 67%
where the time goes in v3:
time: 786 us; the launch traced here: 773 us
  Pallas kernels  555 us (71%)
  matrix products  65.1 us (8%)
  local copies, waits for them, and re-layouts  64.6 us (8%)
  waiting for transfers between devices  53.4 us (7%)
  between operations  15 us (2%)
  other arithmetic  14.5 us (2%)
    pallas_call x8, Pallas kernels, communicate(): pl.pallas_call(kernel, out_shape=[shape] + [m.out for m in matmuls] + [ja...  382 us
    pallas_call x4, Pallas kernels, to_columns(): pl.pallas_call(functools.partial(spread_kernel, heads, gain is not None,...  76.9 us
    pallas_call x3, Pallas kernels, to_rows(): pl.pallas_call(kernel, out_shape=outs + [jax.ShapeDtypeStruct(t.shape, t....  75.6 us
    unnamed x107, local copies, waits for them, and re-layouts  59.6 us
    dot_general x3, matrix products, dot_nn(): lax.dot_general(a, b, (((1,), (0,)), ((), ())), preferred_element_type=F32)  44.7 us
    all_gather x5, waiting for transfers between devices, along_z(): return lax.all_gather(part, 'z', axis=0, tiled=True)  37.4 us
  transfers between devices with their start and end apart: 12, of which 2 were waited for; matrix products, arithmetic and copies ran while one was open for 11% of the time, Pallas kernels for 67%

profile of v3, /device:TPU:29, one launch (start us, length us, event | category | flops | bytes accessed | tf_op | source)
XLA Modules:
  0.0 773.0 jit_solution(772594308898653803)
XLA Ops:
  9.9 27.6 %weight_columns.4 = (bf16[512,512]{1,0:T(8,128)(2,1)}, s32[8,2,1024]{2,1,0:T(2,128)}, bf16[2,128,2048]{2,1,0:T(8,128)(2,1)}) custom-call(bf16[64,2048]{1,0:T(8,128)(2,1)} %refs_1_.5, bf16[64,1024]{1,0:T(8,128)(2,1)} %refs_2_.3, bf16[64,1024]{1,0:T(8,128)(2,1)} %refs_3_.1, f32[64,1]{1,0:T(8,128)} %copy.36.refs_3_.refs_4_, s32[2,1024]{1,0:T(2,128)} %bitcast.178, ...), custom_call_target="tpu_custom_call" | custom-call | bytes 1024 | tf_op jit(solution)/shard_map/weight_columns/pallas_call | solution.py:705
  44.1 48.4 %plane_gather.4 = bf16[2,2,2,2,128,2048]{5,4,3,2,1,0:T(8,128)(2,1)S(1)} custom-call(bf16[2,128,2048]{2,1,0:T(8,128)(2,1)S(1)} %copy-done.12, bf16[512,512]{1,0:T(8,128)(2,1)S(1)} %copy-done.25), custom_call_target="tpu_custom_call" | custom-call | bytes 1024 | tf_op jit(solution)/shard_map/plane_gather/pallas_call | solution.py:268
  92.6 3.3 copy-done.1
  95.9 16.3 %weight_columns.5.refs_0_ = bf16[512,1024]{1,0:T(8,128)(2,1)} custom-call(bf16[64,8192]{1,0:T(8,128)(2,1)} %refs_4_.1, f32[64,1]{1,0:T(8,128)} %copy.37.refs_1_.refs_2_.refs_5_, bf16[2048,2048]{1,0:T(8,128)(2,1)} %bitcast.147), custom_call_target="tpu_custom_call" | custom-call | bytes 1024 | tf_op jit(solution)/shard_map/weight_columns/pallas_call | solution.py:705
  114.7 7.7 fusion.28
  123.6 2.8 core_gather.1
  126.6 4.5 attention_forward.1
  132.1 16.4 %weight_columns.6.refs_4_ = bf16[512,1024]{1,0:T(8,128)(2,1)} custom-call(bf16[64,8192]{1,0:T(8,128)(2,1)} %refs_0_.6, bf16[2048,256]{1,0:T(8,128)(2,1)} %bitcast.155), custom_call_target="tpu_custom_call" | custom-call | bytes 1024 | tf_op jit(solution)/shard_map/weight_columns/pallas_call | solution.py:705
  148.6 59.6 %plane_scatter.4 = (f32[2,128,2048]{2,1,0:T(8,128)}, bf16[2,128,2048]{2,1,0:T(8,128)(2,1)}) custom-call(bf16[2,2,2,2,128,256]{5,4,3,2,1,0:T(8,128)(2,1)} %bitcast.156, bf16[256,2048]{1,0:T(8,128)(2,1)} %all-gather.8.cloned.1.call-done.refs_1_, bf16[2,128,2048]{2,1,0:T(8,128)(2,1)} %get-tuple-element.38.refs_0_.refs_2_, bf16[2,128,2048]{2,1,0:T(8,128)(2,1)} %bitcast.175, ...), custom_call_target="tpu_custom_call" | custom-call | bytes 1024 | tf_op jit(solution)/shard_map/plane_scatter/pallas_call | solution.py:268
  209.8 38.5 %plane_gather.5 = bf16[2,2,2,2,128,2048]{5,4,3,2,1,0:T(8,128)(2,1)S(1)} custom-call(f32[2,128,2048]{2,1,0:T(8,128)S(1)} %copy-done.3), custom_call_target="tpu_custom_call" | custom-call | bytes 1024 | tf_op jit(solution)/shard_map/plane_gather/pallas_call | solution.py:268
  248.4 3.3 copy-done
  251.7 16.5 %weight_columns.7.refs_3_ = bf16[512,1024]{1,0:T(8,128)(2,1)} custom-call(bf16[64,8192]{1,0:T(8,128)(2,1)} %refs_1_.4, f32[64,1]{1,0:T(8,128)} %copy.37.refs_1_.refs_2_.refs_5_, bf16[2048,2048]{1,0:T(8,128)(2,1)} %bitcast.142), custom_call_target="tpu_custom_call" | custom-call | bytes 1024 | tf_op jit(solution)/shard_map/weight_columns/pallas_call | solution.py:705
  272.1 39.3 %plane_gather.6 = (bf16[2,2,2,2,128,2048]{5,4,3,2,1,0:T(8,128)(2,1)}, f32[2048,1024]{1,0:T(8,128)}) custom-call(bf16[2,128,2048]{2,1,0:T(8,128)(2,1)S(1)} %copy-done.16, bf16[2048,2048]{1,0:T(8,128)(2,1)} %bitcast.143, bf16[2048,1024]{1,0:T(8,128)(2,1)S(1)} %copy-done.5, bf16[512,1024]{1,0:T(8,128)(2,1)S(1)} %copy-done.7), custom_call_target="tpu_custom_call" | custom-call | bytes 1024 | tf_op jit(solution)/shard_map/plane_gather/pallas_call | solution.py:268
  311.4 16.5 %multiply_convert_fusion.2 = (bf16[2048,1024]{1,0:T(8,128)(2,1)S(1)}, f32[2048,1024]{1,0:T(8,128)}) fusion(f32[2048,1024]{1,0:T(8,128)} %get-tuple-element.44, bf16[2048,2048]{1,0:T(8,128)(2,1)} %bitcast.162, bf16[2048,1024]{1,0:T(8,128)(2,1)} %all-gather.12.cloned.1.call-done.refs_1_), kind=kOutput, calls=%fused_computation.2 | convolution fusion | flops 8602517504 | bytes 33554432 | tf_op jit(solution)/shard_map/dot_general | solution.py:31
  329.9 13.3 %convolution_convert_fusion.refs_0_ = bf16[2048,1024]{1,0:T(8,128)(2,1)} fusion(bf16[2048,2048]{1,0:T(8,128)(2,1)} %bitcast.144, bf16[2048,1024]{1,0:T(8,128)(2,1)S(1)} %get-tuple-element.101), kind=kOutput, calls=%fused_computation.5 | convolution fusion | flops 8592031744 | bytes 16777216 | tf_op jit(solution)/shard_map/dot_general | solution.py:39
  343.3 37.3 %all-gather.14.cloned.1.call-done.a_ref = bf16[2048,1024]{1,0:T(8,128)(2,1)} async-done(((bf16[512,1024]{1,0:T(8,128)(2,1)}), bf16[2048,1024]{1,0:T(8,128)(2,1)}) %all-gather.14.cloned.1.call-update) | async-done | bytes 4194320 | tf_op jit(solution)/shard_map/all_gather | solution.py:856
  380.7 20.5 %multiply_convert_fusion = (bf16[2048,1024]{1,0:T(8,128)(2,1)}, bf16[2048,1024]{1,0:T(8,128)(2,1)}) fusion(f32[2048,1024]{1,0:T(8,128)} %get-tuple-element.44, f32[2048,1024]{1,0:T(8,128)} %get-tuple-element.102, bf16[2048,2048]{1,0:T(8,128)(2,1)} %bitcast.145, bf16[2048,1024]{1,0:T(8,128)(2,1)} %tie.2.refs_3_), kind=kOutput, calls=%fused_computation | convolution fusion | flops 8617197568 | bytes 37748736 | tf_op jit(solution)/shard_map/dot_general | solution.py:31
  401.2 58.6 %plane_scatter.5 = (f32[2,128,2048]{2,1,0:T(8,128)}, bf16[2048,1024]{1,0:T(8,128)(2,1)}) custom-call(bf16[2,2,2,2,128,1024]{5,4,3,2,1,0:T(8,128)(2,1)} %bitcast.161, bf16[2048,1024]{1,0:T(8,128)(2,1)} %all-gather.10.cloned.1.call-done.refs_2_.refs_1_, bf16[2,2,2,2,128,1024]{5,4,3,2,1,0:T(8,128)(2,1)} %bitcast.170, bf16[2048,1024]{1,0:T(8,128)(2,1)} %tie.2.refs_3_, ...), custom_call_target="tpu_custom_call" | custom-call | bytes 1024 | tf_op jit(solution)/shard_map/plane_scatter/pallas_call | solution.py:268
  463.7 39.3 %plane_gather.7 = (bf16[2,2,2,2,128,2048]{5,4,3,2,1,0:T(8,128)(2,1)}, bf16[2048,1024]{1,0:T(8,128)(2,1)S(1)}) custom-call(f32[2,128,2048]{2,1,0:T(8,128)S(1)} %copy-done.15, bf16[2048,2048]{1,0:T(8,128)(2,1)} %bitcast.163, bf16[2048,1024]{1,0:T(8,128)(2,1)S(1)} %copy-done.4), custom_call_target="tpu_custom_call" | custom-call | bytes 1024 | tf_op jit(solution)/shard_map/plane_gather/pallas_call | solution.py:268
  505.1 7.1 convolution_convert_fusion.1
  514.6 9.7 %attention_backward.1 = (f32[2,1024,256]{2,1,0:T(8,128)}, bf16[2,2,1024,256]{3,2,1,0:T(8,128)(2,1)}) custom-call(bf16[2,1024,256]{2,1,0:T(8,128)(2,1)S(1)} %pad_maximum_fusion.2.q_ref, bf16[2,2,1024,256]{3,2,1,0:T(8,128)(2,1)} %bitcast.152, bf16[2,2,1024,256]{3,2,1,0:T(8,128)(2,1)} %bitcast.153, bf16[2,1024,256]{2,1,0:T(8,128)(2,1)S(1)} %bitcast.159, ...), custom_call_target="tpu_custom_call" | custom-call | bytes 1024 | tf_op jit(solution)/shard_map/attention_backward/pallas_call | solution.py:133
  524.3 15.3 %reduce-scatter.10.cloned.1.call-done.refs_0_.refs_3_ = bf16[512,1024]{1,0:T(8,128)(2,1)} async-done(((bf16[2048,1024]{1,0:T(8,128)(2,1)}), bf16[512,1024]{1,0:T(8,128)(2,1)}) %reduce-scatter.10.cloned.1.call-update) | async-done | bytes 1048592 | tf_op jit(solution)/shard_map/reduce_scatter | solution.py:860
  542.5 3.4 core_scatter.1
  550.8 51.5 %plane_scatter.6 = (bf16[2,128,2048]{2,1,0:T(8,128)(2,1)}, bf16[2048,512]{1,0:T(8,128)(2,1)}, bf16[256,2048]{1,0:T(8,128)(2,1)}) custom-call(bf16[2,2,2,2,128,512]{5,4,3,2,1,0:T(8,128)(2,1)} %pad_maximum_fusion.refs_0_, bf16[2048,512]{1,0:T(8,128)(2,1)} %all-gather.6.cloned.1.call-done.refs_1_, bf16[2,128,2048]{2,1,0:T(8,128)(2,1)} %get-tuple-element.38.refs_0_.refs_2_, ...), custom_call_target="tpu_custom_call" | custom-call | bytes 1024 | tf_op jit(solution)/shard_map/plane_scatter/pallas_call | solution.py:268
  607.8 32.3 %weight_rows.3 = (f32[64,8192]{1,0:T(8,128)S(1)}, f32[64,1]{1,0:T(8,128)S(1)}, f32[64,8192]{1,0:T(8,128)S(1)}, f32[64,1]{1,0:T(8,128)S(1)}, bf16[2,128,2048]{2,1,0:T(8,128)(2,1)S(1)}) custom-call(bf16[512,1024]{1,0:T(8,128)(2,1)S(1)} %copy-done.22, bf16[64,8192]{1,0:T(8,128)(2,1)S(1)} %copy-done.20, f32[64,1]{1,0:T(8,128)S(1)} %copy-done.34, ...), custom_call_target="tpu_custom_call" | custom-call | bytes 1024 | tf_op jit(solution)/shard_map/weight_rows/pallas_call | solution.py:825
  645.0 47.2 %plane_scatter.7.refs_1_.refs_0_ = bf16[2,128,2048]{2,1,0:T(8,128)(2,1)} custom-call(bf16[2,2,2,2,128,1024]{5,4,3,2,1,0:T(8,128)(2,1)} %bitcast.154, bf16[2048,1024]{1,0:T(8,128)(2,1)} %all-gather.12.cloned.1.call-done.refs_1_, f32[2,128,2048]{2,1,0:T(8,128)} %get-tuple-element.42.refs_0_.refs_4_.refs_2_, f32[64,8192]{1,0:T(8,128)} %copy-done.13, ...), custom_call_target="tpu_custom_call" | custom-call | bytes 1024 | tf_op jit(solution)/shard_map/plane_scatter/pallas_call | solution.py:268
  692.3 3.7 collective-permute-start.1
  696.0 2.8 bitcast_convert_fusion
  700.0 33.2 %weight_rows.4 = (f32[64,8192]{1,0:T(8,128)S(1)}, bf16[2,128,2048]{2,1,0:T(8,128)(2,1)S(1)}) custom-call(bf16[512,1024]{1,0:T(8,128)(2,1)S(1)} %copy-done.17, bf16[2,128,2048]{2,1,0:T(8,128)(2,1)S(1)} %copy-done.8), custom_call_target="tpu_custom_call" | custom-call | bytes 1024 | tf_op jit(solution)/shard_map/weight_rows/pallas_call | solution.py:825
  740.2 10.1 %weight_rows.5 = (f32[64,2048]{1,0:T(8,128)S(1)}, f32[64,1024]{1,0:T(8,128)S(1)}, f32[64,1024]{1,0:T(8,128)S(1)}, f32[64,1]{1,0:T(8,128)S(1)}) custom-call(bf16[512,512]{1,0:T(8,128)(2,1)S(1)} %copy-done.35, bf16[64,2048]{1,0:T(8,128)(2,1)S(1)} %copy-done.29, bf16[64,1024]{1,0:T(8,128)(2,1)S(1)} %copy-done.36, bf16[64,1024]{1,0:T(8,128)(2,1)S(1)} %copy-done.37, ...), custom_call_target="tpu_custom_call" | custom-call | bytes 1024 | tf_op jit(solution)/shard_map/weight_rows/pallas_call | solution.py:825
  753.7 2.5 copy.69
  760.3 3.1 copy.73
  (161 shorter events, 66.3 us)
Async XLA Ops:
  7.2 107.5 %all-gather.6.cloned.1.call-start = ((), (), s32[]{:S(2)}) async-start(), calls=%async_computation.5 | async-start | bytes 2621440 | tf_op jit(solution)/shard_map/all_gather | solution.py:856
  37.6 111.1 %all-gather.8.cloned.1.call-start = ((), (), s32[]{:S(2)}) async-start(), calls=%async_computation.6 | async-start | bytes 1310720 | tf_op jit(solution)/shard_map/all_gather | solution.py:856
  39.0 0.7 collective-permute-start
  40.4 228.1 %all-gather.10.cloned.1.call-start = ((), (), s32[]{:S(2)}) async-start(), calls=%async_computation.7 | async-start | bytes 5242880 | tf_op jit(solution)/shard_map/all_gather | solution.py:856
  92.5 3.3 copy-start.1
  95.9 16.4 %copy-start.48 = (s32[8,2,1024]{2,1,0:T(2,128)S(1)}, s32[8,2,1024]{2,1,0:T(2,128)}, u32[]{:S(2)}) copy-start(s32[8,2,1024]{2,1,0:T(2,128)} %get-tuple-element.40) | copy-start | bytes 196612
  112.2 199.2 %all-gather.12.cloned.1.call-start = ((), (), s32[]{:S(2)}) async-start(), calls=%async_computation.8 | async-start | bytes 5242880 | tf_op jit(solution)/shard_map/all_gather | solution.py:856
  112.7 13.8 %copy-start.10 = (s32[2,1024,1]{2,1,0:T(8,128)}, s32[2,1024,1]{2,1,0:T(8,128)S(1)}, u32[]{:S(2)}) copy-start(s32[2,1024,1]{2,1,0:T(8,128)S(1)} %copy.39.qseg_ref) | copy-start | bytes 24580
  114.7 7.7 %copy-start.44 = (f32[1024,128]{1,0:T(8,128)}, f32[1024,128]{1,0:T(8,128)S(1)}, u32[]{:S(2)}) copy-start(f32[1024,128]{1,0:T(8,128)S(1)} %get-tuple-element.100) | copy-start | bytes 1572868
  126.4 4.7 copy-start.2
  148.6 232.1 %all-gather.14.cloned.1.call-start = ((), (), s32[]{:S(2)}) async-start(), calls=%async_computation.9 | async-start | bytes 5242880 | tf_op jit(solution)/shard_map/all_gather | solution.py:856
  248.4 3.3 copy-start
  251.7 16.9 %copy-start.16 = (bf16[2,128,2048]{2,1,0:T(8,128)(2,1)S(1)}, bf16[2,128,2048]{2,1,0:T(8,128)(2,1)}, u32[]{:S(2)}) copy-start(bf16[2,128,2048]{2,1,0:T(8,128)(2,1)} %get-tuple-element.41.refs_0_.refs_5_) | copy-start | bytes 3145732
  268.3 243.9 %reduce-scatter.8.cloned.1.call-start = ((), (), s32[]{:S(2)}) async-start(), calls=%async_computation.11 | async-start | bytes 5242880 | tf_op jit(solution)/shard_map/reduce_scatter | solution.py:860
  268.6 2.2 copy-start.5
  327.9 2.1 copy-start.45
  343.3 196.4 %reduce-scatter.10.cloned.1.call-start = ((), (), s32[]{:S(2)}) async-start(), calls=%async_computation.12 | async-start | bytes 5242880 | tf_op jit(solution)/shard_map/reduce_scatter | solution.py:860
  459.8 185.1 %reduce-scatter.6.cloned.1.call-start = ((), (), s32[]{:S(2)}) async-start(), calls=%async_computation.10 | async-start | bytes 5242880 | tf_op jit(solution)/shard_map/reduce_scatter | solution.py:860
  459.9 2.2 copy-start.4
  502.9 2.1 copy-start.18
  505.0 187.2 %reduce-scatter.14.cloned.1.call-start = ((), (), s32[]{:S(2)}) async-start(), calls=%async_computation.14 | async-start | bytes 1310720 | tf_op jit(solution)/shard_map/reduce_scatter | solution.py:860
  505.1 7.1 copy-start.11
  542.5 3.4 copy-start.46
  550.7 52.1 %copy-start.19 = (bf16[64,8192]{1,0:T(8,128)(2,1)S(1)}, bf16[64,8192]{1,0:T(8,128)(2,1)}, u32[]{:S(2)}) copy-start(bf16[64,8192]{1,0:T(8,128)(2,1)} %refs_4_.1) | copy-start | bytes 3145732
  550.8 52.1 %copy-start.34 = (f32[64,1]{1,0:T(8,128)S(1)}, f32[64,1]{1,0:T(8,128)}, u32[]{:S(2)}) copy-start(f32[64,1]{1,0:T(8,128)} %copy.37.refs_1_.refs_2_.refs_5_) | copy-start | bytes 772
  602.3 135.1 %reduce-scatter.12.cloned.1.call-start = ((), (), s32[]{:S(2)}) async-start(), calls=%async_computation.13 | async-start | bytes 2621440 | tf_op jit(solution)/shard_map/reduce_scatter | solution.py:860
  692.2 6.6 copy-start.8
  692.2 45.1 %copy-start.29 = (bf16[64,2048]{1,0:T(8,128)(2,1)S(1)}, bf16[64,2048]{1,0:T(8,128)(2,1)}, u32[]{:S(2)}) copy-start(bf16[64,2048]{1,0:T(8,128)(2,1)} %refs_1_.5) | copy-start | bytes 786436
  692.2 45.1 %copy-start.36 = (bf16[64,1024]{1,0:T(8,128)(2,1)S(1)}, bf16[64,1024]{1,0:T(8,128)(2,1)}, u32[]{:S(2)}) copy-start(bf16[64,1024]{1,0:T(8,128)(2,1)} %refs_2_.3) | copy-start | bytes 393220
  692.3 43.3 %collective-permute-start.1 = (bf16[64,2048]{1,0:T(8,128)(2,1)}, bf16[64,2048]{1,0:T(8,128)(2,1)}, u32[]{:S(2)}, u32[]{:S(2)}) collective-permute-start(bf16[64,2048]{1,0:T(8,128)(2,1)} %tie.3), channel_id=1, source_target_pairs={{0,0},{2,1},{4,2},{6,3},{1,8},{3,9},{5,10},{7,11},{8,4},{10,5},{12... | collective-permute-start | bytes 786440 | tf_op jit(solution)/shard_map/ppermute | solution.py:1030
  737.3 26.1 %copy-start.26 = (f32[64,2048]{1,0:T(8,128)}, f32[64,2048]{1,0:T(8,128)S(1)}, u32[]{:S(2)}) copy-start(f32[64,2048]{1,0:T(8,128)S(1)} %reshape.231.refs_6_) | copy-start | bytes 1572868
  753.7 9.7 %copy-start.14 = (f32[64,8192]{1,0:T(8,128)S(1)}, f32[64,8192]{1,0:T(8,128)}, u32[]{:S(2)}) copy-start(f32[64,8192]{1,0:T(8,128)} %copy-done.13) | copy-start | bytes 6291460
  (29 other events, 31.7 us)
Sparse Core Ops, SparseCore 0:
  37.7 43.5 all-gather.5
  83.5 28.6 all-gather.7
  113.7 105.5 all-gather.9
  220.7 79.1 all-gather.11
  301.3 79.2 all-gather.13
  382.8 77.0 reduce-scatter.7
  462.3 77.2 reduce-scatter.9
  541.9 83.1 reduce-scatter.5
  627.5 33.1 reduce-scatter.13
  662.9 49.6 reduce-scatter.11

commit v4 on v3

v4 whole, which is shorter than its diff:
```python
import functools
import itertools

import jax
import jax.numpy as jnp
from jax import lax
from jax.experimental import pallas as pl
from jax.experimental.pallas import tpu as pltpu
from jax.sharding import Mesh
from jax.sharding import PartitionSpec as P

HEADS = 8
KV_HEADS = 4
HEAD_DIM = 256
WINDOW = 1024
NORM_EPS = 1e-06
ROPE_BASE = 1000042.0
NEG_LARGE = -1e30
SCALE = HEAD_DIM**-0.5
PLANE = ("x", "core", "y")
EVERY = ("x", "core", "z", "y")
BF16 = jnp.bfloat16
F32 = jnp.float32
MESH = pl.DeviceIdType.MESH
GATHER_PARTS = 4
SCATTER_PARTS = 4


def dot_nn(a, b):
    return lax.dot_general(a, b, (((1,), (0,)), ((), ())), preferred_element_type=F32)


def dot_nt(a, b):
    return lax.dot_general(a, b, (((1,), (1,)), ((), ())), preferred_element_type=F32)


def dot_tn(a, b):
    return lax.dot_general(a, b, (((0,), (0,)), ((), ())), preferred_element_type=F32)


def rotate(values, cosine, sine):
    half = values.shape[-1] // 2
    a, b = values[:, :half], values[:, half:]
    return jnp.concatenate([a * cosine - b * sine, b * cosine + a * sine], -1)


def reorder(values, outer, inner):
    block = values.shape[-1] // (outer * inner)
    return jnp.concatenate(
        [
            values[..., (o * inner + i) * block : (o * inner + i + 1) * block]
            for i in range(inner)
            for o in range(outer)
        ],
        -1,
    )


QUERY_ROWS = 256


def query_blocks(seq_len):
    out = []
    for first in range(0, seq_len, QUERY_ROWS):
        low = max(0, first - WINDOW + 1) // 128 * 128
        out.append((first, low, min(seq_len, first + QUERY_ROWS)))
    return out


def masked_prob(q, k, first, low, qseg, kseg):
    scores = dot_nt(q, k) * SCALE
    qpos = first + lax.broadcasted_iota(jnp.int32, scores.shape, 0)
    kpos = low + lax.broadcasted_iota(jnp.int32, scores.shape, 1)
    allowed = (kpos <= qpos) & (qpos - kpos < WINDOW) & (qseg == kseg)
    masked = jnp.where(allowed, scores, NEG_LARGE)
    e = jnp.exp(masked - jnp.max(masked, -1, keepdims=True))
    return e / jnp.sum(e, -1, keepdims=True)


def attn_fwd_kernel(q_ref, k_ref, v_ref, qseg_ref, kseg_ref, o_ref):
    for first, low, end in query_blocks(q_ref.shape[0]):
        rows, keys = pl.ds(first, QUERY_ROWS), pl.ds(low, end - low)
        prob = masked_prob(q_ref[rows, :], k_ref[keys, :], first, low, qseg_ref[rows, :], kseg_ref[:, keys])
        o_ref[rows, :] = dot_nn(prob.astype(BF16), v_ref[keys, :]).astype(BF16)


def attention_specs(seq_len):
    qspec = pl.BlockSpec((None, seq_len, HEAD_DIM), lambda s: (s, 0, 0))
    kspec = pl.BlockSpec((None, None, seq_len, HEAD_DIM), lambda s: (0, s, 0, 0))
    vspec = pl.BlockSpec((None, None, seq_len, HEAD_DIM), lambda s: (1, s, 0, 0))
    qseg = pl.BlockSpec((None, seq_len, 1), lambda s: (s, 0, 0))
    kseg = pl.BlockSpec((None, 1, seq_len), lambda s: (s, 0, 0))
    return qspec, kspec, vspec, qseg, kseg


def attn_forward(q, kv, qseg, kseg):
    seqs, seq_len, _ = q.shape
    qspec, kspec, vspec, qi, ks = attention_specs(seq_len)
    return pl.pallas_call(
        attn_fwd_kernel,
        grid=(seqs,),
        in_specs=[qspec, kspec, vspec, qi, ks],
        out_specs=qspec,
        out_shape=jax.ShapeDtypeStruct(q.shape, BF16),
        compiler_params=pltpu.CompilerParams(vmem_limit_bytes=48 << 20),
        cost_estimate=light(),
        name="attention_forward",
    )(q, kv, kv, qseg, kseg)


NUMBERS = [0]


def fresh():
    NUMBERS[0] += 1
    return NUMBERS[0] - 1


def flips():
    x, c, y = (lax.axis_index(a) for a in PLANE)
    return x, c, y, {"x": 1 - x}, {"y": 1 - y}, {"core": 1 - c}


def greet(*targets):
    join([([(target, None) for target in targets], len(targets))])


def join(parties):
    barrier = pltpu.get_barrier_semaphore()

    def signal(target):
        pl.semaphore_signal(barrier, 1, device_id=target, device_id_type=MESH)

    count = 0
    for signals, number in parties:
        for target, remote in signals:
            if remote is None:
                signal(target)
            else:
                pl.when(remote)(functools.partial(signal, target))
        count = count + number
    pl.semaphore_wait(barrier, count)


def own_place():
    x, c, z, y = (lax.axis_index(a) for a in EVERY)
    return x, c, z, y, ((x * 2 + c) * lax.axis_size("z") + z) * 2 + y


def at_place(x, c, z, y):
    me = own_place()[-1]
    return {"x": x, "core": c, "z": z, "y": y}, ((x * 2 + c) * lax.axis_size("z") + z) * 2 + y != me


def send_or_keep(src, dst, send_sem, recv_sem, target, remote):
    def away():
        return pltpu.make_async_remote_copy(
            src_ref=src, dst_ref=dst, send_sem=send_sem, recv_sem=recv_sem, device_id=target, device_id_type=MESH
        )

    pl.when(remote)(lambda: away().start())
    pl.when(jnp.logical_not(remote))(lambda: pltpu.make_async_copy(src, dst, recv_sem).start())
    return lambda: pl.when(remote)(lambda: away().wait_send())


def remotes(devices):
    return sum(remote.astype(jnp.int32) for _, remote in devices)


def pieces_at(ref, split, px, pc, py):
    return ref.at[px, :, pc, py] if split == 2 else ref.at[:, pc, px, py]


def plane_shape(split, slots, *rest):
    return (2, slots, 2, 2, *rest) if split == 2 else (slots, 2, 2, 2, *rest)


ANY = pl.BlockSpec(memory_space=pl.ANY)
WHOLE = pl.BlockSpec(memory_space=pltpu.VMEM)


def light(bytes_accessed=1024):
    return pl.CostEstimate(flops=0, bytes_accessed=bytes_accessed, transcendentals=0)


FORMS = {"nn": dot_nn, "nt": dot_nt, "tn": dot_tn}


class Matmul:
    def __init__(self, form, a, b, dtype=BF16):
        self.form, self.operands = form, [a, b]
        rows = a.shape[1] if form == "tn" else a.shape[0]
        cols = b.shape[0] if form == "nt" else b.shape[1]
        self.out = jax.ShapeDtypeStruct((rows, cols), dtype)
        self.parts = max(1, rows // 256)
        self.scratch = [
            pltpu.VMEM(a.shape, a.dtype),
            pltpu.VMEM(b.shape, b.dtype),
            pltpu.VMEM(self.out.shape, dtype),
            pltpu.SemaphoreType.DMA((2,)),
            pltpu.SemaphoreType.DMA((self.parts,)),
        ]

    def steps(self, a_ref, b_ref, o_ref, a, b, out, load_sem, store_sem):
        loads = [
            pltpu.make_async_copy(a_ref, a, load_sem.at[0]),
            pltpu.make_async_copy(b_ref, b, load_sem.at[1]),
        ]
        for load in loads:
            load.start()
        yield
        for load in loads:
            load.wait()
        step = out.shape[0] // self.parts
        stores = []
        for i in range(self.parts):
            rows = pl.ds(i * step, step)
            left = a[:, rows] if self.form == "tn" else a[rows, :]
            out[rows, :] = FORMS[self.form](left, b[...]).astype(out.dtype)
            store = pltpu.make_async_copy(out.at[rows, :], o_ref.at[rows, :], store_sem.at[i])
            store.start()
            stores.append(store)
            yield
        for store in stores:
            store.wait()


def interleave(main, side):
    for matmul in side:
        next(matmul)
    rest = itertools.chain(*side)
    for _ in main:
        next(rest, None)
    for _ in rest:
        pass


def communicate(name, steps, operands, earlier, out, scratch, matmuls, vmem, specs=None, movers=()):
    n_in = len(operands)
    n_scratch = len(scratch)
    side_in = [a for m in matmuls for a in m.operands]

    def kernel(*refs):
        refs = list(refs)
        ins, refs = refs[:n_in], refs[n_in:]
        move_ins = [[refs.pop(0) for _ in m.operands] for m in movers]
        side_ins, refs = refs[: len(side_in)], refs[len(side_in) + len(earlier) :]
        outs, refs = refs[: 1 + len(matmuls)], refs[1 + len(matmuls) :]
        move_outs = [[refs.pop(0) for _ in m.out] for m in movers]
        own, refs = refs[:n_scratch], refs[n_scratch:]
        move_held = [[refs.pop(0) for _ in m.scratch] for m in movers]
        moving = [m.begin(i, o, h) for m, i, o, h in zip(movers, move_ins, move_outs, move_held)]

        def meet(*targets):
            for m in moving:
                next(m)
            join([([(t, None) for t in targets], len(targets))] + [m.party() for m in movers])
            for m in moving:
                next(m)

        side = []
        for i, m in enumerate(matmuls):
            side.append(m.steps(*side_ins[2 * i : 2 * i + 2], outs[1 + i], *refs[5 * i : 5 * i + 5]))
        interleave(steps(meet, *ins, outs[0], *own), side)
        for m in moving:
            next(m, None)

    shape, spec = out
    move_out = [o for m in movers for o in m.out]
    return pl.pallas_call(
        kernel,
        out_shape=[shape] + [m.out for m in matmuls] + move_out,
        in_specs=(specs or [ANY] * n_in)
        + [spec for m in movers for spec in m.specs]
        + [ANY] * (len(side_in) + len(earlier)),
        out_specs=[spec] + [ANY] * len(matmuls) + [spec for m in movers for spec in m.out_specs],
        scratch_shapes=scratch + [t for m in movers for t in m.scratch] + [t for m in matmuls for t in m.scratch],
        compiler_params=pltpu.CompilerParams(
            collective_id=fresh(), has_side_effects=True, vmem_limit_bytes=vmem << 20
        ),
        cost_estimate=light(),
        name=name,
    )(*operands, *[a for m in movers for a in m.operands], *side_in, *earlier)


def gather_steps(split, prepare, meet, *refs):
    sources, (o_ref, a_ref, own_sem, send_sem, recv_sem) = refs[:-5], refs[-5:]
    x, c, y, to_x, to_y, to_c = flips()
    slots, piece, _ = a_ref.shape
    per_slot = GATHER_PARTS // slots
    step = piece // per_slot
    meet(to_x, to_y, to_c)

    def rows_of(i):
        return i // per_slot, pl.ds(i % per_slot * step, step)

    def part(px, pc, py, i):
        return pieces_at(o_ref, split, px, pc, py).at[rows_of(i)]

    def send(kind, i, src, dst, target):
        copy = pltpu.make_async_remote_copy(
            src_ref=src, dst_ref=dst, send_sem=send_sem.at[kind, i], recv_sem=recv_sem.at[kind, i],
            device_id=target, device_id_type=MESH,
        )
        copy.start()
        return copy

    copies = {}
    for i in range(GATHER_PARTS):
        a_ref[rows_of(i)] = prepare(*(source[rows_of(i)] for source in sources)).astype(BF16)
        own = a_ref.at[rows_of(i)]
        for kind, target in enumerate((to_x, to_y, to_c)):
            copies[kind, i] = send(kind, i, own, part(x, c, y, i), target)
    own_copy = pltpu.make_async_copy(a_ref, pieces_at(o_ref, split, x, c, y), own_sem)
    own_copy.start()
    yield
    src_x, src_y = jnp.where(c == 0, x, 1 - x), jnp.where(c == 0, 1 - y, y)
    dst_x, dst_y = jnp.where(c == 0, 1 - x, x), jnp.where(c == 0, y, 1 - y)
    for i in range(GATHER_PARTS):
        for kind, (px, py) in enumerate(((1 - x, y), (x, 1 - y))):
            copies[kind, i].wait_recv()
            block = part(px, c, py, i)
            copies[3 + kind, i] = send(3 + kind, i, block, block, to_c)
        block = part(src_x, c, src_y, i)
        copies[5, i] = send(5, i, block, block, {"x": dst_x, "y": dst_y})
        yield
        yield
    for i in range(GATHER_PARTS):
        copies[5, i].wait_recv()
        block = part(1 - x, c, 1 - y, i)
        copies[6, i] = send(6, i, block, block, to_c)
        yield
    for i in range(GATHER_PARTS):
        for kind in (2, 3, 4, 6):
            copies[kind, i].wait_recv()
    own_copy.wait()
    for i in range(GATHER_PARTS):
        for kind in range(7):
            copies[kind, i].wait_send()


def plane_gather(sources, prepare, split, *earlier, matmuls=(), movers=()):
    slots, piece, width = sources[0].shape
    out = jax.ShapeDtypeStruct(plane_shape(split, slots, piece, width), BF16)
    scratch = [
        pltpu.VMEM((slots, piece, width), BF16),
        pltpu.SemaphoreType.DMA,
        pltpu.SemaphoreType.DMA((7, GATHER_PARTS)),
        pltpu.SemaphoreType.DMA((7, GATHER_PARTS)),
    ]
    result = communicate(
        "plane_gather", functools.partial(gather_steps, split, prepare), list(sources), earlier, (out, ANY), scratch,
        matmuls, 40 if matmuls else 16, [WHOLE] * len(sources), movers,
    )
    got = result[0].reshape(-1, width)
    return (got, *result[1:]) if matmuls or movers else got


def scatter_steps(split, forms, finish, n_sources, meet, *refs):
    n = len(forms)
    hbm, refs = refs[: 2 * n], refs[2 * n :]
    sources, refs = refs[:n_sources], refs[n_sources:]
    o_ref, refs = refs[0], refs[1:]
    held, refs = refs[: 2 * n], refs[2 * n :]
    own, put_c, got_c, put_x, put_y, got_x, got_y, fin_x, fin_y, end_x, end_y, load_sem, send_sem, recv_sem = refs
    x, c, y, to_x, to_y, to_c = flips()
    parts, _, _, step, width = own.shape
    slots = o_ref.shape[0]
    per_slot = parts // slots
    half = width // 2
    left, right = pl.ds(0, half), pl.ds(half, half)
    loads = [pltpu.make_async_copy(of, to, load_sem.at[i]) for i, (of, to) in enumerate(zip(hbm, held))]
    for load in loads:
        load.start()
    meet(to_x, to_y, to_c)
    for load in loads:
        load.wait()

    def rows_of(i):
        return i // per_slot, pl.ds(i % per_slot * step, step)

    def partial_sums(pc, i, columns):
        slot, rows = rows_of(i)
        total = None
        for form, a, b in zip(forms, held[::2], held[1::2]):
            if split == 2:
                block = a[:, slot, pc, :, rows, :]
            else:
                block = a[slot, pc, :, :, rows, :]
            block = block.reshape(4 * step, block.shape[-1])
            term = dot_nn(block, b[:, columns]) if form == "nn" else dot_nt(block, b[columns, :])
            total = term if total is None else total + term
        return total.astype(BF16).reshape(2, 2, step, half)

    def send(kind, i, src, dst, target):
        copy = pltpu.make_async_remote_copy(
            src_ref=src.at[i], dst_ref=dst.at[i], send_sem=send_sem.at[kind, i], recv_sem=recv_sem.at[kind, i],
            device_id=target, device_id_type=MESH,
        )
        copy.start()
        return copy

    def f32(ref, *index):
        return ref[index].astype(F32)

    first, second, third = [], [], []

    def along_first_axis(i):
        first[i].wait_recv()
        for j in range(2):
            put_x[i, j] = (f32(own, i, 1 - x, j, slice(None), left) + f32(got_c, i, 1 - x, j, slice(None), left)).astype(BF16)
            put_y[i, j] = (f32(own, i, j, 1 - y, slice(None), right) + f32(got_c, i, j, 1 - y, slice(None), right)).astype(BF16)
        second.append((send(1, i, put_x, got_x, to_x), send(2, i, put_y, got_y, to_y)))

    for i in range(parts):
        for columns in (left, right):
            put_c[i, :, :, :, columns] = partial_sums(1 - c, i, columns)
        first.append(send(0, i, put_c, got_c, to_c))
        for columns in (left, right):
            own[i, :, :, :, columns] = partial_sums(c, i, columns)
        if i:
            along_first_axis(i - 1)
    along_first_axis(parts - 1)
    yield
    yield
    for i in range(parts):
        for copy in second[i]:
            copy.wait_recv()
        fin_y[i] = (
            f32(own, i, x, 1 - y, slice(None), left) + f32(got_c, i, x, 1 - y, slice(None), left) + f32(got_x, i, 1 - y)
        ).astype(BF16)
        fin_x[i] = (
            f32(own, i, 1 - x, y, slice(None), right) + f32(got_c, i, 1 - x, y, slice(None), right) + f32(got_y, i, 1 - x)
        ).astype(BF16)
        third.append((send(3, i, fin_y, end_y, to_y), send(4, i, fin_x, end_x, to_x)))
        yield
        yield
    for i in range(parts):
        for copy in third[i]:
            copy.wait_recv()
        slot, rows = rows_of(i)
        total = jnp.concatenate(
            [
                f32(own, i, x, y, slice(None), left) + f32(got_c, i, x, y, slice(None), left)
                + f32(got_x, i, y) + f32(end_y, i),
                f32(own, i, x, y, slice(None), right) + f32(got_c, i, x, y, slice(None), right)
                + f32(got_y, i, x) + f32(end_x, i),
            ],
            -1,
        )
        o_ref[slot, rows, :] = finish(total, *(source[slot, rows, :] for source in sources)).astype(o_ref.dtype)
        yield
    for i in range(parts):
        for copy in (first[i], *second[i], *third[i]):
            copy.wait_send()


def plane_scatter(products, sources, finish, dtype, split, slots, *earlier, matmuls=(), movers=()):
    forms = [form for form, _, _ in products]
    _, a, b = products[0]
    rows, width = a.shape[0] // 8, (b.shape[1] if forms[0] == "nn" else b.shape[0])
    piece = rows // slots
    n = SCATTER_PARTS
    step, half = rows // n, width // 2
    operands = []
    for _, a, b in products:
        operands += [a.reshape(plane_shape(split, slots, piece, a.shape[1])), b]
    whole, two, one = (
        pltpu.VMEM((n, 2, 2, step, width), BF16),
        pltpu.VMEM((n, 2, step, half), BF16),
        pltpu.VMEM((n, step, half), BF16),
    )
    scratch = [pltpu.VMEM(t.shape, t.dtype) for t in operands]
    scratch += [whole] * 3 + [two] * 4 + [one] * 4
    scratch += [
        pltpu.SemaphoreType.DMA((len(operands),)),
        pltpu.SemaphoreType.DMA((5, n)),
        pltpu.SemaphoreType.DMA((5, n)),
    ]
    out = jax.ShapeDtypeStruct((slots, piece, width), dtype)
    result = communicate(
        "plane_scatter", functools.partial(scatter_steps, split, forms, finish, len(sources)),
        operands + list(sources), earlier, (out, WHOLE), scratch, matmuls, 62,
        [ANY] * len(operands) + [WHOLE] * len(sources), movers,
    )
    return result if matmuls or movers else result[0]


def pair_kernel(a_ref, *refs):
    o_ref, own_sem, send_sem, recv_sem = refs[-4:]
    c = lax.axis_index("core")
    greet({"core": 1 - c})
    keep = pltpu.make_async_copy(a_ref, o_ref.at[c], own_sem)
    keep.start()
    copy = pltpu.make_async_remote_copy(
        src_ref=a_ref, dst_ref=o_ref.at[c], send_sem=send_sem, recv_sem=recv_sem,
        device_id={"core": 1 - c}, device_id_type=MESH,
    )
    copy.start()
    keep.wait()
    copy.wait()


def core_gather(a, *earlier):
    return pl.pallas_call(
        pair_kernel,
        out_shape=jax.ShapeDtypeStruct((2, *a.shape), a.dtype),
        in_specs=[WHOLE] + [ANY] * len(earlier),
        out_specs=ANY,
        scratch_shapes=[pltpu.SemaphoreType.DMA] * 3,
        compiler_params=pltpu.CompilerParams(
            collective_id=fresh(), has_side_effects=True, vmem_limit_bytes=32 << 20
        ),
        cost_estimate=light(),
        name="core_gather",
    )(a, *earlier)


def others():
    x, c, y, *_ = flips()
    out = []
    for dx, dc, dy in ((1, 0, 1), (1, 1, 1), (1, 0, 0), (0, 0, 1), (1, 1, 0), (0, 1, 1), (0, 1, 0)):
        px, pc, py = (1 - x if dx else x), (1 - c if dc else c), (1 - y if dy else y)
        out.append(((px * 2 + pc) * 2 + py, {"x": px, "core": pc, "y": py}))
    return (x * 2 + c) * 2 + y, out


class TokenMoves:
    def __init__(self, tokens, split, back=False):
        self.split, self.back, self.operands = split, back, [tokens]
        self.out = [jax.ShapeDtypeStruct(tokens.shape, tokens.dtype)]
        self.specs = self.out_specs = [ANY]
        self.scratch = [pltpu.SemaphoreType.DMA((tokens.shape[0],))] * 2

    def places(self):
        ms = self.out[0].shape[0]
        x, c, z, y, _ = own_place()
        if self.split == 2:
            slot = group = z // 2
            to = [at_place(x, z % 2, 2 * j + c, y) for j in range(ms)]
            of = [at_place(x, z % 2, 2 * k + c, y) for k in range(ms)]
        else:
            slot = group = z // 4
            to = [at_place(z % 2, z // 2 % 2, (2 * j + x) * 2 + c, y) for j in range(ms)]
            of = [at_place(z // 2 % 2, z % 2, 4 * k + 2 * c + x, y) for k in range(ms)]
        return (group, of, to) if self.back else (slot, to, of)

    def party(self):
        _, to, of = self.places()
        return of, remotes(to)

    def begin(self, ins, outs, held):
        (t_ref,), (o_ref,), (send_sem, recv_sem) = ins, outs, held
        slot, to, _ = self.places()
        yield
        waits = [
            send_or_keep(t_ref.at[j], o_ref.at[slot], send_sem.at[j], recv_sem.at[slot], *place)
            for j, place in enumerate(to)
        ]
        yield
        for k in range(len(to)):
            pltpu.make_async_copy(t_ref.at[0], o_ref.at[k], recv_sem.at[k]).wait()
        for wait in waits:
            wait()


def head_device(h, z):
    return at_place(h // 4, h % 2, z, h // 2 % 2)


def head_owner(h, k):
    nz = lax.axis_size("z")
    rest = h % 2 * nz + k
    return at_place(h // 4, h // 2 % 2, rest // 2, rest % 2)


class HeadRows:
    def __init__(self, w, inward):
        rows, width = w.shape
        self.nz, self.inward, self.operands = lax.axis_size("z"), inward, [w]
        self.out = [jax.ShapeDtypeStruct((self.nz * rows, width), BF16)]
        self.specs, self.out_specs = [WHOLE], [ANY]
        self.scratch = [pltpu.VMEM((rows, width), BF16)] + [pltpu.SemaphoreType.DMA((self.nz,))] * 2

    def places(self):
        x, c, z, y, me = own_place()
        targets = [head_device(me // self.nz, t) for t in range(self.nz)]
        return targets, [head_owner(4 * x + 2 * y + c, k) for k in range(self.nz)], me % self.nz

    def party(self):
        targets, sources, _ = self.places()
        return sources, remotes(targets)

    def begin(self, ins, outs, held):
        (w_ref,), (o_ref,), (turned, send_sem, recv_sem) = ins, outs, held
        rows = turned.shape[0]
        targets, _, k = self.places()
        turned[...] = self.inward(w_ref[...])
        yield
        to = o_ref.at[pl.ds(pl.multiple_of(k * rows, rows), rows), :]
        waits = [send_or_keep(turned, to, send_sem.at[t], recv_sem.at[k], *place) for t, place in enumerate(targets)]
        yield
        for j in range(self.nz):
            pltpu.make_async_copy(turned, o_ref.at[pl.ds(j * rows, rows), :], recv_sem.at[j]).wait()
        for wait in waits:
            wait()


class HeadSums:
    def __init__(self, d):
        self.nz, self.operands = lax.axis_size("z"), [d]
        rows, width = d.shape[0] // self.nz, d.shape[1]
        self.out = [jax.ShapeDtypeStruct((rows, width), F32)]
        self.specs, self.out_specs = [ANY], [WHOLE]
        self.scratch = [pltpu.VMEM((self.nz, rows, width), BF16)] + [pltpu.SemaphoreType.DMA((self.nz,))] * 2

    def places(self):
        x, c, z, y, me = own_place()
        targets = [head_owner(4 * x + 2 * y + c, k) for k in range(self.nz)]
        return targets, [head_device(me // self.nz, t) for t in range(self.nz)], z

    def party(self):
        targets, sources, _ = self.places()
        return sources, remotes(targets)

    def begin(self, ins, outs, held):
        (d_ref,), (o_ref,), (got, send_sem, recv_sem) = ins, outs, held
        rows = got.shape[1]
        targets, _, z = self.places()
        yield
        waits = [
            send_or_keep(d_ref.at[pl.ds(k * rows, rows), :], got.at[z], send_sem.at[k], recv_sem.at[z], *place)
            for k, place in enumerate(targets)
        ]
        yield
        total = None
        for t in range(self.nz):
            pltpu.make_async_copy(d_ref.at[pl.ds(0, rows), :], got.at[t], recv_sem.at[t]).wait()
            total = got[t].astype(F32) if total is None else total + got[t].astype(F32)
        o_ref[...] = total
        for wait in waits:
            wait()


def head_columns(px, pc, py):
    return tuple(pl.ds(pl.multiple_of(h * HEAD_DIM, HEAD_DIM), HEAD_DIM) for h in (4 * px + 2 * py + pc, 2 * px + py))


class Columns:
    def __init__(self, weights, gain=None):
        rows = weights[0].shape[0]
        self.heads, self.scaled = len(weights) == 3, gain is not None
        cols = 2 * HEAD_DIM if self.heads else weights[0].shape[1] // 8
        self.operands = list(weights) + ([gain] if self.scaled else [])
        self.out = [jax.ShapeDtypeStruct((8 * rows, cols), BF16)]
        self.specs, self.out_specs = [ANY] * len(self.operands), [ANY]
        self.scratch = [
            pltpu.VMEM((8, rows, cols), BF16),
            pltpu.SemaphoreType.DMA,
            pltpu.SemaphoreType.DMA((7,)),
            pltpu.SemaphoreType.DMA((7,)),
        ]
        if self.scaled:
            self.scratch += [pltpu.VMEM(t.shape, t.dtype) for t in self.operands]
            self.scratch.append(pltpu.SemaphoreType.DMA((len(self.operands),)))

    def begin(self, ins, outs, held):
        (o_ref,), (scaled, own_sem, send_sem, recv_sem, *loaded) = outs, held
        _, rows, cols = scaled.shape
        me, peers = others()
        x, c, y, *_ = flips()
        to = o_ref.at[pl.ds(pl.multiple_of(me * rows, rows), rows), :]
        loads = [pltpu.make_async_copy(of, to_, loaded[-1].at[i]) for i, (of, to_) in enumerate(zip(ins, loaded[:-1]))]
        for load in loads:
            load.start()

        def piece(p, px, pc, py):
            if self.heads:
                wq, wk, wv, gain = loaded[:-1]
                q_cols, kv_cols = head_columns(px, pc, py)
                scaled[p, :, :HEAD_DIM] = (wq[:, q_cols].astype(F32) * gain[...]).astype(BF16)
                for_kv = jnp.where(pc == 0, wk[:, kv_cols].astype(F32), wv[:, kv_cols].astype(F32))
                scaled[p, :, HEAD_DIM:] = (for_kv * gain[...]).astype(BF16)
                return scaled.at[p]
            columns = pl.ds(pl.multiple_of(p * cols, cols), cols)
            if self.scaled:
                scaled[p] = (loaded[0][:, columns].astype(F32) * loaded[1][...]).astype(BF16)
                return scaled.at[p]
            return ins[0].at[:, columns]

        yield
        for load in loads:
            load.wait()
        copies = []
        for kind, (p, target) in enumerate(peers):
            copy = pltpu.make_async_remote_copy(
                src_ref=piece(p, target["x"], target["core"], target["y"]), dst_ref=to,
                send_sem=send_sem.at[kind], recv_sem=recv_sem.at[kind], device_id=target, device_id_type=MESH,
            )
            copy.start()
            copies.append(copy)
        keep = pltpu.make_async_copy(piece(me, x, c, y), to, own_sem)
        keep.start()
        yield
        keep.wait()
        for copy in copies:
            copy.wait()


class Segments:
    def __init__(self, seg):
        self.operands, self.out = [seg], [jax.ShapeDtypeStruct((8, *seg.shape), seg.dtype)]
        self.specs, self.out_specs = [WHOLE], [ANY]
        self.scratch = [pltpu.SemaphoreType.DMA, pltpu.SemaphoreType.DMA((7,)), pltpu.SemaphoreType.DMA((7,))]

    def begin(self, ins, outs, held):
        (seg_ref,), (o_ref,), (own_sem, send_sem, recv_sem) = ins, outs, held
        me, peers = others()
        yield
        copies = []
        for kind, (_, target) in enumerate(peers):
            copy = pltpu.make_async_remote_copy(
                src_ref=seg_ref, dst_ref=o_ref.at[me], send_sem=send_sem.at[kind], recv_sem=recv_sem.at[kind],
                device_id=target, device_id_type=MESH,
            )
            copy.start()
            copies.append(copy)
        keep = pltpu.make_async_copy(seg_ref, o_ref.at[me], own_sem)
        keep.start()
        yield
        keep.wait()
        for copy in copies:
            copy.wait()


def exchange(name, items, *earlier, movers=()):
    parts = [*movers, *items]

    def kernel(*refs):
        refs = list(refs)
        ins = [[refs.pop(0) for _ in part.operands] for part in parts]
        refs = refs[len(earlier) :]
        outs = [[refs.pop(0) for _ in part.out] for part in parts]
        held = [[refs.pop(0) for _ in part.scratch] for part in parts]
        running = [part.begin(*given) for part, *given in zip(parts, ins, outs, held)]
        for part in running:
            next(part)
        targets = [(target, None) for _, target in others()[1]]
        join([(targets, len(targets))] + [mover.party() for mover in movers])
        for part in running:
            next(part)
        for part in running:
            next(part, None)

    result = pl.pallas_call(
        kernel,
        out_shape=[o for part in parts for o in part.out],
        in_specs=[spec for part in parts for spec in part.specs] + [ANY] * len(earlier),
        out_specs=[spec for part in parts for spec in part.out_specs],
        scratch_shapes=[t for part in parts for t in part.scratch],
        compiler_params=pltpu.CompilerParams(
            collective_id=fresh(), has_side_effects=True, vmem_limit_bytes=62 << 20
        ),
        cost_estimate=light(),
        name=name,
    )(*[a for part in parts for a in part.operands], *earlier)
    return result


class Rows:
    def __init__(self, part):
        self.cols, rows = part.shape[1], part.shape[0] // 8
        self.operands, self.specs = [part], [ANY]
        self.out, self.out_specs = [jax.ShapeDtypeStruct((rows, 8 * self.cols), BF16)], [ANY]
        self.scratch = [pltpu.SemaphoreType.DMA, pltpu.SemaphoreType.DMA((7,)), pltpu.SemaphoreType.DMA((7,))]

    def begin(self, ins, outs, held):
        (p_ref,), (o_ref,), (own_sem, send_sem, recv_sem) = ins, outs, held
        rows = o_ref.shape[0]
        me, peers = others()
        to = o_ref.at[:, pl.ds(pl.multiple_of(me * self.cols, self.cols), self.cols)]

        def block(p):
            return p_ref.at[pl.ds(pl.multiple_of(p * rows, rows), rows), :]

        yield
        copies = []
        for kind, (p, target) in enumerate(peers):
            copy = pltpu.make_async_remote_copy(
                src_ref=block(p), dst_ref=to, send_sem=send_sem.at[kind], recv_sem=recv_sem.at[kind],
                device_id=target, device_id_type=MESH,
            )
            copy.start()
            copies.append(copy)
        keep = pltpu.make_async_copy(block(me), to, own_sem)
        keep.start()
        yield
        keep.wait()
        for copy in copies:
            copy.wait()


class HeadGradients:
    def __init__(self, part, widths):
        rows = part.shape[0] // 8
        self.operands, self.specs = [part], [ANY]
        self.out = [jax.ShapeDtypeStruct((rows, n), BF16) for n in widths]
        self.out_specs = [ANY] * 3
        self.scratch = [pltpu.SemaphoreType.DMA((2,)), pltpu.SemaphoreType.DMA((14,)), pltpu.SemaphoreType.DMA((14,))]

    def begin(self, ins, outs, held):
        (p_ref,), (q_out, k_out, v_out), (own_sem, send_sem, recv_sem) = ins, outs, held
        rows = q_out.shape[0]
        me, peers = others()
        x, c, y, *_ = flips()
        q_cols, kv_cols = head_columns(x, c, y)
        halves = pl.ds(0, HEAD_DIM), pl.ds(HEAD_DIM, HEAD_DIM)

        def block(p, half):
            return p_ref.at[pl.ds(pl.multiple_of(p * rows, rows), rows), halves[half]]

        def away(kind, half, to):
            p, target = peers[kind]
            return pltpu.make_async_remote_copy(
                src_ref=block(p, half), dst_ref=to,
                send_sem=send_sem.at[2 * kind + half], recv_sem=recv_sem.at[2 * kind + half],
                device_id=target, device_id_type=MESH,
            )

        q_to, k_to, v_to = q_out.at[:, q_cols], k_out.at[:, kv_cols], v_out.at[:, kv_cols]
        yield
        for kind in range(7):
            away(kind, 0, q_to).start()
            pl.when(c == 0)(lambda: away(kind, 1, k_to).start())
            pl.when(c == 1)(lambda: away(kind, 1, v_to).start())
        pltpu.make_async_copy(block(me, 0), q_to, own_sem.at[0]).start()
        pl.when(c == 0)(lambda: pltpu.make_async_copy(block(me, 1), k_to, own_sem.at[1]).start())
        pl.when(c == 1)(lambda: pltpu.make_async_copy(block(me, 1), v_to, own_sem.at[1]).start())
        yield
        for half in range(2):
            pltpu.make_async_copy(block(me, half), q_to, own_sem.at[half]).wait()
        for kind in range(7):
            for half in range(2):
                away(kind, half, q_to).wait()


class AttentionBackward:
    def __init__(self, da, w_out, q, kv, qseg, kseg, cosine, sine):
        seqs, seq_len, hd = q.shape
        self.operands = [da.reshape(seqs, seq_len, -1), w_out, q, kv, qseg, kseg, cosine, sine]
        self.specs = [ANY] * 4 + [WHOLE] * 2 + [ANY] * 2
        self.out = [jax.ShapeDtypeStruct((seqs, seq_len, 2 * hd), BF16)]
        self.out_specs = [WHOLE]
        self.loaded = (1, 2, 3, 6, 7)
        self.scratch = [pltpu.VMEM(self.operands[i].shape, self.operands[i].dtype) for i in self.loaded]
        self.scratch += [
            pltpu.SemaphoreType.DMA((len(self.loaded),)),
            pltpu.VMEM(self.operands[0].shape, BF16),
            pltpu.VMEM((seq_len, hd), F32),
            pltpu.VMEM((seq_len, hd), F32),
            pltpu.VMEM((2, seqs, seq_len, hd), BF16),
            pltpu.VMEM((seqs, seq_len, hd), BF16),
            pltpu.SemaphoreType.DMA((seqs,)),
            pltpu.SemaphoreType.DMA((seqs,)),
            pltpu.SemaphoreType.DMA((seqs,)),
        ]

    def begin(self, ins, outs, held):
        n = len(self.loaded)
        w_out, q_ref, kv_ref, cos_ref, sin_ref = copied = held[:n]
        da, dk_sum, dv_sum, dkv, got, da_sem, send_sem, recv_sem = held[n + 1 :]
        qseg_ref, kseg_ref = ins[4:6]
        (o_ref,) = outs
        c = lax.axis_index("core")
        seqs, seq_len, hd = q_ref.shape
        first_loads = [pltpu.make_async_copy(ins[i], copied[j], held[n].at[j]) for j, i in enumerate(self.loaded)]
        loads = [pltpu.make_async_copy(ins[0].at[s], da.at[s], da_sem.at[s]) for s in range(seqs)]
        for load in first_loads + loads:
            load.start()
        yield
        yield
        for load in first_loads:
            load.wait()
        copies = []
        for s, load in enumerate(loads):
            load.wait()
            dk_sum[...] = jnp.zeros_like(dk_sum)
            dv_sum[...] = jnp.zeros_like(dv_sum)
            for first, low, end in query_blocks(seq_len):
                rows, keys = pl.ds(first, QUERY_ROWS), pl.ds(low, end - low)
                q, k, v = q_ref[s, rows, :], kv_ref[0, s, keys, :], kv_ref[1, s, keys, :]
                do = dot_nt(da[s, rows, :], w_out[...]).astype(BF16)
                prob = masked_prob(q, k, first, low, qseg_ref[s, rows, :], kseg_ref[s, :, keys])
                dprob = dot_nt(do, v)
                ds = prob * (dprob - jnp.sum(prob * dprob, -1, keepdims=True))
                dsb = ds.astype(BF16)
                dq = dot_nn(dsb, k) * SCALE
                o_ref[s, rows, :hd] = rotate(dq, cos_ref[rows, :], -sin_ref[rows, :]).astype(BF16)
                dk_sum[keys, :] += dot_tn(dsb, q)
                dv_sum[keys, :] += dot_tn(prob.astype(BF16), do)
            dkv[0, s] = (dk_sum[...] * SCALE).astype(BF16)
            dkv[1, s] = dv_sum[...].astype(BF16)
            copy = pltpu.make_async_remote_copy(
                src_ref=dkv.at[1 - c, s], dst_ref=got.at[s], send_sem=send_sem.at[s], recv_sem=recv_sem.at[s],
                device_id={"core": 1 - c}, device_id_type=MESH,
            )
            copy.start()
            copies.append(copy)
        for s, copy in enumerate(copies):
            copy.wait_recv()
            total = dkv[c, s].astype(F32) + got[s].astype(F32)
            turned = rotate(total, cos_ref[...], -sin_ref[...])
            o_ref[s, :, hd:] = jnp.where(c == 0, turned, total).astype(BF16)
        for copy in copies:
            copy.wait_send()


def tie_kernel(a_ref, *refs):
    pass


def tie(a, *earlier):
    return pl.pallas_call(
        tie_kernel,
        out_shape=jax.ShapeDtypeStruct(a.shape, a.dtype),
        in_specs=[ANY] * (1 + len(earlier)),
        out_specs=ANY,
        input_output_aliases={0: 0},
        cost_estimate=light(),
        name="tie",
    )(a, *earlier)


def along_z(part):
    return lax.all_gather(part, "z", axis=0, tiled=True)


def sum_along_z(g):
    return lax.psum_scatter(g, "z", scatter_dimension=0, tiled=True)


def shards(
    tokens,
    segments,
    attn_gain,
    query_weight,
    key_weight,
    value_weight,
    out_weight,
    ffn_gain,
    gate_weight,
    up_weight,
    down_weight,
    cotangent,
):
    NUMBERS[0] = 0
    micro, seq_local, pl_len, width = tokens.shape
    seq_len = segments.shape[2]
    ms = micro * seq_local
    rows_w = gate_weight.shape[0]
    nx, nc, nz, ny = (lax.axis_size(a) for a in EVERY)
    dp = nx * nc
    n_plane = 8 * ms * pl_len
    col_block = width // (dp * nz)
    z_index = lax.axis_index("z")
    core = lax.axis_index("core")
    split = dp * ms // nz

    def perm(a):
        lead = a.shape[:-1]
        return a.reshape(*lead, dp, nz, col_block).swapaxes(-3, -2).reshape(*lead, width)

    def unperm(a):
        lead = a.shape[:-1]
        return a.reshape(*lead, nz, dp, col_block).swapaxes(-3, -2).reshape(*lead, width)

    whole_lanes = col_block % 128 == 0

    def inward(v):
        return reorder(v, dp, nz) if whole_lanes else v

    def outward(v):
        return reorder(v, nz, dp) if whole_lanes else v

    def inside(a):
        return a if whole_lanes else perm(a)

    def outside(a):
        return a if whole_lanes else unperm(a)

    def scale_of(v):
        return lax.rsqrt(jnp.mean(v * v, -1, keepdims=True) + NORM_EPS)

    def norm_back(v, d_hat):
        scale = scale_of(v)
        hat = v * scale
        return scale * (d_hat - hat * jnp.mean(d_hat * hat, -1, keepdims=True))

    def pick(a, index):
        return lax.dynamic_index_in_dim(a, index, 0, keepdims=False)

    g1 = attn_gain.astype(F32)[:, None]
    g2 = ffn_gain.astype(F32)[:, None]

    wqkv = (query_weight, key_weight, value_weight)
    x, wqkv_part, gate_part, seg_all = exchange(
        "weight_columns",
        [Columns(wqkv, g1), Columns([gate_weight], g2), Segments(segments.reshape(ms, seq_len))],
        movers=[TokenMoves(tokens.reshape(ms, pl_len, width), split)],
    )
    w_qkv = along_z(wqkv_part)

    seg_all = seg_all.reshape(2, 2, 2, ms, seq_len)[:, :, 0]
    if split == 2:
        seg = pick(pick(seg_all.swapaxes(0, 1), z_index % 2).swapaxes(0, 1), z_index // 2)
    else:
        seg = pick(pick(pick(seg_all, z_index // 2 % 2), z_index % 2), z_index // 4)[None]
    qseg, kseg = seg[:, :, None], seg[:, None, :]

    x = inside(x)

    def norm_in(v):
        v = inward(v.astype(F32))
        return v * scale_of(v)

    xa, w_out = plane_gather([x], norm_in, split, wqkv_part, movers=[HeadRows(inside(out_weight), inward)])

    inv_freq = 1.0 / ROPE_BASE ** (jnp.arange(0, HEAD_DIM, 2, dtype=F32) / HEAD_DIM)
    angles = jnp.arange(seq_len, dtype=jnp.int32).astype(F32)[:, None] * inv_freq[None, :]
    cosine, sine = jnp.cos(angles), jnp.sin(angles)
    cos_q, sin_q = (jnp.tile(t, (split, 1)) for t in (cosine, sine))
    cos_k = jnp.where(core == 0, cos_q, 1.0)
    sin_k = jnp.where(core == 0, sin_q, 0.0)

    qkv = dot_nn(xa, w_qkv)
    qb = rotate(qkv[:, :HEAD_DIM], cos_q, sin_q).astype(BF16).reshape(split, seq_len, HEAD_DIM)
    kvb = rotate(qkv[:, HEAD_DIM:], cos_k, sin_k).astype(BF16)
    kv_all = core_gather(kvb).reshape(2, split, seq_len, HEAD_DIM)

    w_gate = along_z(gate_part)
    ob = attn_forward(qb, kv_all, qseg, kseg).reshape(n_plane, HEAD_DIM)
    (down_part,) = exchange("weight_columns", [Columns([down_weight])], ob)
    w_down = along_z(down_part)
    h, cot = plane_scatter(
        [("nn", ob, w_out)], [x], lambda total, v: inward(v.astype(F32)) + total, F32, split, ms, down_part,
        movers=[TokenMoves(cotangent.reshape(ms, pl_len, width), split)],
    )
    cot = inside(cot)

    ha = plane_gather([h], lambda v: v * scale_of(v), split)
    (up_part,) = exchange("weight_columns", [Columns([up_weight], g2)], ha)
    w_up = along_z(up_part)
    ca, gate = plane_gather([cot], inward, split, up_part, matmuls=[Matmul("nn", ha, w_gate, F32)])
    sig = jax.nn.sigmoid(gate)
    silu = gate * sig
    d_mid = dot_nn(ca, w_down)
    dub = (d_mid * silu).astype(BF16)
    d_up = dot_tn(ha, dub).astype(BF16)
    w_up = tie(w_up, d_up)
    up = dot_nn(ha, w_up)
    dgb = (d_mid * up * sig * (1.0 + gate * (1.0 - sig))).astype(BF16)
    mid = (silu * up).astype(BF16)
    dh, d_gate = plane_scatter(
        [("nt", dgb, w_gate), ("nt", dub, w_up)],
        [h, cot],
        lambda total, v, dy: inward(dy.astype(F32)) + norm_back(v, total),
        F32, split, ms, matmuls=[Matmul("tn", ha, dgb)],
    )
    up_z = sum_along_z(d_up)
    gate_z = sum_along_z(d_gate)
    da, d_down = plane_gather([dh], lambda v: v, split, matmuls=[Matmul("tn", ca, mid)])

    down_z = sum_along_z(d_down)
    output = plane_scatter(
        [("nt", mid, w_down)], [h], lambda total, v: outward(v + total), BF16, split, ms, d_down
    )

    up_rows, dqkv = exchange(
        "attention_backward",
        [Rows(up_z), AttentionBackward(da, w_out, qb, kv_all, qseg, kseg, cosine, sine)],
        output,
    )
    dqkv = dqkv.reshape(n_plane, 2 * HEAD_DIM)
    input_grad, d_qkv, d_out, output = plane_scatter(
        [("nt", dqkv, w_qkv)],
        [x, dh],
        lambda total, v, direct: outward(direct + norm_back(inward(v.astype(F32)), total)),
        BF16, split, ms, gate_z, matmuls=[Matmul("tn", xa, dqkv), Matmul("tn", ob, da)],
        movers=[TokenMoves(outside(output), split, True)],
    )
    qkv_z = sum_along_z(d_qkv)
    input_grad, gate_rows, down_rows = exchange(
        "weight_rows", [Rows(gate_z), Rows(down_z)], d_qkv, movers=[TokenMoves(outside(input_grad), split, True)]
    )
    output = output.reshape(tokens.shape)
    input_grad = input_grad.astype(F32).reshape(tokens.shape)
    up_rows, gate_rows, down_back = (t.astype(F32) for t in (up_rows, gate_rows, down_rows))
    ffn_gain_term = jnp.sum(up_rows * up_weight.astype(F32) + gate_rows * gate_weight.astype(F32), -1)
    up_back, gate_back = up_rows * g2, gate_rows * g2
    out_back, *qkv_rows = exchange(
        "weight_rows", [HeadGradients(qkv_z, [w.shape[1] for w in wqkv])],
        up_back, gate_back, down_back, input_grad, ffn_gain_term,
        movers=[HeadSums(d_out)],
    )
    out_back = unperm(out_back)
    qkv_rows = [t.astype(F32) for t in qkv_rows]
    attn_gain_term = sum(jnp.sum(w.astype(F32) * g, -1) for w, g in zip(wqkv, qkv_rows))
    q_back, k_back, v_back = (t * g1 for t in qkv_rows)

    return (
        output,
        input_grad,
        attn_gain_term,
        q_back,
        k_back,
        v_back,
        out_back,
        ffn_gain_term,
        gate_back,
        up_back,
        down_back,
    )


def solution(mesh):
    dp, seq = mesh.shape["dp"], mesh.shape["seq"]
    fine = Mesh(mesh.devices.reshape(dp // 2, 2, seq // 2, 2), EVERY)
    dp_axes, seq_axes = ("x", "core"), ("z", "y")
    tok = P(None, dp_axes, seq_axes, None)
    vec, mat = P(EVERY), P(EVERY, None)
    return jax.shard_map(
        shards,
        mesh=fine,
        in_specs=(tok, P(None, dp_axes, None), vec, mat, mat, mat, mat, vec, mat, mat, mat, tok),
        out_specs=(tok, tok, vec, mat, mat, mat, mat, vec, mat, mat, mat),
        check_vma=False,
    )
```

time: 786 us -> 745 us (0.948)
  local copies, waits for them, and re-layouts: 64.6 us -> 31.4 us
  Pallas kernels: 555 us -> 568 us
    unnamed x107 -> x61, local copies, waits for them, and re-layouts: 59.6 us -> 26.2 us
    reduce_scatter x5 -> x4, waiting for transfers between devices: 15.4 us -> 0.68 us  [sum_along_z(): return lax.psum_scatter(g, 'z', scatter_dimension=0, tiled=True)]
    pallas_call x17 -> x14, Pallas kernels: 548 us -> 561 us  [the longest x8 385 us: communicate(): pl.pallas_call(kernel, out_shape=[shape] + [m.out for m in matmuls] + mov...]
    all_gather x5 -> x4, waiting for transfers between devices: 37.4 us -> 45 us  [along_z(): return lax.all_gather(part, 'z', axis=0, tiled=True)]
  transfers between devices with their start and end apart: 12 -> 8, of which waited for: 2 -> 3; matrix products, arithmetic and copies ran while one was open for 11% -> 10% of each run, Pallas kernels for 67% -> 68%
where the time goes in v4:
time: 745 us; the launch traced here: 738 us
  Pallas kernels  568 us (76%)
  matrix products  58.5 us (8%)
  waiting for transfers between devices  46.5 us (6%)
  local copies, waits for them, and re-layouts  31.4 us (4%)
  other arithmetic  17.2 us (2%)
  between operations  15.2 us (2%)
    pallas_call x8, Pallas kernels, communicate(): pl.pallas_call(kernel, out_shape=[shape] + [m.out for m in matmuls] + mov...  385 us
    pallas_call x6, Pallas kernels, exchange(): pl.pallas_call(kernel, out_shape=[o for part in parts for o in part.out],...  176 us
    dot_general x3, matrix products, dot_nn(): lax.dot_general(a, b, (((1,), (0,)), ((), ())), preferred_element_type=F32)  45.2 us
    all_gather x4, waiting for transfers between devices, along_z(): return lax.all_gather(part, 'z', axis=0, tiled=True)  45 us
    unnamed x61, local copies, waits for them, and re-layouts  26.2 us
  transfers between devices with their start and end apart: 8, of which 3 were waited for; matrix products, arithmetic and copies ran while one was open for 10% of the time, Pallas kernels for 68%

profile of v4, /device:TPU:29, one launch (start us, length us, event | category | flops | bytes accessed | tf_op | source)
XLA Modules:
  0.0 737.6 jit_solution(8260541387126963927)
XLA Ops:
  11.3 27.3 %weight_columns.3 = (bf16[2,128,2048]{2,1,0:T(8,128)(2,1)}, bf16[512,512]{1,0:T(8,128)(2,1)}, bf16[512,1024]{1,0:T(8,128)(2,1)}, s32[8,2,1024]{2,1,0:T(2,128)}) custom-call(bf16[2,128,2048]{2,1,0:T(8,128)(2,1)} %bitcast.112, bf16[64,2048]{1,0:T(8,128)(2,1)} %refs_1_.2, bf16[64,1024]{1,0:T(8,128)(2,1)} %refs_2_.1, bf16[64,1024]{1,0:T(8,128)(2,1)} %refs_3_.1, ...), custom_call_target="tpu_custom_call" | custom-call | bytes 1024 | tf_op jit(solution)/shard_map/weight_columns/pallas_call | solution.py:755
  43.3 48.8 %plane_gather.4 = (bf16[2,2,2,2,128,2048]{5,4,3,2,1,0:T(8,128)(2,1)S(1)}, bf16[256,2048]{1,0:T(8,128)(2,1)S(1)}) custom-call(bf16[2,128,2048]{2,1,0:T(8,128)(2,1)S(1)} %copy-done.8, bf16[64,2048]{1,0:T(8,128)(2,1)S(1)} %copy-done.16, bf16[512,512]{1,0:T(8,128)(2,1)S(1)} %copy-done.15), custom_call_target="tpu_custom_call" | custom-call | bytes 1024 | tf_op jit(solution)/shard_map/plane_gather/pallas_call | solution.py:270
  92.1 3.3 copy-done.12
  96.4 1.9 multiply_cosine_fusion
  98.3 5.7 all-gather.5.cloned.1.call-done.refs_1_
  104.0 7.5 %fusion.20 = f32[2048,512]{1,0:T(8,128)S(1)} fusion(bf16[2048,2048]{1,0:T(8,128)(2,1)} %bitcast.97, bf16[2048,512]{1,0:T(8,128)(2,1)} %all-gather.5.cloned.1.call-done.refs_1_), kind=kOutput, calls=%fused_computation.54 | convolution fusion | flops 4294967296 | bytes 14680064 | tf_op jit(solution)/shard_map/dot_general | solution.py:30
  112.3 2.9 core_gather.1
  115.4 4.5 attention_forward.1
  120.9 16.8 %weight_columns.4.refs_4_ = bf16[512,1024]{1,0:T(8,128)(2,1)} custom-call(bf16[64,8192]{1,0:T(8,128)(2,1)} %refs_0_.2, bf16[2048,256]{1,0:T(8,128)(2,1)} %bitcast.93), custom_call_target="tpu_custom_call" | custom-call | bytes 1024 | tf_op jit(solution)/shard_map/weight_columns/pallas_call | solution.py:755
  137.8 56.7 %plane_scatter.4 = (f32[2,128,2048]{2,1,0:T(8,128)}, bf16[2,128,2048]{2,1,0:T(8,128)(2,1)}) custom-call(bf16[2,2,2,2,128,256]{5,4,3,2,1,0:T(8,128)(2,1)} %bitcast.94, bf16[256,2048]{1,0:T(8,128)(2,1)} %copy-done.14, bf16[2,128,2048]{2,1,0:T(8,128)(2,1)} %get-tuple-element.38.refs_0_.refs_2_, bf16[2,128,2048]{2,1,0:T(8,128)(2,1)} %bitcast.110, ...), custom_call_target="tpu_custom_call" | custom-call | bytes 1024 | tf_op jit(solution)/shard_map/plane_scatter/pallas_call | solution.py:270
  196.0 38.1 %plane_gather.5 = bf16[2,2,2,2,128,2048]{5,4,3,2,1,0:T(8,128)(2,1)S(1)} custom-call(f32[2,128,2048]{2,1,0:T(8,128)S(1)} %copy-done.2), custom_call_target="tpu_custom_call" | custom-call | bytes 1024 | tf_op jit(solution)/shard_map/plane_gather/pallas_call | solution.py:270
  234.2 3.3 copy-done
  237.5 15.2 %weight_columns.5.refs_3_ = bf16[512,1024]{1,0:T(8,128)(2,1)} custom-call(bf16[64,8192]{1,0:T(8,128)(2,1)} %refs_0_.3, f32[64,1]{1,0:T(8,128)} %copy.31.refs_6_.refs_1_, bf16[2048,2048]{1,0:T(8,128)(2,1)} %bitcast.85), custom_call_target="tpu_custom_call" | custom-call | bytes 1024 | tf_op jit(solution)/shard_map/weight_columns/pallas_call | solution.py:755
  253.0 2.2 copy-done.6
  256.5 39.3 %plane_gather.6 = (bf16[2,2,2,2,128,2048]{5,4,3,2,1,0:T(8,128)(2,1)}, f32[2048,1024]{1,0:T(8,128)}) custom-call(bf16[2,128,2048]{2,1,0:T(8,128)(2,1)S(1)} %copy-done.13, bf16[2048,2048]{1,0:T(8,128)(2,1)} %bitcast.86, bf16[2048,1024]{1,0:T(8,128)(2,1)S(1)} %copy-done.6, bf16[512,1024]{1,0:T(8,128)(2,1)S(1)} %copy-done.7), custom_call_target="tpu_custom_call" | custom-call | bytes 1024 | tf_op jit(solution)/shard_map/plane_gather/pallas_call | solution.py:270
  295.7 17.2 %multiply_convert_fusion.2 = (bf16[2048,1024]{1,0:T(8,128)(2,1)S(1)}, f32[2048,1024]{1,0:T(8,128)}) fusion(f32[2048,1024]{1,0:T(8,128)} %get-tuple-element.47, bf16[2048,2048]{1,0:T(8,128)(2,1)} %bitcast.104, bf16[2048,1024]{1,0:T(8,128)(2,1)} %all-gather.9.cloned.1.call-done.refs_1_), kind=kOutput, calls=%fused_computation.2 | convolution fusion | flops 8602517504 | bytes 33554432 | tf_op jit(solution)/shard_map/dot_general | solution.py:30
  312.9 2.0 copy-done.21
  314.9 13.3 %convolution_convert_fusion.refs_0_ = bf16[2048,1024]{1,0:T(8,128)(2,1)} fusion(bf16[2048,2048]{1,0:T(8,128)(2,1)} %bitcast.87, bf16[2048,1024]{1,0:T(8,128)(2,1)S(1)} %get-tuple-element.110), kind=kOutput, calls=%fused_computation.5 | convolution fusion | flops 8592031744 | bytes 16777216 | tf_op jit(solution)/shard_map/dot_general | solution.py:38
  328.3 39.4 %all-gather.11.cloned.1.call-done.a_ref = bf16[2048,1024]{1,0:T(8,128)(2,1)} async-done(((bf16[512,1024]{1,0:T(8,128)(2,1)}), bf16[2048,1024]{1,0:T(8,128)(2,1)}) %all-gather.11.cloned.1.call-update) | async-done | bytes 4194320 | tf_op jit(solution)/shard_map/all_gather | solution.py:935
  367.6 20.5 %multiply_convert_fusion = (bf16[2048,1024]{1,0:T(8,128)(2,1)}, bf16[2048,1024]{1,0:T(8,128)(2,1)}) fusion(f32[2048,1024]{1,0:T(8,128)} %get-tuple-element.47, f32[2048,1024]{1,0:T(8,128)} %get-tuple-element.111, bf16[2048,2048]{1,0:T(8,128)(2,1)} %bitcast.88, bf16[2048,1024]{1,0:T(8,128)(2,1)} %tie.1.refs_3_), kind=kOutput, calls=%fused_computation | convolution fusion | flops 8617197568 | bytes 37748736 | tf_op jit(solution)/shard_map/dot_general | solution.py:30
  388.1 58.6 %plane_scatter.5 = (f32[2,128,2048]{2,1,0:T(8,128)}, bf16[2048,1024]{1,0:T(8,128)(2,1)}) custom-call(bf16[2,2,2,2,128,1024]{5,4,3,2,1,0:T(8,128)(2,1)} %bitcast.101, bf16[2048,1024]{1,0:T(8,128)(2,1)} %all-gather.7.cloned.1.call-done.refs_2_.refs_1_, bf16[2,2,2,2,128,1024]{5,4,3,2,1,0:T(8,128)(2,1)} %bitcast.106, bf16[2048,1024]{1,0:T(8,128)(2,1)} %tie.1.refs_3_, ...), custom_call_target="tpu_custom_call" | custom-call | bytes 1024 | tf_op jit(solution)/shard_map/plane_scatter/pallas_call | solution.py:270
  448.4 2.2 copy-done.4
  450.5 39.3 %plane_gather.7 = (bf16[2,2,2,2,128,2048]{5,4,3,2,1,0:T(8,128)(2,1)}, bf16[2048,1024]{1,0:T(8,128)(2,1)S(1)}) custom-call(f32[2,128,2048]{2,1,0:T(8,128)S(1)} %copy-done.11, bf16[2048,2048]{1,0:T(8,128)(2,1)} %bitcast.105, bf16[2048,1024]{1,0:T(8,128)(2,1)S(1)} %copy-done.4), custom_call_target="tpu_custom_call" | custom-call | bytes 1024 | tf_op jit(solution)/shard_map/plane_gather/pallas_call | solution.py:270
  489.8 2.0 copy-done.5
  492.0 47.7 %plane_scatter.6.refs_9_.refs_4_ = bf16[2,128,2048]{2,1,0:T(8,128)(2,1)} custom-call(bf16[2,2,2,2,128,1024]{5,4,3,2,1,0:T(8,128)(2,1)} %bitcast.96, bf16[2048,1024]{1,0:T(8,128)(2,1)} %all-gather.9.cloned.1.call-done.refs_1_, f32[2,128,2048]{2,1,0:T(8,128)} %get-tuple-element.43.refs_0_.refs_4_.refs_2_, bf16[2048,1024]{1,0:T(8,128)(2,1)} %copy-done.5), custom_call_target="tpu_custom_call" | custom-call | bytes 1024 | tf_op jit(solution)/shard_map/plane_scatter/pallas_call | solution.py:270
  539.7 29.7 %attention_backward.1 = (bf16[64,8192]{1,0:T(8,128)(2,1)}, bf16[2,1024,512]{2,1,0:T(8,128)(2,1)}) custom-call(bf16[512,1024]{1,0:T(8,128)(2,1)} %reduce-scatter.5.cloned.1.call-done.refs_0_, bf16[2,1024,2048]{2,1,0:T(8,128)(2,1)} %bitcast.99, bf16[256,2048]{1,0:T(8,128)(2,1)} %copy-done.14, bf16[2,1024,256]{2,1,0:T(8,128)(2,1)} %copy-done.10, ...), custom_call_target="tpu_custom_call" | custom-call | bytes 1024 | tf_op jit(solution)/shard_map/attention_backward/pallas_call | solution.py:755
  569.5 56.5 %plane_scatter.7 = (bf16[2,128,2048]{2,1,0:T(8,128)(2,1)}, bf16[2048,512]{1,0:T(8,128)(2,1)}, bf16[256,2048]{1,0:T(8,128)(2,1)}, bf16[2,128,2048]{2,1,0:T(8,128)(2,1)}) custom-call(bf16[2,2,2,2,128,512]{5,4,3,2,1,0:T(8,128)(2,1)} %bitcast.102, bf16[2048,512]{1,0:T(8,128)(2,1)} %all-gather.5.cloned.1.call-done.refs_1_, ...), custom_call_target="tpu_custom_call" | custom-call | bytes 1024 | tf_op jit(solution)/shard_map/plane_scatter/pallas_call | solution.py:270
  626.0 49.1 %weight_rows.2 = (bf16[2,128,2048]{2,1,0:T(8,128)(2,1)}, bf16[64,8192]{1,0:T(8,128)(2,1)}, bf16[64,8192]{1,0:T(8,128)(2,1)}) custom-call(bf16[2,128,2048]{2,1,0:T(8,128)(2,1)} %get-tuple-element.54.refs_0_, bf16[512,1024]{1,0:T(8,128)(2,1)} %reduce-scatter.7.cloned.1.call-done.refs_9_.refs_1_, bf16[512,1024]{1,0:T(8,128)(2,1)} %reduce-scatter.9.cloned.1.call-done.refs_2_, ...), custom_call_target="tpu_custom_call" | custom-call | bytes 1024 | tf_op jit(solution)/shard_map/weight_rows/pallas_call | solution.py:755
  675.1 2.7 convert_element_type.86.refs_4_
  677.8 5.3 fusion.2
  685.3 37.8 %weight_rows.3 = (f32[64,2048]{1,0:T(8,128)}, bf16[64,2048]{1,0:T(8,128)(2,1)}, bf16[64,1024]{1,0:T(8,128)(2,1)}, bf16[64,1024]{1,0:T(8,128)(2,1)}) custom-call(bf16[256,2048]{1,0:T(8,128)(2,1)} %get-tuple-element.57.refs_0_, bf16[512,512]{1,0:T(8,128)(2,1)} %reduce-scatter.11.cloned.1.call-done.refs_1_, f32[64,8192]{1,0:T(8,128)} %get-tuple-element.132.refs_2_, ...), custom_call_target="tpu_custom_call" | custom-call | bytes 1024 | tf_op jit(solution)/shard_map/weight_rows/pallas_call | solution.py:755
  725.8 2.0 convert_multiply_fusion.4
  (97 shorter events, 24.1 us)
Async XLA Ops:
  7.2 33.5 %copy-start.16 = (bf16[64,2048]{1,0:T(8,128)(2,1)S(1)}, bf16[64,2048]{1,0:T(8,128)(2,1)}, u32[]{:S(2)}) copy-start(bf16[64,2048]{1,0:T(8,128)(2,1)} %refs_1_.3) | copy-start | bytes 786436
  7.2 96.8 %all-gather.5.cloned.1.call-start = ((), (), s32[]{:S(2)}) async-start(), calls=%async_computation.4 | async-start | bytes 2621440 | tf_op jit(solution)/shard_map/all_gather | solution.py:935
  38.7 214.3 %all-gather.7.cloned.1.call-start = ((), (), s32[]{:S(2)}) async-start(), calls=%async_computation.5 | async-start | bytes 5242880 | tf_op jit(solution)/shard_map/all_gather | solution.py:935
  39.4 256.3 %all-gather.9.cloned.1.call-start = ((), (), s32[]{:S(2)}) async-start(), calls=%async_computation.6 | async-start | bytes 5242880 | tf_op jit(solution)/shard_map/all_gather | solution.py:935
  40.7 74.7 %copy-start.9 = (s32[2,1024,1]{2,1,0:T(8,128)}, s32[2,1024,1]{2,1,0:T(8,128)S(1)}, u32[]{:S(2)}) copy-start(s32[2,1024,1]{2,1,0:T(8,128)S(1)} %copy.33.qseg_ref.refs_5_) | copy-start | bytes 24580
  40.7 1.6 copy-start.8
  92.1 3.3 copy-start.12
  96.4 19.0 %copy-start.17 = (s32[2,1,1024]{2,1,0:T(1,128)}, s32[2,1,1024]{2,1,0:T(1,128)S(1)}, u32[]{:S(2)}) copy-start(s32[2,1,1024]{2,1,0:T(1,128)S(1)} %fusion.29.kseg_ref.refs_6_) | copy-start | bytes 24580
  98.3 13.2 %copy-start.18 = (f32[1024,128]{1,0:T(8,128)}, f32[1024,128]{1,0:T(8,128)S(1)}, u32[]{:S(2)}) copy-start(f32[1024,128]{1,0:T(8,128)S(1)} %get-tuple-element.102.refs_7_) | copy-start | bytes 1572868
  98.3 13.2 %copy-start.19 = (f32[1024,128]{1,0:T(8,128)}, f32[1024,128]{1,0:T(8,128)S(1)}, u32[]{:S(2)}) copy-start(f32[1024,128]{1,0:T(8,128)S(1)} %get-tuple-element.103.refs_8_) | copy-start | bytes 1572868
  115.2 4.7 copy-start.1
  115.3 4.6 copy-start.10
  137.7 229.9 %all-gather.11.cloned.1.call-start = ((), (), s32[]{:S(2)}) async-start(), calls=%async_computation.8 | async-start | bytes 5242880 | tf_op jit(solution)/shard_map/all_gather | solution.py:935
  234.2 3.3 copy-start
  237.5 15.5 %copy-start.13 = (bf16[2,128,2048]{2,1,0:T(8,128)(2,1)S(1)}, bf16[2,128,2048]{2,1,0:T(8,128)(2,1)}, u32[]{:S(2)}) copy-start(bf16[2,128,2048]{2,1,0:T(8,128)(2,1)} %get-tuple-element.44.refs_0_.refs_5_) | copy-start | bytes 3145732
  252.7 287.1 %reduce-scatter.5.cloned.1.call-start = ((), (), s32[]{:S(2)}) async-start(), calls=%async_computation.7 | async-start | bytes 5242880 | tf_op jit(solution)/shard_map/reduce_scatter | solution.py:939
  253.0 2.2 copy-start.6
  312.9 2.0 copy-start.21
  328.2 241.2 %reduce-scatter.7.cloned.1.call-start = ((), (), s32[]{:S(2)}) async-start(), calls=%async_computation.9 | async-start | bytes 5242880 | tf_op jit(solution)/shard_map/reduce_scatter | solution.py:939
  446.8 1.6 copy-start.11
  446.8 179.2 %reduce-scatter.9.cloned.1.call-start = ((), (), s32[]{:S(2)}) async-start(), calls=%async_computation.10 | async-start | bytes 5242880 | tf_op jit(solution)/shard_map/reduce_scatter | solution.py:939
  448.4 2.2 copy-start.4
  489.8 2.0 copy-start.5
  491.8 193.5 %reduce-scatter.11.cloned.1.call-start = ((), (), s32[]{:S(2)}) async-start(), calls=%async_computation.11 | async-start | bytes 2621440 | tf_op jit(solution)/shard_map/reduce_scatter | solution.py:939
  626.0 51.8 %copy-start.20 = (bf16[64,8192]{1,0:T(8,128)(2,1)S(1)}, bf16[64,8192]{1,0:T(8,128)(2,1)}, u32[]{:S(2)}) copy-start(bf16[64,8192]{1,0:T(8,128)(2,1)} %refs_0_.3) | copy-start | bytes 3145732
  677.8 5.3 copy-start.22
  685.3 40.5 %copy-start.24 = (bf16[64,2048]{1,0:T(8,128)(2,1)S(1)}, bf16[64,2048]{1,0:T(8,128)(2,1)}, u32[]{:S(2)}) copy-start(bf16[64,2048]{1,0:T(8,128)(2,1)} %refs_1_.2) | copy-start | bytes 786436
  723.1 4.7 copy-start.25
  723.1 4.7 copy-start.26
  723.1 4.7 copy-start.27
  723.1 4.7 copy-start.28
  723.1 6.2 copy-start.23
  (5 other events, 5.8 us)
Sparse Core Ops, SparseCore 0:
  38.8 65.1 all-gather.4
  105.5 100.4 all-gather.6
  207.6 79.1 all-gather.8
  288.3 79.2 all-gather.10
  369.7 77.0 reduce-scatter.4
  449.1 77.2 reduce-scatter.6
  528.8 93.9 reduce-scatter.8
  626.1 59.1 reduce-scatter.10

commit v5 on v4

--- a/solution.py
+++ b/solution.py
@@ -1003,9 +1003,9 @@
     g2 = ffn_gain.astype(F32)[:, None]
 
     wqkv = (query_weight, key_weight, value_weight)
-    x, wqkv_part, gate_part, seg_all = exchange(
-        "weight_columns",
-        [Columns(wqkv, g1), Columns([gate_weight], g2), Segments(segments.reshape(ms, seq_len))],
+    (wqkv_part,) = exchange("weight_columns", [Columns(wqkv, g1)])
+    x, gate_part, seg_all = exchange(
+        "weight_columns", [Columns([gate_weight], g2), Segments(segments.reshape(ms, seq_len))], wqkv_part,
         movers=[TokenMoves(tokens.reshape(ms, pl_len, width), split)],
     )
     w_qkv = along_z(wqkv_part)

time: 745 us -> 728 us (0.977)
  waiting for transfers between devices: 46.5 us -> 8.8 us
  Pallas kernels: 568 us -> 590 us
    all_gather x4, waiting for transfers between devices: 45 us -> 7.93 us  [along_z(): return lax.all_gather(part, 'z', axis=0, tiled=True)]
    pallas_call x6 -> x7, Pallas kernels: 176 us -> 209 us  [exchange(): pl.pallas_call(kernel, out_shape=[o for part in parts for o in part.out],...]
    pallas_call x8, Pallas kernels: 385 us -> 374 us  [communicate(): pl.pallas_call(kernel, out_shape=[shape] + [m.out for m in matmuls] + mov...]
  transfers between devices with their start and end apart: 8 -> 8, of which waited for: 3 -> 2; matrix products, arithmetic and copies ran while one was open for 10% -> 10% of each run, Pallas kernels for 68% -> 75%
where the time goes in v5:
time: 728 us; the launch traced here: 720 us
  Pallas kernels  590 us (81%)
  matrix products  58 us (8%)
  local copies, waits for them, and re-layouts  30.4 us (4%)
  other arithmetic  17.2 us (2%)
  between operations  15.2 us (2%)
  waiting for transfers between devices  8.8 us (1%)
    pallas_call x8, Pallas kernels, communicate(): pl.pallas_call(kernel, out_shape=[shape] + [m.out for m in matmuls] + mov...  374 us
    pallas_call x7, Pallas kernels, exchange(): pl.pallas_call(kernel, out_shape=[o for part in parts for o in part.out],...  209 us
    dot_general x3, matrix products, dot_nn(): lax.dot_general(a, b, (((1,), (0,)), ((), ())), preferred_element_type=F32)  44.7 us
    unnamed x61, local copies, waits for them, and re-layouts  25.1 us
  transfers between devices with their start and end apart: 8, of which 2 were waited for; matrix products, arithmetic and copies ran while one was open for 10% of the time, Pallas kernels for 75%

profile of v5, /device:TPU:29, one launch (start us, length us, event | category | flops | bytes accessed | tf_op | source)
XLA Modules:
  0.0 720.2 jit_solution(15517907944869361111)
XLA Ops:
  8.6 10.2 %weight_columns.4.refs_4_.refs_2_ = bf16[512,512]{1,0:T(8,128)(2,1)} custom-call(bf16[64,2048]{1,0:T(8,128)(2,1)} %refs_0_.3, bf16[64,1024]{1,0:T(8,128)(2,1)} %refs_1_.3, bf16[64,1024]{1,0:T(8,128)(2,1)} %refs_2_.1, f32[64,1]{1,0:T(8,128)} %copy.30.refs_3_), custom_call_target="tpu_custom_call" | custom-call | bytes 1024 | tf_op jit(solution)/shard_map/weight_columns/pallas_call | solution.py:755
  21.6 50.6 %weight_columns.5 = (bf16[2,128,2048]{2,1,0:T(8,128)(2,1)}, bf16[512,1024]{1,0:T(8,128)(2,1)}, s32[8,2,1024]{2,1,0:T(2,128)}) custom-call(bf16[2,128,2048]{2,1,0:T(8,128)(2,1)} %bitcast.112, bf16[64,8192]{1,0:T(8,128)(2,1)} %refs_1_.4, f32[64,1]{1,0:T(8,128)} %copy.31.refs_2_.refs_1_, s32[2,1024]{1,0:T(2,128)} %bitcast.113, ...), custom_call_target="tpu_custom_call" | custom-call | bytes 1024 | tf_op jit(solution)/shard_map/weight_columns/pallas_call | solution.py:755
  75.2 49.7 %plane_gather.4 = (bf16[2,2,2,2,128,2048]{5,4,3,2,1,0:T(8,128)(2,1)S(1)}, bf16[256,2048]{1,0:T(8,128)(2,1)S(1)}) custom-call(bf16[2,128,2048]{2,1,0:T(8,128)(2,1)S(1)} %copy-done.8, bf16[64,2048]{1,0:T(8,128)(2,1)S(1)} %copy-done.16, bf16[512,512]{1,0:T(8,128)(2,1)S(1)} %copy-done.13), custom_call_target="tpu_custom_call" | custom-call | bytes 1024 | tf_op jit(solution)/shard_map/plane_gather/pallas_call | solution.py:270
  124.9 3.3 copy-done.12
  129.2 1.9 multiply_cosine_fusion
  131.1 7.9 %fusion.20 = f32[2048,512]{1,0:T(8,128)S(1)} fusion(bf16[2048,2048]{1,0:T(8,128)(2,1)} %bitcast.97, bf16[2048,512]{1,0:T(8,128)(2,1)} %all-gather.5.cloned.1.call-done.refs_1_), kind=kOutput, calls=%fused_computation.54 | convolution fusion | flops 4294967296 | bytes 14680064 | tf_op jit(solution)/shard_map/dot_general | solution.py:30
  139.8 2.8 core_gather.1
  142.8 4.5 attention_forward.1
  148.4 16.5 %weight_columns.6.refs_4_ = bf16[512,1024]{1,0:T(8,128)(2,1)} custom-call(bf16[64,8192]{1,0:T(8,128)(2,1)} %refs_0_.4, bf16[2048,256]{1,0:T(8,128)(2,1)} %bitcast.93), custom_call_target="tpu_custom_call" | custom-call | bytes 1024 | tf_op jit(solution)/shard_map/weight_columns/pallas_call | solution.py:755
  164.9 44.1 %plane_scatter.4 = (f32[2,128,2048]{2,1,0:T(8,128)}, bf16[2,128,2048]{2,1,0:T(8,128)(2,1)}) custom-call(bf16[2,2,2,2,128,256]{5,4,3,2,1,0:T(8,128)(2,1)} %bitcast.94, bf16[256,2048]{1,0:T(8,128)(2,1)} %copy-done.15, bf16[2,128,2048]{2,1,0:T(8,128)(2,1)} %get-tuple-element.37.refs_0_.refs_2_, bf16[2,128,2048]{2,1,0:T(8,128)(2,1)} %bitcast.110, ...), custom_call_target="tpu_custom_call" | custom-call | bytes 1024 | tf_op jit(solution)/shard_map/plane_scatter/pallas_call | solution.py:270
  210.7 38.5 %plane_gather.5 = bf16[2,2,2,2,128,2048]{5,4,3,2,1,0:T(8,128)(2,1)S(1)} custom-call(f32[2,128,2048]{2,1,0:T(8,128)S(1)} %copy-done.2), custom_call_target="tpu_custom_call" | custom-call | bytes 1024 | tf_op jit(solution)/shard_map/plane_gather/pallas_call | solution.py:270
  249.2 3.3 copy-done
  252.5 15.0 %weight_columns.7.refs_3_ = bf16[512,1024]{1,0:T(8,128)(2,1)} custom-call(bf16[64,8192]{1,0:T(8,128)(2,1)} %refs_0_.5, f32[64,1]{1,0:T(8,128)} %copy.31.refs_2_.refs_1_, bf16[2048,2048]{1,0:T(8,128)(2,1)} %bitcast.85), custom_call_target="tpu_custom_call" | custom-call | bytes 1024 | tf_op jit(solution)/shard_map/weight_columns/pallas_call | solution.py:755
  267.9 2.2 copy-done.6
  271.3 39.3 %plane_gather.6 = (bf16[2,2,2,2,128,2048]{5,4,3,2,1,0:T(8,128)(2,1)}, f32[2048,1024]{1,0:T(8,128)}) custom-call(bf16[2,128,2048]{2,1,0:T(8,128)(2,1)S(1)} %copy-done.14, bf16[2048,2048]{1,0:T(8,128)(2,1)} %bitcast.86, bf16[2048,1024]{1,0:T(8,128)(2,1)S(1)} %copy-done.6, bf16[512,1024]{1,0:T(8,128)(2,1)S(1)} %copy-done.7), custom_call_target="tpu_custom_call" | custom-call | bytes 1024 | tf_op jit(solution)/shard_map/plane_gather/pallas_call | solution.py:270
  310.6 16.3 %multiply_convert_fusion.2 = (bf16[2048,1024]{1,0:T(8,128)(2,1)S(1)}, f32[2048,1024]{1,0:T(8,128)}) fusion(f32[2048,1024]{1,0:T(8,128)} %get-tuple-element.45, bf16[2048,2048]{1,0:T(8,128)(2,1)} %bitcast.104, bf16[2048,1024]{1,0:T(8,128)(2,1)} %all-gather.9.cloned.1.call-done.refs_1_), kind=kOutput, calls=%fused_computation.2 | convolution fusion | flops 8602517504 | bytes 33554432 | tf_op jit(solution)/shard_map/dot_general | solution.py:30
  326.9 2.0 copy-done.21
  328.9 13.3 %convolution_convert_fusion.refs_0_ = bf16[2048,1024]{1,0:T(8,128)(2,1)} fusion(bf16[2048,2048]{1,0:T(8,128)(2,1)} %bitcast.87, bf16[2048,1024]{1,0:T(8,128)(2,1)S(1)} %get-tuple-element.108), kind=kOutput, calls=%fused_computation.5 | convolution fusion | flops 8592031744 | bytes 16777216 | tf_op jit(solution)/shard_map/dot_general | solution.py:38
  342.3 7.9 %all-gather.11.cloned.1.call-done.a_ref = bf16[2048,1024]{1,0:T(8,128)(2,1)} async-done(((bf16[512,1024]{1,0:T(8,128)(2,1)}), bf16[2048,1024]{1,0:T(8,128)(2,1)}) %all-gather.11.cloned.1.call-update) | async-done | bytes 4194320 | tf_op jit(solution)/shard_map/all_gather | solution.py:935
  350.1 20.5 %multiply_convert_fusion = (bf16[2048,1024]{1,0:T(8,128)(2,1)}, bf16[2048,1024]{1,0:T(8,128)(2,1)}) fusion(f32[2048,1024]{1,0:T(8,128)} %get-tuple-element.45, f32[2048,1024]{1,0:T(8,128)} %get-tuple-element.109, bf16[2048,2048]{1,0:T(8,128)(2,1)} %bitcast.88, bf16[2048,1024]{1,0:T(8,128)(2,1)} %tie.1.refs_3_), kind=kOutput, calls=%fused_computation | convolution fusion | flops 8617197568 | bytes 37748736 | tf_op jit(solution)/shard_map/dot_general | solution.py:30
  370.6 58.6 %plane_scatter.5 = (f32[2,128,2048]{2,1,0:T(8,128)}, bf16[2048,1024]{1,0:T(8,128)(2,1)}) custom-call(bf16[2,2,2,2,128,1024]{5,4,3,2,1,0:T(8,128)(2,1)} %bitcast.101, bf16[2048,1024]{1,0:T(8,128)(2,1)} %all-gather.7.cloned.1.call-done.refs_2_.refs_1_, bf16[2,2,2,2,128,1024]{5,4,3,2,1,0:T(8,128)(2,1)} %bitcast.106, bf16[2048,1024]{1,0:T(8,128)(2,1)} %tie.1.refs_3_, ...), custom_call_target="tpu_custom_call" | custom-call | bytes 1024 | tf_op jit(solution)/shard_map/plane_scatter/pallas_call | solution.py:270
  430.8 2.2 copy-done.4
  433.0 39.3 %plane_gather.7 = (bf16[2,2,2,2,128,2048]{5,4,3,2,1,0:T(8,128)(2,1)}, bf16[2048,1024]{1,0:T(8,128)(2,1)S(1)}) custom-call(f32[2,128,2048]{2,1,0:T(8,128)S(1)} %copy-done.11, bf16[2048,2048]{1,0:T(8,128)(2,1)} %bitcast.105, bf16[2048,1024]{1,0:T(8,128)(2,1)S(1)} %copy-done.4), custom_call_target="tpu_custom_call" | custom-call | bytes 1024 | tf_op jit(solution)/shard_map/plane_gather/pallas_call | solution.py:270
  472.3 2.0 copy-done.5
  474.5 47.6 %plane_scatter.6.refs_9_.refs_4_ = bf16[2,128,2048]{2,1,0:T(8,128)(2,1)} custom-call(bf16[2,2,2,2,128,1024]{5,4,3,2,1,0:T(8,128)(2,1)} %bitcast.96, bf16[2048,1024]{1,0:T(8,128)(2,1)} %all-gather.9.cloned.1.call-done.refs_1_, f32[2,128,2048]{2,1,0:T(8,128)} %get-tuple-element.41.refs_0_.refs_4_.refs_2_, bf16[2048,1024]{1,0:T(8,128)(2,1)} %copy-done.5), custom_call_target="tpu_custom_call" | custom-call | bytes 1024 | tf_op jit(solution)/shard_map/plane_scatter/pallas_call | solution.py:270
  522.2 29.7 %attention_backward.1 = (bf16[64,8192]{1,0:T(8,128)(2,1)}, bf16[2,1024,512]{2,1,0:T(8,128)(2,1)}) custom-call(bf16[512,1024]{1,0:T(8,128)(2,1)} %reduce-scatter.5.cloned.1.call-done.refs_0_, bf16[2,1024,2048]{2,1,0:T(8,128)(2,1)} %bitcast.99, bf16[256,2048]{1,0:T(8,128)(2,1)} %copy-done.15, bf16[2,1024,256]{2,1,0:T(8,128)(2,1)} %copy-done.10, ...), custom_call_target="tpu_custom_call" | custom-call | bytes 1024 | tf_op jit(solution)/shard_map/attention_backward/pallas_call | solution.py:755
  552.0 56.5 %plane_scatter.7 = (bf16[2,128,2048]{2,1,0:T(8,128)(2,1)}, bf16[2048,512]{1,0:T(8,128)(2,1)}, bf16[256,2048]{1,0:T(8,128)(2,1)}, bf16[2,128,2048]{2,1,0:T(8,128)(2,1)}) custom-call(bf16[2,2,2,2,128,512]{5,4,3,2,1,0:T(8,128)(2,1)} %bitcast.102, bf16[2048,512]{1,0:T(8,128)(2,1)} %all-gather.5.cloned.1.call-done.refs_1_, ...), custom_call_target="tpu_custom_call" | custom-call | bytes 1024 | tf_op jit(solution)/shard_map/plane_scatter/pallas_call | solution.py:270
  608.6 49.1 %weight_rows.2 = (bf16[2,128,2048]{2,1,0:T(8,128)(2,1)}, bf16[64,8192]{1,0:T(8,128)(2,1)}, bf16[64,8192]{1,0:T(8,128)(2,1)}) custom-call(bf16[2,128,2048]{2,1,0:T(8,128)(2,1)} %get-tuple-element.52.refs_0_, bf16[512,1024]{1,0:T(8,128)(2,1)} %reduce-scatter.7.cloned.1.call-done.refs_9_.refs_1_, bf16[512,1024]{1,0:T(8,128)(2,1)} %reduce-scatter.9.cloned.1.call-done.refs_2_, ...), custom_call_target="tpu_custom_call" | custom-call | bytes 1024 | tf_op jit(solution)/shard_map/weight_rows/pallas_call | solution.py:755
  657.7 2.7 convert_element_type.86.refs_4_
  660.3 5.3 fusion.2
  667.9 37.7 %weight_rows.3 = (f32[64,2048]{1,0:T(8,128)}, bf16[64,2048]{1,0:T(8,128)(2,1)}, bf16[64,1024]{1,0:T(8,128)(2,1)}, bf16[64,1024]{1,0:T(8,128)(2,1)}) custom-call(bf16[256,2048]{1,0:T(8,128)(2,1)} %get-tuple-element.55.refs_0_, bf16[512,512]{1,0:T(8,128)(2,1)} %reduce-scatter.11.cloned.1.call-done.refs_1_, f32[64,8192]{1,0:T(8,128)} %get-tuple-element.130.refs_2_, ...), custom_call_target="tpu_custom_call" | custom-call | bytes 1024 | tf_op jit(solution)/shard_map/weight_rows/pallas_call | solution.py:755
  708.3 2.0 convert_multiply_fusion.4
  (98 shorter events, 22.5 us)
Async XLA Ops:
  7.2 66.4 %copy-start.16 = (bf16[64,2048]{1,0:T(8,128)(2,1)S(1)}, bf16[64,2048]{1,0:T(8,128)(2,1)}, u32[]{:S(2)}) copy-start(bf16[64,2048]{1,0:T(8,128)(2,1)} %refs_1_.5) | copy-start | bytes 786436
  7.2 123.9 %all-gather.5.cloned.1.call-start = ((), (), s32[]{:S(2)}) async-start(), calls=%async_computation.4 | async-start | bytes 2621440 | tf_op jit(solution)/shard_map/all_gather | solution.py:935
  18.8 54.7 %copy-start.13 = (bf16[512,512]{1,0:T(8,128)(2,1)S(1)}, bf16[512,512]{1,0:T(8,128)(2,1)}, u32[]{:S(2)}) copy-start(bf16[512,512]{1,0:T(8,128)(2,1)} %weight_columns.4.refs_4_.refs_2_) | copy-start | bytes 1572868
  18.9 249.0 %all-gather.7.cloned.1.call-start = ((), (), s32[]{:S(2)}) async-start(), calls=%async_computation.5 | async-start | bytes 5242880 | tf_op jit(solution)/shard_map/all_gather | solution.py:935
  72.3 238.3 %all-gather.9.cloned.1.call-start = ((), (), s32[]{:S(2)}) async-start(), calls=%async_computation.6 | async-start | bytes 5242880 | tf_op jit(solution)/shard_map/all_gather | solution.py:935
  73.5 69.3 %copy-start.9 = (s32[2,1024,1]{2,1,0:T(8,128)}, s32[2,1024,1]{2,1,0:T(8,128)S(1)}, u32[]{:S(2)}) copy-start(s32[2,1024,1]{2,1,0:T(8,128)S(1)} %copy.33.qseg_ref.refs_5_) | copy-start | bytes 24580
  73.5 1.6 copy-start.8
  124.9 3.3 copy-start.12
  129.2 13.7 %copy-start.17 = (s32[2,1,1024]{2,1,0:T(1,128)}, s32[2,1,1024]{2,1,0:T(1,128)S(1)}, u32[]{:S(2)}) copy-start(s32[2,1,1024]{2,1,0:T(1,128)S(1)} %fusion.29.kseg_ref.refs_6_) | copy-start | bytes 24580
  131.1 8.0 %copy-start.18 = (f32[1024,128]{1,0:T(8,128)}, f32[1024,128]{1,0:T(8,128)S(1)}, u32[]{:S(2)}) copy-start(f32[1024,128]{1,0:T(8,128)S(1)} %get-tuple-element.100.refs_7_) | copy-start | bytes 1572868
  131.1 8.0 %copy-start.19 = (f32[1024,128]{1,0:T(8,128)}, f32[1024,128]{1,0:T(8,128)S(1)}, u32[]{:S(2)}) copy-start(f32[1024,128]{1,0:T(8,128)S(1)} %get-tuple-element.101.refs_8_) | copy-start | bytes 1572868
  142.7 4.7 copy-start.1
  142.8 4.6 copy-start.10
  164.9 185.2 %all-gather.11.cloned.1.call-start = ((), (), s32[]{:S(2)}) async-start(), calls=%async_computation.8 | async-start | bytes 5242880 | tf_op jit(solution)/shard_map/all_gather | solution.py:935
  249.2 3.3 copy-start
  252.5 15.4 %copy-start.14 = (bf16[2,128,2048]{2,1,0:T(8,128)(2,1)S(1)}, bf16[2,128,2048]{2,1,0:T(8,128)(2,1)}, u32[]{:S(2)}) copy-start(bf16[2,128,2048]{2,1,0:T(8,128)(2,1)} %get-tuple-element.42.refs_0_.refs_5_) | copy-start | bytes 3145732
  267.6 254.7 %reduce-scatter.5.cloned.1.call-start = ((), (), s32[]{:S(2)}) async-start(), calls=%async_computation.7 | async-start | bytes 5242880 | tf_op jit(solution)/shard_map/reduce_scatter | solution.py:939
  267.9 2.2 copy-start.6
  326.9 2.0 copy-start.21
  342.2 209.7 %reduce-scatter.7.cloned.1.call-start = ((), (), s32[]{:S(2)}) async-start(), calls=%async_computation.9 | async-start | bytes 5242880 | tf_op jit(solution)/shard_map/reduce_scatter | solution.py:939
  429.3 179.2 %reduce-scatter.9.cloned.1.call-start = ((), (), s32[]{:S(2)}) async-start(), calls=%async_computation.10 | async-start | bytes 5242880 | tf_op jit(solution)/shard_map/reduce_scatter | solution.py:939
  430.8 2.2 copy-start.4
  472.3 2.0 copy-start.5
  474.3 193.6 %reduce-scatter.11.cloned.1.call-start = ((), (), s32[]{:S(2)}) async-start(), calls=%async_computation.11 | async-start | bytes 2621440 | tf_op jit(solution)/shard_map/reduce_scatter | solution.py:939
  608.5 51.8 %copy-start.20 = (bf16[64,8192]{1,0:T(8,128)(2,1)S(1)}, bf16[64,8192]{1,0:T(8,128)(2,1)}, u32[]{:S(2)}) copy-start(bf16[64,8192]{1,0:T(8,128)(2,1)} %refs_0_.5) | copy-start | bytes 3145732
  660.3 5.3 copy-start.22
  667.9 40.4 %copy-start.24 = (bf16[64,2048]{1,0:T(8,128)(2,1)S(1)}, bf16[64,2048]{1,0:T(8,128)(2,1)}, u32[]{:S(2)}) copy-start(bf16[64,2048]{1,0:T(8,128)(2,1)} %refs_0_.3) | copy-start | bytes 786436
  705.6 4.7 copy-start.25
  705.6 4.7 copy-start.26
  705.6 4.7 copy-start.27
  705.6 4.7 copy-start.28
  705.6 6.2 copy-start.23
  (5 other events, 6.4 us)
Sparse Core Ops, SparseCore 0:
  19.0 64.0 all-gather.4
  84.6 95.2 all-gather.6
  181.5 87.7 all-gather.8
  270.8 79.2 all-gather.10
  352.3 77.0 reduce-scatter.4
  431.6 77.2 reduce-scatter.6
  511.3 93.9 reduce-scatter.8
  608.6 59.2 reduce-scatter.10

commit v6 on v5

--- a/solution.py
+++ b/solution.py
@@ -560,6 +560,42 @@
         yield
         for k in range(len(to)):
             pltpu.make_async_copy(t_ref.at[0], o_ref.at[k], recv_sem.at[k]).wait()
+        for wait in waits:
+            wait()
+
+
+class TokenRounds(TokenMoves):
+    def __init__(self, tokens, split, rounds):
+        super().__init__(tokens, split)
+        self.rounds = rounds
+        self.out = [jax.ShapeDtypeStruct((len(rounds), *tokens.shape[1:]), tokens.dtype)]
+        self.scratch = [pltpu.SemaphoreType.DMA((len(rounds),))] * 2
+
+    def places(self):
+        ms = self.operands[0].shape[0]
+        x, c, z, y, _ = own_place()
+        slot = group = z // 2 if self.split == 2 else z // 4
+        js = [(r + slot) % ms for r in self.rounds]
+        ks = [(group - r + ms) % ms for r in self.rounds]
+        if self.split == 2:
+            to = [at_place(x, z % 2, 2 * j + c, y) for j in js]
+            of = [at_place(x, z % 2, 2 * k + c, y) for k in ks]
+        else:
+            to = [at_place(z % 2, z // 2 % 2, (2 * j + x) * 2 + c, y) for j in js]
+            of = [at_place(z // 2 % 2, z % 2, 4 * k + 2 * c + x, y) for k in ks]
+        return js, to, of
+
+    def begin(self, ins, outs, held):
+        (t_ref,), (o_ref,), (send_sem, recv_sem) = ins, outs, held
+        js, to, _ = self.places()
+        yield
+        waits = [
+            send_or_keep(t_ref.at[j], o_ref.at[i], send_sem.at[i], recv_sem.at[i], *place)
+            for i, (j, place) in enumerate(zip(js, to))
+        ]
+        yield
+        for i in range(len(to)):
+            pltpu.make_async_copy(t_ref.at[0], o_ref.at[i], recv_sem.at[i]).wait()
         for wait in waits:
             wait()
 
@@ -1003,11 +1039,19 @@
     g2 = ffn_gain.astype(F32)[:, None]
 
     wqkv = (query_weight, key_weight, value_weight)
-    (wqkv_part,) = exchange("weight_columns", [Columns(wqkv, g1)])
-    x, gate_part, seg_all = exchange(
+    pieces = tokens.reshape(ms, pl_len, width)
+    x_first, wqkv_part = exchange(
+        "weight_columns", [Columns(wqkv, g1)], movers=[TokenRounds(pieces, split, range(ms // 2))]
+    )
+    x_last, gate_part, seg_all = exchange(
         "weight_columns", [Columns([gate_weight], g2), Segments(segments.reshape(ms, seq_len))], wqkv_part,
-        movers=[TokenMoves(tokens.reshape(ms, pl_len, width), split)],
-    )
+        movers=[TokenRounds(pieces, split, range(ms // 2, ms))],
+    )
+    group = z_index // 2 if split == 2 else z_index // 4
+    came_in = (group - jnp.arange(ms, dtype=jnp.int32)[:, None, None] + ms) % ms
+    x = x_first[0][None]
+    for r in range(1, ms):
+        x = jnp.where(came_in == r, x_first[r] if r < ms // 2 else x_last[r - ms // 2], x)
     w_qkv = along_z(wqkv_part)
 
     seg_all = seg_all.reshape(2, 2, 2, ms, seq_len)[:, :, 0]

time: 728 us -> 737 us (1.012)
  Pallas kernels: 590 us -> 600 us
    pallas_call x7, Pallas kernels: 209 us -> 218 us  [exchange(): pl.pallas_call(kernel, out_shape=[o for part in parts for o in part.out],...]
where the time goes in v6:
time: 737 us; the launch traced here: 729 us
  Pallas kernels  600 us (81%)
  matrix products  58 us (8%)
  local copies, waits for them, and re-layouts  28.8 us (4%)
  other arithmetic  19 us (3%)
  between operations  15.2 us (2%)
    pallas_call x8, Pallas kernels, communicate(): pl.pallas_call(kernel, out_shape=[shape] + [m.out for m in matmuls] + mov...  375 us
    pallas_call x7, Pallas kernels, exchange(): pl.pallas_call(kernel, out_shape=[o for part in parts for o in part.out],...  218 us
    dot_general x3, matrix products, dot_nn(): lax.dot_general(a, b, (((1,), (0,)), ((), ())), preferred_element_type=F32)  44.7 us
    unnamed x61, local copies, waits for them, and re-layouts  23.5 us
  transfers between devices with their start and end apart: 8, of which 2 were waited for; matrix products, arithmetic and copies ran while one was open for 10% of the time, Pallas kernels for 75%

profile of v6, /device:TPU:29, one launch (start us, length us, event | category | flops | bytes accessed | tf_op | source)
XLA Modules:
  0.0 729.3 jit_solution(3077788721011492843)
XLA Ops:
  8.6 19.0 %weight_columns.4 = (bf16[1,128,2048]{2,1,0:T(8,128)(2,1)}, bf16[512,512]{1,0:T(8,128)(2,1)}) custom-call(bf16[2,128,2048]{2,1,0:T(8,128)(2,1)} %bitcast.108, bf16[64,2048]{1,0:T(8,128)(2,1)} %refs_1_.3, bf16[64,1024]{1,0:T(8,128)(2,1)} %refs_2_.1, bf16[64,1024]{1,0:T(8,128)(2,1)} %refs_3_.1, f32[64,1]{1,0:T(8,128)} %copy.30.refs_4_), custom_call_target="tpu_custom_call" | custom-call | bytes 1024 | tf_op jit(solution)/shard_map/weight_columns/pallas_call | solution.py:791
  30.4 51.7 %weight_columns.5 = (bf16[1,128,2048]{2,1,0:T(8,128)(2,1)}, bf16[512,1024]{1,0:T(8,128)(2,1)}, s32[8,2,1024]{2,1,0:T(2,128)}) custom-call(bf16[2,128,2048]{2,1,0:T(8,128)(2,1)} %bitcast.109, bf16[64,8192]{1,0:T(8,128)(2,1)} %refs_1_.4, f32[64,1]{1,0:T(8,128)} %copy.31.refs_2_.refs_1_, s32[2,1024]{1,0:T(2,128)} %bitcast.118, ...), custom_call_target="tpu_custom_call" | custom-call | bytes 1024 | tf_op jit(solution)/shard_map/weight_columns/pallas_call | solution.py:791
  85.2 49.4 %plane_gather.4 = (bf16[2,2,2,2,128,2048]{5,4,3,2,1,0:T(8,128)(2,1)S(1)}, bf16[256,2048]{1,0:T(8,128)(2,1)S(1)}) custom-call(bf16[2,128,2048]{2,1,0:T(8,128)(2,1)S(1)} %broadcast_select_fusion.refs_0_.refs_2_, bf16[64,2048]{1,0:T(8,128)(2,1)S(1)} %copy-done.16, bf16[512,512]{1,0:T(8,128)(2,1)S(1)} %copy-done.13), custom_call_target="tpu_custom_call" | custom-call | bytes 1024 | tf_op jit(solution)/shard_map/plane_gather/pallas_call | solution.py:270
  134.6 3.3 copy-done.12
  138.9 1.9 multiply_cosine_fusion
  140.9 7.9 %fusion.22 = f32[2048,512]{1,0:T(8,128)S(1)} fusion(bf16[2048,2048]{1,0:T(8,128)(2,1)} %bitcast.99, bf16[2048,512]{1,0:T(8,128)(2,1)} %all-gather.5.cloned.1.call-done.refs_1_), kind=kOutput, calls=%fused_computation.60 | convolution fusion | flops 4294967296 | bytes 14680064 | tf_op jit(solution)/shard_map/dot_general | solution.py:30
  149.6 2.8 core_gather.1
  152.6 4.5 attention_forward.1
  158.2 15.6 %weight_columns.6.refs_4_ = bf16[512,1024]{1,0:T(8,128)(2,1)} custom-call(bf16[64,8192]{1,0:T(8,128)(2,1)} %refs_0_.2, bf16[2048,256]{1,0:T(8,128)(2,1)} %bitcast.95), custom_call_target="tpu_custom_call" | custom-call | bytes 1024 | tf_op jit(solution)/shard_map/weight_columns/pallas_call | solution.py:791
  173.9 45.0 %plane_scatter.4 = (f32[2,128,2048]{2,1,0:T(8,128)}, bf16[2,128,2048]{2,1,0:T(8,128)(2,1)}) custom-call(bf16[2,2,2,2,128,256]{5,4,3,2,1,0:T(8,128)(2,1)} %bitcast.96, bf16[256,2048]{1,0:T(8,128)(2,1)} %copy-done.15, bf16[2,128,2048]{2,1,0:T(8,128)(2,1)} %copy-done.3, bf16[2,128,2048]{2,1,0:T(8,128)(2,1)} %bitcast.114, bf16[512,1024]{1,0:T(8,128)(2,1)} %weight_columns.6.refs_4_), custom_call_target="tpu_custom_call" | custom-call | bytes 1024 | tf_op jit(solution)/shard_map/plane_scatter/pallas_call | solution.py:270
  220.5 39.5 %plane_gather.5 = bf16[2,2,2,2,128,2048]{5,4,3,2,1,0:T(8,128)(2,1)S(1)} custom-call(f32[2,128,2048]{2,1,0:T(8,128)S(1)} %copy-done.2), custom_call_target="tpu_custom_call" | custom-call | bytes 1024 | tf_op jit(solution)/shard_map/plane_gather/pallas_call | solution.py:270
  260.0 3.3 copy-done
  263.3 15.0 %weight_columns.7.refs_3_ = bf16[512,1024]{1,0:T(8,128)(2,1)} custom-call(bf16[64,8192]{1,0:T(8,128)(2,1)} %refs_0_.3, f32[64,1]{1,0:T(8,128)} %copy.31.refs_2_.refs_1_, bf16[2048,2048]{1,0:T(8,128)(2,1)} %bitcast.87), custom_call_target="tpu_custom_call" | custom-call | bytes 1024 | tf_op jit(solution)/shard_map/weight_columns/pallas_call | solution.py:791
  278.7 2.2 copy-done.7
  282.1 39.2 %plane_gather.6 = (bf16[2,2,2,2,128,2048]{5,4,3,2,1,0:T(8,128)(2,1)}, f32[2048,1024]{1,0:T(8,128)}) custom-call(bf16[2,128,2048]{2,1,0:T(8,128)(2,1)S(1)} %copy-done.14, bf16[2048,2048]{1,0:T(8,128)(2,1)} %bitcast.88, bf16[2048,1024]{1,0:T(8,128)(2,1)S(1)} %copy-done.7, bf16[512,1024]{1,0:T(8,128)(2,1)S(1)} %copy-done.8), custom_call_target="tpu_custom_call" | custom-call | bytes 1024 | tf_op jit(solution)/shard_map/plane_gather/pallas_call | solution.py:270
  321.3 16.3 %multiply_convert_fusion.2 = (bf16[2048,1024]{1,0:T(8,128)(2,1)S(1)}, f32[2048,1024]{1,0:T(8,128)}) fusion(f32[2048,1024]{1,0:T(8,128)} %get-tuple-element.49, bf16[2048,2048]{1,0:T(8,128)(2,1)} %bitcast.106, bf16[2048,1024]{1,0:T(8,128)(2,1)} %all-gather.9.cloned.1.call-done.refs_1_), kind=kOutput, calls=%fused_computation.2 | convolution fusion | flops 8602517504 | bytes 33554432 | tf_op jit(solution)/shard_map/dot_general | solution.py:30
  337.6 2.0 copy-done.21
  339.6 13.3 %convolution_convert_fusion.refs_0_ = bf16[2048,1024]{1,0:T(8,128)(2,1)} fusion(bf16[2048,2048]{1,0:T(8,128)(2,1)} %bitcast.89, bf16[2048,1024]{1,0:T(8,128)(2,1)S(1)} %get-tuple-element.112), kind=kOutput, calls=%fused_computation.5 | convolution fusion | flops 8592031744 | bytes 16777216 | tf_op jit(solution)/shard_map/dot_general | solution.py:38
  353.0 6.3 all-gather.11.cloned.1.call-done.a_ref
  359.3 20.5 %multiply_convert_fusion = (bf16[2048,1024]{1,0:T(8,128)(2,1)}, bf16[2048,1024]{1,0:T(8,128)(2,1)}) fusion(f32[2048,1024]{1,0:T(8,128)} %get-tuple-element.49, f32[2048,1024]{1,0:T(8,128)} %get-tuple-element.113, bf16[2048,2048]{1,0:T(8,128)(2,1)} %bitcast.90, bf16[2048,1024]{1,0:T(8,128)(2,1)} %tie.1.refs_3_), kind=kOutput, calls=%fused_computation | convolution fusion | flops 8617197568 | bytes 37748736 | tf_op jit(solution)/shard_map/dot_general | solution.py:30
  379.8 58.6 %plane_scatter.5 = (f32[2,128,2048]{2,1,0:T(8,128)}, bf16[2048,1024]{1,0:T(8,128)(2,1)}) custom-call(bf16[2,2,2,2,128,1024]{5,4,3,2,1,0:T(8,128)(2,1)} %bitcast.103, bf16[2048,1024]{1,0:T(8,128)(2,1)} %all-gather.7.cloned.1.call-done.refs_2_.refs_1_, bf16[2,2,2,2,128,1024]{5,4,3,2,1,0:T(8,128)(2,1)} %bitcast.110, bf16[2048,1024]{1,0:T(8,128)(2,1)} %tie.1.refs_3_, ...), custom_call_target="tpu_custom_call" | custom-call | bytes 1024 | tf_op jit(solution)/shard_map/plane_scatter/pallas_call | solution.py:270
  440.0 2.2 copy-done.5
  442.2 39.3 %plane_gather.7 = (bf16[2,2,2,2,128,2048]{5,4,3,2,1,0:T(8,128)(2,1)}, bf16[2048,1024]{1,0:T(8,128)(2,1)S(1)}) custom-call(f32[2,128,2048]{2,1,0:T(8,128)S(1)} %copy-done.11, bf16[2048,2048]{1,0:T(8,128)(2,1)} %bitcast.107, bf16[2048,1024]{1,0:T(8,128)(2,1)S(1)} %copy-done.5), custom_call_target="tpu_custom_call" | custom-call | bytes 1024 | tf_op jit(solution)/shard_map/plane_gather/pallas_call | solution.py:270
  481.4 2.0 copy-done.6
  483.7 47.6 %plane_scatter.6.refs_9_.refs_4_ = bf16[2,128,2048]{2,1,0:T(8,128)(2,1)} custom-call(bf16[2,2,2,2,128,1024]{5,4,3,2,1,0:T(8,128)(2,1)} %bitcast.98, bf16[2048,1024]{1,0:T(8,128)(2,1)} %all-gather.9.cloned.1.call-done.refs_1_, f32[2,128,2048]{2,1,0:T(8,128)} %get-tuple-element.45.refs_0_.refs_4_.refs_2_, bf16[2048,1024]{1,0:T(8,128)(2,1)} %copy-done.6), custom_call_target="tpu_custom_call" | custom-call | bytes 1024 | tf_op jit(solution)/shard_map/plane_scatter/pallas_call | solution.py:270
  531.3 29.7 %attention_backward.1 = (bf16[64,8192]{1,0:T(8,128)(2,1)}, bf16[2,1024,512]{2,1,0:T(8,128)(2,1)}) custom-call(bf16[512,1024]{1,0:T(8,128)(2,1)} %reduce-scatter.5.cloned.1.call-done.refs_0_, bf16[2,1024,2048]{2,1,0:T(8,128)(2,1)} %bitcast.101, bf16[256,2048]{1,0:T(8,128)(2,1)} %copy-done.15, bf16[2,1024,256]{2,1,0:T(8,128)(2,1)} %copy-done.10, ...), custom_call_target="tpu_custom_call" | custom-call | bytes 1024 | tf_op jit(solution)/shard_map/attention_backward/pallas_call | solution.py:791
  561.1 56.5 %plane_scatter.7 = (bf16[2,128,2048]{2,1,0:T(8,128)(2,1)}, bf16[2048,512]{1,0:T(8,128)(2,1)}, bf16[256,2048]{1,0:T(8,128)(2,1)}, bf16[2,128,2048]{2,1,0:T(8,128)(2,1)}) custom-call(bf16[2,2,2,2,128,512]{5,4,3,2,1,0:T(8,128)(2,1)} %bitcast.104, bf16[2048,512]{1,0:T(8,128)(2,1)} %all-gather.5.cloned.1.call-done.refs_1_, bf16[2,128,2048]{2,1,0:T(8,128)(2,1)} %copy-done.3, ...), custom_call_target="tpu_custom_call" | custom-call | bytes 1024 | tf_op jit(solution)/shard_map/plane_scatter/pallas_call | solution.py:270
  617.6 49.1 %weight_rows.2 = (bf16[2,128,2048]{2,1,0:T(8,128)(2,1)}, bf16[64,8192]{1,0:T(8,128)(2,1)}, bf16[64,8192]{1,0:T(8,128)(2,1)}) custom-call(bf16[2,128,2048]{2,1,0:T(8,128)(2,1)} %get-tuple-element.56.refs_0_, bf16[512,1024]{1,0:T(8,128)(2,1)} %reduce-scatter.7.cloned.1.call-done.refs_9_.refs_1_, bf16[512,1024]{1,0:T(8,128)(2,1)} %reduce-scatter.9.cloned.1.call-done.refs_2_, ...), custom_call_target="tpu_custom_call" | custom-call | bytes 1024 | tf_op jit(solution)/shard_map/weight_rows/pallas_call | solution.py:791
  666.8 2.7 convert_element_type.86.refs_4_
  669.5 5.3 fusion.2
  677.0 37.7 %weight_rows.3 = (f32[64,2048]{1,0:T(8,128)}, bf16[64,2048]{1,0:T(8,128)(2,1)}, bf16[64,1024]{1,0:T(8,128)(2,1)}, bf16[64,1024]{1,0:T(8,128)(2,1)}) custom-call(bf16[256,2048]{1,0:T(8,128)(2,1)} %get-tuple-element.59.refs_0_, bf16[512,512]{1,0:T(8,128)(2,1)} %reduce-scatter.11.cloned.1.call-done.refs_1_, f32[64,8192]{1,0:T(8,128)} %get-tuple-element.134.refs_2_, ...), custom_call_target="tpu_custom_call" | custom-call | bytes 1024 | tf_op jit(solution)/shard_map/weight_rows/pallas_call | solution.py:791
  717.5 2.0 convert_multiply_fusion.4
  (100 shorter events, 22.7 us)
Async XLA Ops:
  7.2 133.7 %all-gather.5.cloned.1.call-start = ((), (), s32[]{:S(2)}) async-start(), calls=%async_computation.4 | async-start | bytes 2621440 | tf_op jit(solution)/shard_map/all_gather | solution.py:971
  27.6 57.6 %copy-start.13 = (bf16[512,512]{1,0:T(8,128)(2,1)S(1)}, bf16[512,512]{1,0:T(8,128)(2,1)}, u32[]{:S(2)}) copy-start(bf16[512,512]{1,0:T(8,128)(2,1)} %get-tuple-element.39.refs_4_.refs_2_) | copy-start | bytes 1572868
  27.6 57.6 %copy-start.16 = (bf16[64,2048]{1,0:T(8,128)(2,1)S(1)}, bf16[64,2048]{1,0:T(8,128)(2,1)}, u32[]{:S(2)}) copy-start(bf16[64,2048]{1,0:T(8,128)(2,1)} %refs_1_.5) | copy-start | bytes 786436
  27.6 251.0 %all-gather.7.cloned.1.call-start = ((), (), s32[]{:S(2)}) async-start(), calls=%async_computation.5 | async-start | bytes 5242880 | tf_op jit(solution)/shard_map/all_gather | solution.py:971
  82.2 239.2 %all-gather.9.cloned.1.call-start = ((), (), s32[]{:S(2)}) async-start(), calls=%async_computation.6 | async-start | bytes 5242880 | tf_op jit(solution)/shard_map/all_gather | solution.py:971
  83.4 69.2 %copy-start.9 = (s32[2,1024,1]{2,1,0:T(8,128)}, s32[2,1024,1]{2,1,0:T(8,128)S(1)}, u32[]{:S(2)}) copy-start(s32[2,1024,1]{2,1,0:T(8,128)S(1)} %copy.33.qseg_ref.refs_5_) | copy-start | bytes 24580
  85.2 63.6 %copy-start.3 = (bf16[2,128,2048]{2,1,0:T(8,128)(2,1)}, bf16[2,128,2048]{2,1,0:T(8,128)(2,1)S(1)}, u32[]{:S(2)}) copy-start(bf16[2,128,2048]{2,1,0:T(8,128)(2,1)S(1)} %broadcast_select_fusion.refs_0_.refs_2_) | copy-start | bytes 3145732
  134.6 3.3 copy-start.12
  138.9 13.7 %copy-start.17 = (s32[2,1,1024]{2,1,0:T(1,128)}, s32[2,1,1024]{2,1,0:T(1,128)S(1)}, u32[]{:S(2)}) copy-start(s32[2,1,1024]{2,1,0:T(1,128)S(1)} %fusion.31.kseg_ref.refs_6_) | copy-start | bytes 24580
  140.8 8.0 %copy-start.18 = (f32[1024,128]{1,0:T(8,128)}, f32[1024,128]{1,0:T(8,128)S(1)}, u32[]{:S(2)}) copy-start(f32[1024,128]{1,0:T(8,128)S(1)} %get-tuple-element.104.refs_7_) | copy-start | bytes 1572868
  140.8 8.0 %copy-start.19 = (f32[1024,128]{1,0:T(8,128)}, f32[1024,128]{1,0:T(8,128)S(1)}, u32[]{:S(2)}) copy-start(f32[1024,128]{1,0:T(8,128)S(1)} %get-tuple-element.105.refs_8_) | copy-start | bytes 1572868
  152.5 4.7 copy-start.1
  152.6 4.6 copy-start.10
  173.8 185.4 %all-gather.11.cloned.1.call-start = ((), (), s32[]{:S(2)}) async-start(), calls=%async_computation.8 | async-start | bytes 5242880 | tf_op jit(solution)/shard_map/all_gather | solution.py:971
  260.0 3.3 copy-start
  263.3 15.4 %copy-start.14 = (bf16[2,128,2048]{2,1,0:T(8,128)(2,1)S(1)}, bf16[2,128,2048]{2,1,0:T(8,128)(2,1)}, u32[]{:S(2)}) copy-start(bf16[2,128,2048]{2,1,0:T(8,128)(2,1)} %get-tuple-element.46.refs_0_.refs_5_) | copy-start | bytes 3145732
  278.3 253.0 %reduce-scatter.5.cloned.1.call-start = ((), (), s32[]{:S(2)}) async-start(), calls=%async_computation.7 | async-start | bytes 5242880 | tf_op jit(solution)/shard_map/reduce_scatter | solution.py:975
  278.6 2.2 copy-start.7
  337.6 2.0 copy-start.21
  352.9 208.1 %reduce-scatter.7.cloned.1.call-start = ((), (), s32[]{:S(2)}) async-start(), calls=%async_computation.9 | async-start | bytes 5242880 | tf_op jit(solution)/shard_map/reduce_scatter | solution.py:975
  438.4 179.2 %reduce-scatter.9.cloned.1.call-start = ((), (), s32[]{:S(2)}) async-start(), calls=%async_computation.10 | async-start | bytes 5242880 | tf_op jit(solution)/shard_map/reduce_scatter | solution.py:975
  440.0 2.2 copy-start.5
  481.4 2.0 copy-start.6
  483.4 193.6 %reduce-scatter.11.cloned.1.call-start = ((), (), s32[]{:S(2)}) async-start(), calls=%async_computation.11 | async-start | bytes 2621440 | tf_op jit(solution)/shard_map/reduce_scatter | solution.py:975
  617.6 51.8 %copy-start.20 = (bf16[64,8192]{1,0:T(8,128)(2,1)S(1)}, bf16[64,8192]{1,0:T(8,128)(2,1)}, u32[]{:S(2)}) copy-start(bf16[64,8192]{1,0:T(8,128)(2,1)} %refs_0_.3) | copy-start | bytes 3145732
  669.5 5.3 copy-start.22
  677.0 40.4 %copy-start.23 = (bf16[64,2048]{1,0:T(8,128)(2,1)S(1)}, bf16[64,2048]{1,0:T(8,128)(2,1)}, u32[]{:S(2)}) copy-start(bf16[64,2048]{1,0:T(8,128)(2,1)} %refs_1_.3) | copy-start | bytes 786436
  714.8 4.7 copy-start.25
  714.8 4.7 copy-start.26
  714.8 4.7 copy-start.27
  714.8 4.7 copy-start.28
  714.8 6.2 copy-start.24
  (5 other events, 6.4 us)
Sparse Core Ops, SparseCore 0:
  27.8 62.6 all-gather.4
  92.0 94.9 all-gather.6
  188.5 89.9 all-gather.8
  279.9 79.2 all-gather.10
  361.4 77.0 reduce-scatter.4
  440.8 77.2 reduce-scatter.6
  520.4 93.9 reduce-scatter.8
  617.7 59.2 reduce-scatter.10
